TPU v7x, 128 devices: a whole 4x4x4 slice. The times are simulated.
128 devices in a mesh: snap: 8 (over x, core), node: 16 (over z, y).
Axes of the slice: x: 4, y: 4, z: 4, core: 2. Of those that a mesh axis runs over, the one named last changes fastest.
Arguments:
- features: bfloat16 [8, 16384, 256], P('snap', 'node'), may hold values from -6 to 6
- tile_ids: int32 [8, 128, 4], P('snap', 'node'), may hold values from 0 to 23
- tile_values: bfloat16 [8, 128, 4, 128, 128], P('snap', 'node'), may hold values from -0.25 to 0.25
- pos_edges: int32 [8, 2, 16384], P('snap', None, 'node'), may hold values from 0 to 1023
- neg_edges: int32 [8, 2, 16384], P('snap', None, 'node'), may hold values from 0 to 1023
- initial_weight: float32 [256, 256], replicated, may hold values from -0.375 to 0.375
- gate_mats: float32 [4, 256, 256], replicated, may hold values from -0.75 to 0.75
- gate_bias: float32 [3, 256, 256], replicated, may hold values from -1.5 to 1.5
Outputs:
- snapshot_adjoint: float32 [8, 256, 256], P('snap', 'node')
- gate_grads: float32 [7, 256, 256], replicated
- initial_grad: float32 [256, 256], replicated
Inputs may be any that keep to these rules, and one draw needn't show every extreme that they name: `tile_ids`: block numbers count the blocks of the device's extended rows: the 1024 rows before its first row, its own 1024 rows, then the 1024 rows after its last. `pos_edges`: node numbers within the device's own rows. `neg_edges`: node numbers within the device's own rows.
All inputs are finite; a program needn't handle non-finite values.
Results may differ from a plain program's by a relative error of at most 0.0054.
Values may be sent and summed in bfloat16 or wider, within the bound.
No kernel may reach another device: no remote copies, remote signals or barrier semaphores. Data moves between devices by JAX's collectives and lax.ppermute only.
A program may use at most 128 MiB of HBM per device.

v0:
```python
import functools

import jax
import jax.numpy as jnp
from jax import lax
from jax.experimental import pallas as pl
from jax.experimental.pallas import tpu as pltpu
from jax.sharding import PartitionSpec as P

HALO = 1024
RING = 4
PACK_EXTRA = 16
F32 = jnp.float32
BF16 = jnp.bfloat16
INNER = (((1,), (0,)), ((), ()))
LANES = (((1,), (1,)), ((), ()))
ROWS = (((0,), (0,)), ((), ()))


def split(value):
    high = value.astype(BF16)
    return high, (value - high.astype(F32)).astype(BF16)


def dot(left, right, dims=INNER):
    return lax.dot_general(left, right, dims, preferred_element_type=F32)


def dot3(left, right, dims=INNER):
    return (
        dot(left[0], right[0], dims) + dot(left[0], right[1], dims) + dot(left[1], right[0], dims)
    )


def sigmoid(value):
    return 0.5 * jnp.tanh(0.5 * value) + 0.5


def forward_kernel(start, mats, bias, before, update, reset, proposal, low, mats_high, mats_low):
    steps = low.shape[0]
    width = start.shape[0]
    for k in range(4):
        high, rest = split(mats[k])
        mats_high[pl.ds(k * width, width), :] = high
        mats_low[pl.ds(k * width, width), :] = rest
    before[0] = start[...]

    def step(t, carry):
        weight = before[t]
        parts = split(weight)
        top = pl.ds(0, 3 * width)
        gates = dot3((mats_high[top, :], mats_low[top, :]), parts)
        r = sigmoid(gates[width : 2 * width] + bias[1])
        last = pl.ds(3 * width, width)
        inner = gates[2 * width :] + dot3((mats_high[last, :], mats_low[last, :]), split(r * weight))
        u = sigmoid(gates[:width] + bias[0])
        c = jnp.tanh(inner + bias[2])
        fresh = (1.0 - u) * weight + u * c
        update[t] = u
        reset[t] = r
        proposal[t] = c
        low[t] = fresh.astype(BF16)

        @pl.when(t + 1 < steps)
        def _():
            before[t + 1] = fresh

        return carry

    lax.fori_loop(0, steps, step, 0)


def edge_kernel(
    factor, where, ids, own, left, right, tiles, columns, low, packed, extended, aggregated, picked
):
    rows, width = own.shape
    side = tiles.shape[1]
    blocks = rows // side
    per_block = ids.shape[1]
    extended[pl.ds(0, blocks)] = left[...].reshape(blocks, side, width)
    extended[pl.ds(blocks, blocks)] = own[...].reshape(blocks, side, width)
    extended[pl.ds(2 * blocks, blocks)] = right[...].reshape(blocks, side, width)
    for b in range(blocks):
        total = jnp.zeros((side, width), F32)
        for k in range(per_block):
            total = total + dot(tiles[b * per_block + k], extended[ids[b, k]])
        aggregated[pl.ds(b * side, side), :] = total.astype(BF16)

    count = columns.shape[0]
    chunk = 512
    for c in range(count // chunk):
        index = columns[pl.ds(c * chunk, chunk), :]
        lane = lax.broadcasted_iota(jnp.int32, (chunk, rows), 1)
        onehot = (lane == index).astype(F32).astype(BF16)
        picked[pl.ds(c * chunk, chunk), :] = dot(onehot, aggregated[...]).astype(BF16)

    weight_low = low[where[0]]
    edges = count // 4
    half = jnp.zeros((width, width), F32)
    for sign in (0, 1):
        first = picked[pl.ds(2 * sign * edges, edges), :]
        second = picked[pl.ds((2 * sign + 1) * edges, edges), :]
        ends = dot(first, weight_low) * dot(second, weight_low)
        score = jnp.sum(ends, axis=1, keepdims=True) * (1.0 / width)
        if sign == 0:
            slope = sigmoid(-score) * (-factor)
        else:
            slope = sigmoid(score) * factor
        scaled = split(slope * first.astype(F32))
        half = half + dot(scaled[0], second, ROWS) + dot(scaled[1], second, ROWS)
    full = half + half.T
    quarter = width // 2
    upper = full[:quarter, :quarter]
    lower = full[quarter:, quarter:]
    i = lax.broadcasted_iota(jnp.int32, (quarter, quarter), 0)
    j = lax.broadcasted_iota(jnp.int32, (quarter, quarter), 1)
    diagonal = jnp.sum(jnp.where(i == j, lower, 0.0), axis=0, keepdims=True)
    packed[pl.ds(0, quarter), :] = full[:quarter, quarter:].astype(BF16)
    packed[pl.ds(quarter, quarter), :] = jnp.where(i <= j, upper, lower).astype(BF16)
    packed[pl.ds(2 * quarter, PACK_EXTRA), :] = jnp.broadcast_to(
        diagonal, (PACK_EXTRA, quarter)
    ).astype(BF16)


def backward_kernel(
    where,
    pieces,
    before,
    update,
    reset,
    proposal,
    low,
    mats_high,
    mats_low,
    adjoint_rows,
    grads,
    initial_grad,
    flipped_high,
    flipped_low,
    local,
    adjoints,
):
    steps, width = low.shape[0], low.shape[1]
    quarter = width // 2
    x, core, node = where[0], where[1], where[2]
    for k in range(4):
        area = pl.ds(k * width, width)
        flipped_high[k] = mats_high[area, :].T
        flipped_low[k] = mats_low[area, :].T
    i = lax.broadcasted_iota(jnp.int32, (quarter, quarter), 0)
    j = lax.broadcasted_iota(jnp.int32, (quarter, quarter), 1)
    for t in range(steps):
        side = lax.rem(core + t % 2, 2)
        turn = lax.rem(x - t // 2 + RING, RING)
        piece = pieces[side, turn]
        corner = piece[:quarter]
        mixed = piece[quarter : 2 * quarter].astype(F32)
        diagonal = piece[2 * quarter :].astype(F32)[0:1]
        turned = mixed.T
        upper = jnp.where(i <= j, mixed, turned).astype(BF16)
        lower = jnp.where(i > j, mixed, jnp.where(i < j, turned, diagonal)).astype(BF16)
        weight = low[t]
        top, bottom = weight[:quarter], weight[quarter:]
        local[t, pl.ds(0, quarter), :] = dot(upper, top) + dot(corner, bottom)
        local[t, pl.ds(quarter, quarter), :] = dot(corner.T, top) + dot(lower, bottom)

    grads[...] = jnp.zeros_like(grads)

    def step(s, carry):
        t = steps - 1 - s
        g = local[t] + carry
        adjoints[t] = g
        weight, u, r, c = before[t], update[t], reset[t], proposal[t]
        keep = 1.0 - u
        d0 = g * (c - weight) * (u * keep)
        d2 = g * u * (1.0 - c * c)
        d2_parts = split(d2)
        inner = dot3((flipped_high[3], flipped_low[3]), d2_parts)
        d0_parts = split(d0)
        d1 = inner * weight * (r * (1.0 - r))
        d1_parts = split(d1)
        fresh = g * keep + inner * r
        fresh = fresh + dot3((flipped_high[0], flipped_low[0]), d0_parts)
        fresh = fresh + dot3((flipped_high[2], flipped_low[2]), d2_parts)
        fresh = fresh + dot3((flipped_high[1], flipped_low[1]), d1_parts)
        weight_parts = split(weight)
        grads[0] += dot3(d0_parts, weight_parts, LANES)
        grads[1] += dot3(d1_parts, weight_parts, LANES)
        grads[2] += dot3(d2_parts, weight_parts, LANES)
        grads[3] += dot3(d2_parts, split(r * weight), LANES)
        grads[4] += d0
        grads[5] += d1
        grads[6] += d2
        return fresh

    initial_grad[...] = lax.fori_loop(0, steps, step, jnp.zeros((width, width), F32))
    share = adjoint_rows.shape[0]
    start = pl.multiple_of(node * share, share)
    adjoint_rows[...] = adjoints[2 * x + core, pl.ds(start, share), :]


def params(megabytes):
    return pltpu.CompilerParams(vmem_limit_bytes=megabytes * 2**20)


VMEM = pl.BlockSpec(memory_space=pltpu.VMEM)
SMEM = pl.BlockSpec(memory_space=pltpu.SMEM)


def ring_parts(block, axis, stride, count):
    size = lax.axis_size(axis)
    span = stride * count
    parts = []
    for turn in range(1, count):
        route = [
            (i, i - i % span + (i % span + turn * stride) % span) for i in range(size)
        ]
        parts.append(lax.ppermute(block, axis, route))
    return parts


def ring_sum(block, axis, stride, count):
    parts = ring_parts(block, axis, stride, count)
    total = block.astype(F32)
    for part in parts:
        total = total + part.astype(F32)
    return total.astype(BF16)


def body(
    features, tile_ids, tile_values, pos_edges, neg_edges, initial_weight, gate_mats, gate_bias
):
    snap_count = lax.axis_size("snap")
    node_count = lax.axis_size("node")
    place = lax.axis_index("snap")
    node = lax.axis_index("node")
    own = features[0]
    rows, width = own.shape
    side = tile_values.shape[-1]
    per_block = tile_ids.shape[-1]
    square = (snap_count, width, width)

    ends = node_count - 1
    left = lax.ppermute(own[rows - HALO :], "node", [(i, i + 1) for i in range(ends)])
    right = lax.ppermute(own[:HALO], "node", [(i + 1, i) for i in range(ends)])

    wide = jax.ShapeDtypeStruct(square, F32)
    tall = jax.ShapeDtypeStruct((4 * width, width), BF16)
    before, update, reset, proposal, low, mats_high, mats_low = pl.pallas_call(
        forward_kernel,
        out_shape=[wide, wide, wide, wide, jax.ShapeDtypeStruct(square, BF16), tall, tall],
        in_specs=[VMEM] * 3,
        out_specs=[VMEM] * 7,
        compiler_params=params(32),
        name="forward_chain",
    )(initial_weight, gate_mats, gate_bias)

    columns = jnp.concatenate(
        [pos_edges[0, 0], pos_edges[0, 1], neg_edges[0, 0], neg_edges[0, 1]]
    ).reshape(-1, 1)
    factor = float(rows * node_count) ** (-0.5)
    pack_rows = width + PACK_EXTRA
    packed = pl.pallas_call(
        functools.partial(edge_kernel, factor),
        out_shape=jax.ShapeDtypeStruct((pack_rows, width // 2), BF16),
        in_specs=[SMEM, SMEM] + [VMEM] * 6,
        out_specs=VMEM,
        scratch_shapes=[
            pltpu.VMEM(((rows + 2 * HALO) // side, side, width), BF16),
            pltpu.VMEM((rows, width), BF16),
            pltpu.VMEM((columns.shape[0], width), BF16),
        ],
        compiler_params=params(40),
        name="edge_products",
    )(
        jnp.stack([place, node]),
        tile_ids[0],
        own,
        left,
        right,
        tile_values.reshape(-1, side, side),
        columns,
        low,
    )

    packed = ring_sum(packed, "node", 1, RING)
    packed = ring_sum(packed, "node", RING, node_count // RING)
    along = jnp.stack([packed] + ring_parts(packed, "snap", 2, snap_count // 2))
    other = lax.ppermute(along, "snap", [(i, i ^ 1) for i in range(snap_count)])
    pieces = jnp.stack([along, other])

    share = width // node_count
    adjoint_rows, grads, initial_grad = pl.pallas_call(
        backward_kernel,
        out_shape=[
            jax.ShapeDtypeStruct((share, width), F32),
            jax.ShapeDtypeStruct((7, width, width), F32),
            jax.ShapeDtypeStruct((width, width), F32),
        ],
        in_specs=[SMEM] + [VMEM] * 8,
        out_specs=[VMEM] * 3,
        scratch_shapes=[
            pltpu.VMEM((4, width, width), BF16),
            pltpu.VMEM((4, width, width), BF16),
            pltpu.VMEM(square, F32),
            pltpu.VMEM(square, F32),
        ],
        compiler_params=params(40),
        name="backward_chain",
    )(
        jnp.stack([place // 2, place % 2, node]),
        pieces,
        before,
        update,
        reset,
        proposal,
        low,
        mats_high,
        mats_low,
    )
    return adjoint_rows[None], grads, initial_grad


def solution(mesh):
    placed = (
        P("snap", "node", None),
        P("snap", "node", None),
        P("snap", "node", None, None, None),
        P("snap", None, "node"),
        P("snap", None, "node"),
        P(),
        P(),
        P(),
    )
    return jax.shard_map(
        body,
        mesh=mesh,
        in_specs=placed,
        out_specs=(P("snap", "node", None), P(), P()),
        check_vma=False,
    )
```

profile of v0, /device:TPU:1, one launch (start us, length us, event | category | flops | bytes accessed | tf_op | source)
XLA Modules:
  0.0 86.3 jit_solution(2325374993102210359)
XLA Ops:
  0.6 0.0 copy-start.16
  0.6 1.4 %collective-permute-start.1 = (bf16[1024,256]{1,0:T(8,128)(2,1)}, bf16[1024,256]{1,0:T(8,128)(2,1)}, u32[]{:S(2)}, u32[]{:S(2)}) collective-permute-start(bf16[1024,256]{1,0:T(8,128)(2,1)} %bitcast.21), channel_id=1, source_target_pairs={{1,0},{2,1},{3,2},{4,3},{5,4},{6,5},{7,6},{8,7},{9,8},{10,9},{11,1... | collective-permute-start | bytes 1572872 | tf_op jit(solution)/shard_map/ppermute | solution.py:245
  2.1 5.5 %collective-permute-start = (bf16[1024,256]{1,0:T(8,128)(2,1)}, bf16[1024,256]{1,0:T(8,128)(2,1)}, u32[]{:S(2)}, u32[]{:S(2)}) collective-permute-start(bf16[1024,256]{1,0:T(8,128)(2,1)} %bitcast.22), channel_id=1, source_target_pairs={{0,1},{1,2},{2,3},{3,4},{4,5},{5,6},{6,7},{7,8},{8,9},{9,10},{10,1... | collective-permute-start | bytes 1572872 | tf_op jit(solution)/shard_map/ppermute | solution.py:244
  7.5 0.8 fusion.1
  8.3 0.8 copy.12.ids
  9.1 0.8 fusion.2
  9.9 0.6 copy.13.columns
  10.5 0.0 copy-done.16
  10.5 0.0 copy-start.8
  10.6 1.2 %copy-done.8 = f32[4,256,256]{2,1,0:T(8,128)S(1)} copy-done((f32[4,256,256]{2,1,0:T(8,128)S(1)}, f32[4,256,256]{2,1,0:T(8,128)}, u32[]{:S(2)}) %copy-start.8) | copy-done | bytes 1048600
  11.8 0.0 copy-start.10
  11.8 1.1 %copy-done.10 = f32[3,256,256]{2,1,0:T(8,128)S(1)} copy-done((f32[3,256,256]{2,1,0:T(8,128)S(1)}, f32[3,256,256]{2,1,0:T(8,128)}, u32[]{:S(2)}) %copy-start.10) | copy-done | bytes 786456
  12.9 0.0 copy-start.9
  12.9 0.0 copy-start.11
  12.9 7.0 %forward_chain.1 = (f32[8,256,256]{2,1,0:T(8,128)S(1)}, f32[8,256,256]{2,1,0:T(8,128)S(1)}, f32[8,256,256]{2,1,0:T(8,128)S(1)}, f32[8,256,256]{2,1,0:T(8,128)S(1...) custom-call(f32[256,256]{1,0:T(8,128)S(1)} %copy-done.16, ...), custom_call_target="tpu_custom_call" | custom-call | tf_op jit(solution)/shard_map/forward_chain/pallas_call | solution.py:249
  20.0 0.0 copy-start
  20.0 1.3 %copy-done = f32[8,256,256]{2,1,0:T(8,128)} copy-done((f32[8,256,256]{2,1,0:T(8,128)}, f32[8,256,256]{2,1,0:T(8,128)S(1)}, u32[]{:S(2)}) %copy-start) | copy-done | bytes 2097176
  21.3 0.0 copy-start.2
  21.3 1.3 %copy-done.2 = f32[8,256,256]{2,1,0:T(8,128)} copy-done((f32[8,256,256]{2,1,0:T(8,128)}, f32[8,256,256]{2,1,0:T(8,128)S(1)}, u32[]{:S(2)}) %copy-start.2) | copy-done | bytes 2097176
  22.6 0.0 copy-start.4
  22.6 1.4 %copy-done.4 = f32[8,256,256]{2,1,0:T(8,128)} copy-done((f32[8,256,256]{2,1,0:T(8,128)}, f32[8,256,256]{2,1,0:T(8,128)S(1)}, u32[]{:S(2)}) %copy-start.4) | copy-done | bytes 2097176
  24.0 0.0 copy-start.6
  24.0 1.4 %copy-done.6 = f32[8,256,256]{2,1,0:T(8,128)} copy-done((f32[8,256,256]{2,1,0:T(8,128)}, f32[8,256,256]{2,1,0:T(8,128)S(1)}, u32[]{:S(2)}) %copy-start.6) | copy-done | bytes 2097176
  25.4 0.0 copy-start.12
  25.4 0.8 copy-done.12
  26.2 0.8 copy-done.14
  27.1 0.1 pad_add_fusion.2.where
  27.1 0.0 collective-permute-done.1.right
  27.1 0.0 collective-permute-done.left
  27.1 0.0 copy-done.9
  27.1 0.0 copy-done.11
  27.2 6.2 %edge_products.1 = bf16[272,128]{1,0:T(8,128)(2,1)S(1)} custom-call(s32[2]{0:T(128)S(1)} %pad_add_fusion.2.where, s32[8,4]{1,0:T(8,128)S(1)} %copy.12.ids, bf16[1024,256]{1,0:T(8,128)(2,1)S(1)} %bitcast.23, bf16[1024,256]{1,0:T(8,128)(2,1)} %collective-permute-done.left, bf16[1024,256]{1,0:T(8,128)(2,1)} %collective-permute-done.1.right, ...), custom_call_target="tpu_custom_call" | custom-call | tf_op jit(solution)/shard_map/edge_products/pallas_call | solution.py:263
  33.3 0.0 copy-start.1
  33.3 4.3 %collective-permute-start.4 = (bf16[272,128]{1,0:T(8,128)(2,1)S(1)}, bf16[272,128]{1,0:T(8,128)(2,1)S(1)}, u32[]{:S(2)}, u32[]{:S(2)}) collective-permute-start(bf16[272,128]{1,0:T(8,128)(2,1)S(1)} %edge_products.1), channel_id=1, source_target_pairs={{0,3},{1,0},{2,1},{3,2},{4,7},{5,4},{6,5},{7,6},{8,11},{9,8},{10,9... | collective-permute-start | bytes 208904 | tf_op jit(solution)/shard_map/ppermute | solution.py:218
  37.6 0.0 collective-permute-start.3
  37.6 0.7 collective-permute-start.2
  38.3 1.3 %collective-permute-done.4 = bf16[272,128]{1,0:T(8,128)(2,1)S(1)} collective-permute-done((bf16[272,128]{1,0:T(8,128)(2,1)S(1)}, bf16[272,128]{1,0:T(8,128)(2,1)S(1)}, u32[]{:S(2)}, u32[]{:S(2)}) %collective-permute-start.4) | collective-permute-done | bytes 69664 | tf_op jit(solution)/shard_map/ppermute | solution.py:218
  39.6 2.8 %collective-permute-done.3 = bf16[272,128]{1,0:T(8,128)(2,1)S(1)} collective-permute-done((bf16[272,128]{1,0:T(8,128)(2,1)S(1)}, bf16[272,128]{1,0:T(8,128)(2,1)S(1)}, u32[]{:S(2)}, u32[]{:S(2)}) %collective-permute-start.3) | collective-permute-done | bytes 69664 | tf_op jit(solution)/shard_map/ppermute | solution.py:218
  42.4 0.4 collective-permute-done.2
  42.8 2.8 %collective-permute-start.7 = (bf16[272,128]{1,0:T(8,128)(2,1)S(1)}, bf16[272,128]{1,0:T(8,128)(2,1)S(1)}, u32[]{:S(2)}, u32[]{:S(2)}) collective-permute-start(bf16[272,128]{1,0:T(8,128)(2,1)S(1)} %add_convert_fusion.1), channel_id=1, source_target_pairs={{0,12},{1,13},{2,14},{3,15},{4,0},{5,1},{6,2},{7,3},{8,4},{9,5},{1... | collective-permute-start | bytes 208904 | tf_op jit(solution)/shard_map/ppermute | solution.py:218
  45.5 1.0 %collective-permute-start.6 = (bf16[272,128]{1,0:T(8,128)(2,1)S(1)}, bf16[272,128]{1,0:T(8,128)(2,1)S(1)}, u32[]{:S(2)}, u32[]{:S(2)}) collective-permute-start(bf16[272,128]{1,0:T(8,128)(2,1)S(1)} %add_convert_fusion.1), channel_id=1, source_target_pairs={{0,8},{1,9},{2,10},{3,11},{4,12},{5,13},{6,14},{7,15},{8,0},{9,1},... | collective-permute-start | bytes 208904 | tf_op jit(solution)/shard_map/ppermute | solution.py:218
  46.5 0.8 collective-permute-start.5
  47.3 0.0 collective-permute-done.7
  47.3 2.9 %collective-permute-done.6 = bf16[272,128]{1,0:T(8,128)(2,1)S(1)} collective-permute-done((bf16[272,128]{1,0:T(8,128)(2,1)S(1)}, bf16[272,128]{1,0:T(8,128)(2,1)S(1)}, u32[]{:S(2)}, u32[]{:S(2)}) %collective-permute-start.6) | collective-permute-done | bytes 69664 | tf_op jit(solution)/shard_map/ppermute | solution.py:218
  50.2 0.7 collective-permute-done.5
  51.0 2.5 %collective-permute-start.10 = (bf16[272,128]{1,0:T(8,128)(2,1)S(1)}, bf16[272,128]{1,0:T(8,128)(2,1)S(1)}, u32[]{:S(2)}, u32[]{:S(2)}) collective-permute-start(bf16[272,128]{1,0:T(8,128)(2,1)S(1)} %add_convert_fusion), channel_id=1, source_target_pairs={{0,96},{16,112},{32,0},{48,16},{64,32},{80,48},{96,64},{112,80},{1... | collective-permute-start | bytes 208904 | tf_op jit(solution)/shard_map/ppermute | solution.py:218
  53.5 0.5 collective-permute-start.9
  54.0 0.6 collective-permute-start.8
  54.7 0.2 collective-permute-done.10
  54.9 3.3 %collective-permute-done.9 = bf16[272,128]{1,0:T(8,128)(2,1)S(1)} collective-permute-done((bf16[272,128]{1,0:T(8,128)(2,1)S(1)}, bf16[272,128]{1,0:T(8,128)(2,1)S(1)}, u32[]{:S(2)}, u32[]{:S(2)}) %collective-permute-start.9) | collective-permute-done | bytes 69664 | tf_op jit(solution)/shard_map/ppermute | solution.py:218
  58.3 0.7 collective-permute-done.8
  58.9 0.8 fusion
  59.7 5.5 %collective-permute-start.11 = (bf16[4,272,128]{2,1,0:T(8,128)(2,1)}, bf16[4,272,128]{2,1,0:T(8,128)(2,1)}, u32[]{:S(2)}, u32[]{:S(2)}) collective-permute-start(bf16[4,272,128]{2,1,0:T(8,128)(2,1)} %get-tuple-element.24), channel_id=1, source_target_pairs={{0,16},{16,0},{32,48},{48,32},{64,80},{80,64},{96,112},{112,96},{1... | collective-permute-start | bytes 835592 | tf_op jit(solution)/shard_map/ppermute | solution.py:289
  65.2 0.1 pad_add_fusion.1.where
  65.3 1.5 %collective-permute-done.11 = bf16[4,272,128]{2,1,0:T(8,128)(2,1)} collective-permute-done((bf16[4,272,128]{2,1,0:T(8,128)(2,1)}, bf16[4,272,128]{2,1,0:T(8,128)(2,1)}, u32[]{:S(2)}, u32[]{:S(2)}) %collective-permute-start.11) | collective-permute-done | bytes 278560 | tf_op jit(solution)/shard_map/ppermute | solution.py:289
  66.7 1.0 %pad_maximum_fusion.pieces = bf16[2,4,272,128]{3,2,1,0:T(8,128)(2,1)S(1)} fusion(bf16[1,4,272,128]{3,2,1,0:T(8,128)(2,1)} %bitcast.17, bf16[1,4,272,128]{3,2,1,0:T(8,128)(2,1)S(1)} %get-tuple-element.23), kind=kLoop, calls=%fused_computation | loop fusion | flops 278528 | bytes 1114112 | tf_op jit(solution)/shard_map/stack | solution.py:290
  67.7 0.0 copy-done.1
  67.7 0.0 copy-start.3
  67.8 1.6 %copy-done.3 = f32[8,256,256]{2,1,0:T(8,128)S(1)} copy-done((f32[8,256,256]{2,1,0:T(8,128)S(1)}, f32[8,256,256]{2,1,0:T(8,128)}, u32[]{:S(2)}) %copy-start.3) | copy-done | bytes 2097176
  69.3 1.6 %copy-done.5 = f32[8,256,256]{2,1,0:T(8,128)S(1)} copy-done((f32[8,256,256]{2,1,0:T(8,128)S(1)}, f32[8,256,256]{2,1,0:T(8,128)}, u32[]{:S(2)}) %copy-start.5) | copy-done | bytes 2097176
  70.9 1.6 %copy-done.7 = f32[8,256,256]{2,1,0:T(8,128)S(1)} copy-done((f32[8,256,256]{2,1,0:T(8,128)S(1)}, f32[8,256,256]{2,1,0:T(8,128)}, u32[]{:S(2)}) %copy-start.7) | copy-done | bytes 2097176
  72.5 1.0 %copy-done.13 = bf16[1024,256]{1,0:T(8,128)(2,1)S(1)} copy-done((bf16[1024,256]{1,0:T(8,128)(2,1)S(1)}, bf16[1024,256]{1,0:T(8,128)(2,1)}, u32[]{:S(2)}) %copy-start.13) | copy-done | bytes 524312
  73.6 1.0 %copy-done.15 = bf16[1024,256]{1,0:T(8,128)(2,1)S(1)} copy-done((bf16[1024,256]{1,0:T(8,128)(2,1)S(1)}, bf16[1024,256]{1,0:T(8,128)(2,1)}, u32[]{:S(2)}) %copy-start.15) | copy-done | bytes 524312
  74.6 11.7 %backward_chain.1 = (f32[16,256]{1,0:T(8,128)}, f32[7,256,256]{2,1,0:T(8,128)}, f32[256,256]{1,0:T(8,128)}) custom-call(s32[3]{0:T(128)S(1)} %pad_add_fusion.1.where, bf16[2,4,272,128]{3,2,1,0:T(8,128)(2,1)S(1)} %pad_maximum_fusion.pieces, f32[8,256,256]{2,1,0:T(8,128)S(1)} %copy-done.1, f32[8,256,256]{2,1,0:T(8,128)S(1)} %copy-done.3, ...), custom_call_target="tpu_custom_call" | custom-call | tf_op jit(solution)/shard_map/backward_chain/pallas_call | solution.py:293
  (8 shorter events, 0.1 us)
Async XLA Ops:
  0.6 9.9 %copy-start.16 = (f32[256,256]{1,0:T(8,128)S(1)}, f32[256,256]{1,0:T(8,128)}, u32[]{:S(2)}) copy-start(f32[256,256]{1,0:T(8,128)} %start.1) | copy-start | bytes 786436
  0.6 26.5 %collective-permute-start.1 = (bf16[1024,256]{1,0:T(8,128)(2,1)}, bf16[1024,256]{1,0:T(8,128)(2,1)}, u32[]{:S(2)}, u32[]{:S(2)}) collective-permute-start(bf16[1024,256]{1,0:T(8,128)(2,1)} %bitcast.21), channel_id=1, source_target_pairs={{1,0},{2,1},{3,2},{4,3},{5,4},{6,5},{7,6},{8,7},{9,8},{10,9},{11,1... | collective-permute-start | bytes 1572872 | tf_op jit(solution)/shard_map/ppermute | solution.py:245
  2.1 25.1 %collective-permute-start = (bf16[1024,256]{1,0:T(8,128)(2,1)}, bf16[1024,256]{1,0:T(8,128)(2,1)}, u32[]{:S(2)}, u32[]{:S(2)}) collective-permute-start(bf16[1024,256]{1,0:T(8,128)(2,1)} %bitcast.22), channel_id=1, source_target_pairs={{0,1},{1,2},{2,3},{3,4},{4,5},{5,6},{6,7},{7,8},{8,9},{9,10},{10,1... | collective-permute-start | bytes 1572872 | tf_op jit(solution)/shard_map/ppermute | solution.py:244
  10.5 1.2 %copy-start.8 = (f32[4,256,256]{2,1,0:T(8,128)S(1)}, f32[4,256,256]{2,1,0:T(8,128)}, u32[]{:S(2)}) copy-start(f32[4,256,256]{2,1,0:T(8,128)} %mats.1) | copy-start | bytes 3145732
  11.8 1.1 %copy-start.10 = (f32[3,256,256]{2,1,0:T(8,128)S(1)}, f32[3,256,256]{2,1,0:T(8,128)}, u32[]{:S(2)}) copy-start(f32[3,256,256]{2,1,0:T(8,128)} %bias.1) | copy-start | bytes 2359300
  12.9 14.2 %copy-start.9 = (bf16[1,8,4,128,128]{4,3,2,1,0:T(8,128)(2,1)S(1)}, bf16[1,8,4,128,128]{4,3,2,1,0:T(8,128)(2,1)}, u32[]{:S(2)}) copy-start(bf16[1,8,4,128,128]{4,3,2,1,0:T(8,128)(2,1)} %param.10) | copy-start | bytes 3145732
  12.9 14.2 %copy-start.11 = (bf16[1,1024,256]{2,1,0:T(8,128)(2,1)S(1)}, bf16[1,1024,256]{2,1,0:T(8,128)(2,1)}, u32[]{:S(2)}) copy-start(bf16[1,1024,256]{2,1,0:T(8,128)(2,1)} %param.8) | copy-start | bytes 1572868
  20.0 1.4 %copy-start = (f32[8,256,256]{2,1,0:T(8,128)}, f32[8,256,256]{2,1,0:T(8,128)S(1)}, u32[]{:S(2)}) copy-start(f32[8,256,256]{2,1,0:T(8,128)S(1)} %get-tuple-element.14.before) | copy-start | bytes 6291460
  21.3 1.3 %copy-start.2 = (f32[8,256,256]{2,1,0:T(8,128)}, f32[8,256,256]{2,1,0:T(8,128)S(1)}, u32[]{:S(2)}) copy-start(f32[8,256,256]{2,1,0:T(8,128)S(1)} %get-tuple-element.15.update) | copy-start | bytes 6291460
  22.6 1.4 %copy-start.4 = (f32[8,256,256]{2,1,0:T(8,128)}, f32[8,256,256]{2,1,0:T(8,128)S(1)}, u32[]{:S(2)}) copy-start(f32[8,256,256]{2,1,0:T(8,128)S(1)} %get-tuple-element.16.reset) | copy-start | bytes 6291460
  24.0 1.4 %copy-start.6 = (f32[8,256,256]{2,1,0:T(8,128)}, f32[8,256,256]{2,1,0:T(8,128)S(1)}, u32[]{:S(2)}) copy-start(f32[8,256,256]{2,1,0:T(8,128)S(1)} %get-tuple-element.17.proposal) | copy-start | bytes 6291460
  25.4 0.8 copy-start.12
  26.2 0.8 copy-start.14
  33.3 34.4 %copy-start.1 = (f32[8,256,256]{2,1,0:T(8,128)S(1)}, f32[8,256,256]{2,1,0:T(8,128)}, u32[]{:S(2)}) copy-start(f32[8,256,256]{2,1,0:T(8,128)} %copy-done) | copy-start | bytes 6291460
  33.3 6.3 %collective-permute-start.4 = (bf16[272,128]{1,0:T(8,128)(2,1)S(1)}, bf16[272,128]{1,0:T(8,128)(2,1)S(1)}, u32[]{:S(2)}, u32[]{:S(2)}) collective-permute-start(bf16[272,128]{1,0:T(8,128)(2,1)S(1)} %edge_products.1), channel_id=1, source_target_pairs={{0,3},{1,0},{2,1},{3,2},{4,7},{5,4},{6,5},{7,6},{8,11},{9,8},{10,9... | collective-permute-start | bytes 208904 | tf_op jit(solution)/shard_map/ppermute | solution.py:218
  37.6 4.8 %collective-permute-start.3 = (bf16[272,128]{1,0:T(8,128)(2,1)S(1)}, bf16[272,128]{1,0:T(8,128)(2,1)S(1)}, u32[]{:S(2)}, u32[]{:S(2)}) collective-permute-start(bf16[272,128]{1,0:T(8,128)(2,1)S(1)} %edge_products.1), channel_id=1, source_target_pairs={{0,2},{1,3},{2,0},{3,1},{4,6},{5,7},{6,4},{7,5},{8,10},{9,11},{10,... | collective-permute-start | bytes 208904 | tf_op jit(solution)/shard_map/ppermute | solution.py:218
  37.6 5.1 %collective-permute-start.2 = (bf16[272,128]{1,0:T(8,128)(2,1)S(1)}, bf16[272,128]{1,0:T(8,128)(2,1)S(1)}, u32[]{:S(2)}, u32[]{:S(2)}) collective-permute-start(bf16[272,128]{1,0:T(8,128)(2,1)S(1)} %edge_products.1), channel_id=1, source_target_pairs={{0,1},{1,2},{2,3},{3,0},{4,5},{5,6},{6,7},{7,4},{8,9},{9,10},{10,1... | collective-permute-start | bytes 208904 | tf_op jit(solution)/shard_map/ppermute | solution.py:218
  42.8 4.5 %collective-permute-start.7 = (bf16[272,128]{1,0:T(8,128)(2,1)S(1)}, bf16[272,128]{1,0:T(8,128)(2,1)S(1)}, u32[]{:S(2)}, u32[]{:S(2)}) collective-permute-start(bf16[272,128]{1,0:T(8,128)(2,1)S(1)} %add_convert_fusion.1), channel_id=1, source_target_pairs={{0,12},{1,13},{2,14},{3,15},{4,0},{5,1},{6,2},{7,3},{8,4},{9,5},{1... | collective-permute-start | bytes 208904 | tf_op jit(solution)/shard_map/ppermute | solution.py:218
  45.5 4.7 %collective-permute-start.6 = (bf16[272,128]{1,0:T(8,128)(2,1)S(1)}, bf16[272,128]{1,0:T(8,128)(2,1)S(1)}, u32[]{:S(2)}, u32[]{:S(2)}) collective-permute-start(bf16[272,128]{1,0:T(8,128)(2,1)S(1)} %add_convert_fusion.1), channel_id=1, source_target_pairs={{0,8},{1,9},{2,10},{3,11},{4,12},{5,13},{6,14},{7,15},{8,0},{9,1},... | collective-permute-start | bytes 208904 | tf_op jit(solution)/shard_map/ppermute | solution.py:218
  46.5 4.4 %collective-permute-start.5 = (bf16[272,128]{1,0:T(8,128)(2,1)S(1)}, bf16[272,128]{1,0:T(8,128)(2,1)S(1)}, u32[]{:S(2)}, u32[]{:S(2)}) collective-permute-start(bf16[272,128]{1,0:T(8,128)(2,1)S(1)} %add_convert_fusion.1), channel_id=1, source_target_pairs={{0,4},{1,5},{2,6},{3,7},{4,8},{5,9},{6,10},{7,11},{8,12},{9,13},{1... | collective-permute-start | bytes 208904 | tf_op jit(solution)/shard_map/ppermute | solution.py:218
  51.0 3.9 %collective-permute-start.10 = (bf16[272,128]{1,0:T(8,128)(2,1)S(1)}, bf16[272,128]{1,0:T(8,128)(2,1)S(1)}, u32[]{:S(2)}, u32[]{:S(2)}) collective-permute-start(bf16[272,128]{1,0:T(8,128)(2,1)S(1)} %add_convert_fusion), channel_id=1, source_target_pairs={{0,96},{16,112},{32,0},{48,16},{64,32},{80,48},{96,64},{112,80},{1... | collective-permute-start | bytes 208904 | tf_op jit(solution)/shard_map/ppermute | solution.py:218
  53.5 4.7 %collective-permute-start.9 = (bf16[272,128]{1,0:T(8,128)(2,1)S(1)}, bf16[272,128]{1,0:T(8,128)(2,1)S(1)}, u32[]{:S(2)}, u32[]{:S(2)}) collective-permute-start(bf16[272,128]{1,0:T(8,128)(2,1)S(1)} %add_convert_fusion), channel_id=1, source_target_pairs={{0,64},{16,80},{32,96},{48,112},{64,0},{80,16},{96,32},{112,48},{1... | collective-permute-start | bytes 208904 | tf_op jit(solution)/shard_map/ppermute | solution.py:218
  54.0 4.9 %collective-permute-start.8 = (bf16[272,128]{1,0:T(8,128)(2,1)S(1)}, bf16[272,128]{1,0:T(8,128)(2,1)S(1)}, u32[]{:S(2)}, u32[]{:S(2)}) collective-permute-start(bf16[272,128]{1,0:T(8,128)(2,1)S(1)} %add_convert_fusion), channel_id=1, source_target_pairs={{0,32},{16,48},{32,64},{48,80},{64,96},{80,112},{96,0},{112,16},{1... | collective-permute-start | bytes 208904 | tf_op jit(solution)/shard_map/ppermute | solution.py:218
  59.7 7.0 %collective-permute-start.11 = (bf16[4,272,128]{2,1,0:T(8,128)(2,1)}, bf16[4,272,128]{2,1,0:T(8,128)(2,1)}, u32[]{:S(2)}, u32[]{:S(2)}) collective-permute-start(bf16[4,272,128]{2,1,0:T(8,128)(2,1)} %get-tuple-element.24), channel_id=1, source_target_pairs={{0,16},{16,0},{32,48},{48,32},{64,80},{80,64},{96,112},{112,96},{1... | collective-permute-start | bytes 835592 | tf_op jit(solution)/shard_map/ppermute | solution.py:289
  67.7 1.6 %copy-start.3 = (f32[8,256,256]{2,1,0:T(8,128)S(1)}, f32[8,256,256]{2,1,0:T(8,128)}, u32[]{:S(2)}) copy-start(f32[8,256,256]{2,1,0:T(8,128)} %copy-done.2) | copy-start | bytes 6291460
  69.3 1.6 %copy-start.5 = (f32[8,256,256]{2,1,0:T(8,128)S(1)}, f32[8,256,256]{2,1,0:T(8,128)}, u32[]{:S(2)}) copy-start(f32[8,256,256]{2,1,0:T(8,128)} %copy-done.4) | copy-start | bytes 6291460
  70.9 1.6 %copy-start.7 = (f32[8,256,256]{2,1,0:T(8,128)S(1)}, f32[8,256,256]{2,1,0:T(8,128)}, u32[]{:S(2)}) copy-start(f32[8,256,256]{2,1,0:T(8,128)} %copy-done.6) | copy-start | bytes 6291460
  72.5 1.0 %copy-start.13 = (bf16[1024,256]{1,0:T(8,128)(2,1)S(1)}, bf16[1024,256]{1,0:T(8,128)(2,1)}, u32[]{:S(2)}) copy-start(bf16[1024,256]{1,0:T(8,128)(2,1)} %copy-done.12) | copy-start | bytes 1572868
  73.6 1.0 %copy-start.15 = (bf16[1024,256]{1,0:T(8,128)(2,1)S(1)}, bf16[1024,256]{1,0:T(8,128)(2,1)}, u32[]{:S(2)}) copy-start(bf16[1024,256]{1,0:T(8,128)(2,1)} %copy-done.14) | copy-start | bytes 1572868
where the time goes:
time: 86.9 us; the launch traced here: 86.3 us
  starting transfers between devices  25.5 us (29%)
  Pallas kernels  24.9 us (29%)
  local copies, waits for them, and re-layouts  19.3 us (22%)
  waiting for transfers between devices  13.8 us (16%)
  other arithmetic  2 us (2%)
    unnamed x34, local copies, waits for them, and re-layouts  16.3 us
    ppermute x9, starting transfers between devices, ring_parts(): parts.append(lax.ppermute(block, axis, route))  13.1 us
    ppermute x9, waiting for transfers between devices, ring_parts(): parts.append(lax.ppermute(block, axis, route))  12.4 us
    pallas_call x1, Pallas kernels, body(): pl.pallas_call(backward_kernel, out_shape=[jax.ShapeDtypeStruct((share, w...  11.7 us
    pallas_call x1, Pallas kernels, body(): pl.pallas_call(forward_kernel, out_shape=[wide, wide, wide, wide, jax.Sha...  7.04 us
    pallas_call x1, Pallas kernels, body(): pl.pallas_call(functools.partial(edge_kernel, factor), out_shape=jax.Shap...  6.16 us
    ppermute x1, starting transfers between devices, body(): other = lax.ppermute(along, 'snap', [(i, i ^ 1) for i in range(snap_count)])  5.5 us
    ppermute x1, starting transfers between devices, body(): lax.ppermute(own[rows - HALO:], 'node', [(i, i + 1) for i in range(ends)])  5.47 us
  transfers between devices with their start and end apart: 12, of which 9 were waited for; matrix products, arithmetic and copies ran while one was open for 4% of the time, Pallas kernels for 8%

commit v1 on v0

--- a/solution.py
+++ b/solution.py
@@ -71,7 +71,21 @@
 
 
 def edge_kernel(
-    factor, where, ids, own, left, right, tiles, columns, low, packed, extended, aggregated, picked
+    factor,
+    ids,
+    own,
+    left,
+    right,
+    tiles,
+    pos,
+    neg,
+    low,
+    first_out,
+    second_out,
+    third_out,
+    extended,
+    aggregated,
+    picked,
 ):
     rows, width = own.shape
     side = tiles.shape[1]
@@ -86,16 +100,26 @@
             total = total + dot(tiles[b * per_block + k], extended[ids[b, k]])
         aggregated[pl.ds(b * side, side), :] = total.astype(BF16)
 
-    count = columns.shape[0]
+    edges = pos.shape[1]
     chunk = 512
-    for c in range(count // chunk):
-        index = columns[pl.ds(c * chunk, chunk), :]
-        lane = lax.broadcasted_iota(jnp.int32, (chunk, rows), 1)
-        onehot = (lane == index).astype(F32).astype(BF16)
+    lane = lax.broadcasted_iota(jnp.int32, (chunk, side), 1)
+    for c in range(4 * edges // chunk):
+        end, offset = divmod(c * chunk, edges)
+        source = (pos, neg)[end // 2]
+        turned = [
+            jnp.broadcast_to(
+                source[pl.ds(end % 2, 1), pl.ds(offset + part * side, side)], (side, side)
+            ).T
+            for part in range(chunk // side)
+        ]
+        index = jnp.concatenate(turned, axis=0)
+        onehot = jnp.concatenate(
+            [(index == lane + part * side).astype(F32).astype(BF16) for part in range(rows // side)],
+            axis=1,
+        )
         picked[pl.ds(c * chunk, chunk), :] = dot(onehot, aggregated[...]).astype(BF16)
 
-    weight_low = low[where[0]]
-    edges = count // 4
+    weight_low = low[lax.axis_index("snap")]
     half = jnp.zeros((width, width), F32)
     for sign in (0, 1):
         first = picked[pl.ds(2 * sign * edges, edges), :]
@@ -115,16 +139,18 @@
     i = lax.broadcasted_iota(jnp.int32, (quarter, quarter), 0)
     j = lax.broadcasted_iota(jnp.int32, (quarter, quarter), 1)
     diagonal = jnp.sum(jnp.where(i == j, lower, 0.0), axis=0, keepdims=True)
-    packed[pl.ds(0, quarter), :] = full[:quarter, quarter:].astype(BF16)
-    packed[pl.ds(quarter, quarter), :] = jnp.where(i <= j, upper, lower).astype(BF16)
-    packed[pl.ds(2 * quarter, PACK_EXTRA), :] = jnp.broadcast_to(
-        diagonal, (PACK_EXTRA, quarter)
-    ).astype(BF16)
+    corner = full[:quarter, quarter:].astype(BF16)
+    mixed = jnp.where(i <= j, upper, lower).astype(BF16)
+    extra = jnp.broadcast_to(diagonal, (PACK_EXTRA, quarter)).astype(BF16)
+    for packed in (first_out, second_out, third_out):
+        packed[pl.ds(0, quarter), :] = corner
+        packed[pl.ds(quarter, quarter), :] = mixed
+        packed[pl.ds(2 * quarter, PACK_EXTRA), :] = extra
 
 
 def backward_kernel(
-    where,
-    pieces,
+    along,
+    other,
     before,
     update,
     reset,
@@ -142,7 +168,8 @@
 ):
     steps, width = low.shape[0], low.shape[1]
     quarter = width // 2
-    x, core, node = where[0], where[1], where[2]
+    place, node = lax.axis_index("snap"), lax.axis_index("node")
+    x, core = lax.div(place, 2), lax.rem(place, 2)
     for k in range(4):
         area = pl.ds(k * width, width)
         flipped_high[k] = mats_high[area, :].T
@@ -150,9 +177,8 @@
     i = lax.broadcasted_iota(jnp.int32, (quarter, quarter), 0)
     j = lax.broadcasted_iota(jnp.int32, (quarter, quarter), 1)
     for t in range(steps):
-        side = lax.rem(core + t % 2, 2)
         turn = lax.rem(x - t // 2 + RING, RING)
-        piece = pieces[side, turn]
+        piece = jnp.where(core == t % 2, along[turn], other[turn])
         corner = piece[:quarter]
         mixed = piece[quarter : 2 * quarter].astype(F32)
         diagonal = piece[2 * quarter :].astype(F32)[0:1]
@@ -183,11 +209,11 @@
         fresh = fresh + dot3((flipped_high[0], flipped_low[0]), d0_parts)
         fresh = fresh + dot3((flipped_high[2], flipped_low[2]), d2_parts)
         fresh = fresh + dot3((flipped_high[1], flipped_low[1]), d1_parts)
-        weight_parts = split(weight)
-        grads[0] += dot3(d0_parts, weight_parts, LANES)
-        grads[1] += dot3(d1_parts, weight_parts, LANES)
-        grads[2] += dot3(d2_parts, weight_parts, LANES)
-        grads[3] += dot3(d2_parts, split(r * weight), LANES)
+        weight_high = weight.astype(BF16)
+        grads[0] += dot(d0_parts[0], weight_high, LANES)
+        grads[1] += dot(d1_parts[0], weight_high, LANES)
+        grads[2] += dot(d2_parts[0], weight_high, LANES)
+        grads[3] += dot(d2_parts[0], (r * weight).astype(BF16), LANES)
         grads[4] += d0
         grads[5] += d1
         grads[6] += d2
@@ -196,7 +222,7 @@
     initial_grad[...] = lax.fori_loop(0, steps, step, jnp.zeros((width, width), F32))
     share = adjoint_rows.shape[0]
     start = pl.multiple_of(node * share, share)
-    adjoint_rows[...] = adjoints[2 * x + core, pl.ds(start, share), :]
+    adjoint_rows[...] = adjoints[place, pl.ds(start, share), :]
 
 
 def params(megabytes):
@@ -207,24 +233,36 @@
 SMEM = pl.BlockSpec(memory_space=pltpu.SMEM)
 
 
-def ring_parts(block, axis, stride, count):
+def ring_parts(copies, axis, stride, count):
     size = lax.axis_size(axis)
     span = stride * count
     parts = []
     for turn in range(1, count):
-        route = [
-            (i, i - i % span + (i % span + turn * stride) % span) for i in range(size)
-        ]
-        parts.append(lax.ppermute(block, axis, route))
+        route = [(i, i - i % span + (i % span + turn * stride) % span) for i in range(size)]
+        parts.append(lax.ppermute(copies[turn - 1], axis, route))
     return parts
 
 
-def ring_sum(block, axis, stride, count):
-    parts = ring_parts(block, axis, stride, count)
-    total = block.astype(F32)
-    for part in parts:
-        total = total + part.astype(F32)
-    return total.astype(BF16)
+def sum_kernel(own, first, second, third, *copies):
+    total = (own[...].astype(F32) + first[...].astype(F32)) + (
+        second[...].astype(F32) + third[...].astype(F32)
+    )
+    total = total.astype(BF16)
+    for copy in copies:
+        copy[...] = total
+
+
+def ring_sum(copies, axis, stride, count):
+    parts = ring_parts(copies, axis, stride, count)
+    like = jax.ShapeDtypeStruct(copies[0].shape, BF16)
+    return pl.pallas_call(
+        sum_kernel,
+        out_shape=[like] * 3,
+        in_specs=[VMEM] * 4,
+        out_specs=[VMEM] * 3,
+        compiler_params=params(4),
+        name="ring_sum",
+    )(copies[0], *parts)
 
 
 def body(
@@ -232,12 +270,9 @@
 ):
     snap_count = lax.axis_size("snap")
     node_count = lax.axis_size("node")
-    place = lax.axis_index("snap")
-    node = lax.axis_index("node")
     own = features[0]
     rows, width = own.shape
     side = tile_values.shape[-1]
-    per_block = tile_ids.shape[-1]
     square = (snap_count, width, width)
 
     ends = node_count - 1
@@ -251,43 +286,39 @@
         out_shape=[wide, wide, wide, wide, jax.ShapeDtypeStruct(square, BF16), tall, tall],
         in_specs=[VMEM] * 3,
         out_specs=[VMEM] * 7,
-        compiler_params=params(32),
+        compiler_params=params(16),
         name="forward_chain",
     )(initial_weight, gate_mats, gate_bias)
 
-    columns = jnp.concatenate(
-        [pos_edges[0, 0], pos_edges[0, 1], neg_edges[0, 0], neg_edges[0, 1]]
-    ).reshape(-1, 1)
     factor = float(rows * node_count) ** (-0.5)
     pack_rows = width + PACK_EXTRA
-    packed = pl.pallas_call(
+    copies = pl.pallas_call(
         functools.partial(edge_kernel, factor),
-        out_shape=jax.ShapeDtypeStruct((pack_rows, width // 2), BF16),
-        in_specs=[SMEM, SMEM] + [VMEM] * 6,
-        out_specs=VMEM,
+        out_shape=[jax.ShapeDtypeStruct((pack_rows, width // 2), BF16)] * 3,
+        in_specs=[SMEM] + [VMEM] * 7,
+        out_specs=[VMEM] * 3,
         scratch_shapes=[
             pltpu.VMEM(((rows + 2 * HALO) // side, side, width), BF16),
             pltpu.VMEM((rows, width), BF16),
-            pltpu.VMEM((columns.shape[0], width), BF16),
+            pltpu.VMEM((4 * pos_edges.shape[-1], width), BF16),
         ],
-        compiler_params=params(40),
+        compiler_params=params(16),
         name="edge_products",
     )(
-        jnp.stack([place, node]),
         tile_ids[0],
         own,
         left,
         right,
         tile_values.reshape(-1, side, side),
-        columns,
+        pos_edges[0],
+        neg_edges[0],
         low,
     )
 
-    packed = ring_sum(packed, "node", 1, RING)
-    packed = ring_sum(packed, "node", RING, node_count // RING)
-    along = jnp.stack([packed] + ring_parts(packed, "snap", 2, snap_count // 2))
+    copies = ring_sum(copies, "node", 1, RING)
+    copies = ring_sum(copies, "node", RING, node_count // RING)
+    along = jnp.stack([copies[0]] + ring_parts(copies, "snap", 2, snap_count // 2))
     other = lax.ppermute(along, "snap", [(i, i ^ 1) for i in range(snap_count)])
-    pieces = jnp.stack([along, other])
 
     share = width // node_count
     adjoint_rows, grads, initial_grad = pl.pallas_call(
@@ -297,7 +328,7 @@
             jax.ShapeDtypeStruct((7, width, width), F32),
             jax.ShapeDtypeStruct((width, width), F32),
         ],
-        in_specs=[SMEM] + [VMEM] * 8,
+        in_specs=[VMEM] * 9,
         out_specs=[VMEM] * 3,
         scratch_shapes=[
             pltpu.VMEM((4, width, width), BF16),
@@ -305,11 +336,11 @@
             pltpu.VMEM(square, F32),
             pltpu.VMEM(square, F32),
         ],
-        compiler_params=params(40),
+        compiler_params=params(16),
         name="backward_chain",
     )(
-        jnp.stack([place // 2, place % 2, node]),
-        pieces,
+        along,
+        other,
         before,
         update,
         reset,

time: 86.9 us -> 67.1 us (0.77)
  local copies, waits for them, and re-layouts: 19.3 us -> 4.08 us
  Pallas kernels: 24.9 us -> 21.6 us
  other arithmetic: 2 us -> 0.04 us
  starting transfers between devices: 25.5 us -> 27.3 us
    unnamed x34 -> x14, local copies, waits for them, and re-layouts: 16.3 us -> 3.32 us
    pallas_call x1, Pallas kernels: 11.7 us -> 8.96 us  [body(): pl.pallas_call(backward_kernel, out_shape=[jax.ShapeDtypeStruct((share, w...]
    ppermute x9, starting transfers between devices: 13.1 us -> 15.6 us  [ring_parts(): parts.append(lax.ppermute(copies[turn - 1], axis, route))]
    another operation x4 -> x1, other arithmetic: 1.91 us -> 0.04 us  [body(): jnp.stack([copies[0]] + ring_parts(copies, 'snap', 2, snap_count // 2))]
    slice x2 -> x0, local copies, waits for them, and re-layouts: 1.56 us -> none  [the longest x1 0.78 us: body(): pos_edges[0, 0]]
    pallas_call x1 -> x3, Pallas kernels: 6.16 us -> 5.65 us  [the longest x1 5.58 us: body(): pl.pallas_call(functools.partial(edge_kernel, factor), out_shape=[jax.Sha...]
  transfers between devices with their start and end apart: 12 -> 12, of which waited for: 9 -> 9; matrix products, arithmetic and copies ran while one was open for 4% -> 1% of each run, Pallas kernels for 8% -> 11%
where the time goes in v1:
time: 67.1 us; the launch traced here: 66.8 us
  starting transfers between devices  27.3 us (41%)
  Pallas kernels  21.6 us (32%)
  waiting for transfers between devices  13 us (19%)
  local copies, waits for them, and re-layouts  4.08 us (6%)
  between operations  0.74 us (1%)
    ppermute x9, starting transfers between devices, ring_parts(): parts.append(lax.ppermute(copies[turn - 1], axis, route))  15.6 us
    ppermute x9, waiting for transfers between devices, ring_parts(): parts.append(lax.ppermute(copies[turn - 1], axis, route))  11.8 us
    pallas_call x1, Pallas kernels, body(): pl.pallas_call(backward_kernel, out_shape=[jax.ShapeDtypeStruct((share, w...  8.96 us
    pallas_call x1, Pallas kernels, body(): pl.pallas_call(forward_kernel, out_shape=[wide, wide, wide, wide, jax.Sha...  7.04 us
    ppermute x1, starting transfers between devices, body(): other = lax.ppermute(along, 'snap', [(i, i ^ 1) for i in range(snap_count)])  5.67 us
    pallas_call x1, Pallas kernels, body(): pl.pallas_call(functools.partial(edge_kernel, factor), out_shape=[jax.Sha...  5.58 us
    ppermute x1, starting transfers between devices, body(): lax.ppermute(own[rows - HALO:], 'node', [(i, i + 1) for i in range(ends)])  4.7 us
    unnamed x14, local copies, waits for them, and re-layouts  3.32 us
  transfers between devices with their start and end apart: 12, of which 9 were waited for; matrix products, arithmetic and copies ran while one was open for 1% of the time, Pallas kernels for 11%

profile of v1, /device:TPU:1, one launch (start us, length us, event | category | flops | bytes accessed | tf_op | source)
XLA Modules:
  0.0 66.8 jit_solution(16030787663624395942)
XLA Ops:
  0.6 0.0 copy-start.5
  0.6 1.3 %collective-permute-start.1 = (bf16[1024,256]{1,0:T(8,128)(2,1)}, bf16[1024,256]{1,0:T(8,128)(2,1)S(1)}, u32[]{:S(2)}, u32[]{:S(2)}) collective-permute-start(bf16[1024,256]{1,0:T(8,128)(2,1)} %bitcast.11), channel_id=1, source_target_pairs={{1,0},{2,1},{3,2},{4,3},{5,4},{6,5},{7,6},{8,7},{9,8},{10,9},{11,1... | collective-permute-start | bytes 1572872 | tf_op jit(solution)/shard_map/ppermute | solution.py:280
  1.9 4.7 %collective-permute-start = (bf16[1024,256]{1,0:T(8,128)(2,1)}, bf16[1024,256]{1,0:T(8,128)(2,1)S(1)}, u32[]{:S(2)}, u32[]{:S(2)}) collective-permute-start(bf16[1024,256]{1,0:T(8,128)(2,1)} %bitcast.12), channel_id=1, source_target_pairs={{0,1},{1,2},{2,3},{3,4},{4,5},{5,6},{6,7},{7,8},{8,9},{9,10},{10,1... | collective-permute-start | bytes 1572872 | tf_op jit(solution)/shard_map/ppermute | solution.py:279
  6.6 0.8 %copy.11.ids = s32[8,4]{1,0:T(8,128)S(1)} copy(s32[8,4]{0,1:T(4,128)} %bitcast.20) | data formatting | bytes 256 | tf_op jit(solution)/shard_map/squeeze | solution.py:308
  7.4 0.0 copy-start
  7.4 1.2 %copy-done = f32[4,256,256]{2,1,0:T(8,128)S(1)} copy-done((f32[4,256,256]{2,1,0:T(8,128)S(1)}, f32[4,256,256]{2,1,0:T(8,128)}, u32[]{:S(2)}) %copy-start) | copy-done | bytes 1048600
  8.6 0.0 copy-start.2
  8.6 1.1 %copy-done.2 = f32[3,256,256]{2,1,0:T(8,128)S(1)} copy-done((f32[3,256,256]{2,1,0:T(8,128)S(1)}, f32[3,256,256]{2,1,0:T(8,128)}, u32[]{:S(2)}) %copy-start.2) | copy-done | bytes 786456
  9.8 0.0 copy-start.4
  9.8 0.9 %copy-done.4 = f32[256,256]{1,0:T(8,128)S(1)} copy-done((f32[256,256]{1,0:T(8,128)S(1)}, f32[256,256]{1,0:T(8,128)}, u32[]{:S(2)}) %copy-start.4) | copy-done | bytes 262168
  10.7 0.0 copy-start.1
  10.7 0.0 copy-start.3
  10.7 0.0 copy-start.6
  10.7 7.0 %forward_chain.1 = (f32[8,256,256]{2,1,0:T(8,128)S(1)}, f32[8,256,256]{2,1,0:T(8,128)S(1)}, f32[8,256,256]{2,1,0:T(8,128)S(1)}, f32[8,256,256]{2,1,0:T(8,128)S(1...) custom-call(f32[256,256]{1,0:T(8,128)S(1)} %copy-done.4, ...), custom_call_target="tpu_custom_call" | custom-call | tf_op jit(solution)/shard_map/forward_chain/pallas_call | solution.py:284
  17.8 0.0 collective-permute-done.1.right
  17.8 0.0 collective-permute-done.left
  17.8 0.0 copy-done.5
  17.8 0.0 copy-done.1
  17.8 0.0 copy-done.3
  17.8 0.0 copy-done.6
  17.8 5.6 %edge_products.1 = (bf16[272,128]{1,0:T(8,128)(2,1)S(1)}, bf16[272,128]{1,0:T(8,128)(2,1)S(1)}, bf16[272,128]{1,0:T(8,128)(2,1)S(1)}) custom-call(s32[8,4]{1,0:T(8,128)S(1)} %copy.11.ids, bf16[1024,256]{1,0:T(8,128)(2,1)S(1)} %bitcast.13, bf16[1024,256]{1,0:T(8,128)(2,1)S(1)} %collective-permute-done.left, ...), custom_call_target="tpu_custom_call" | custom-call | tf_op jit(solution)/shard_map/edge_products/pallas_call | solution.py:295
  23.4 3.3 %collective-permute-start.3 = (bf16[272,128]{1,0:T(8,128)(2,1)S(1)}, bf16[272,128]{1,0:T(8,128)(2,1)S(1)}, u32[]{:S(2)}, u32[]{:S(2)}) collective-permute-start(bf16[272,128]{1,0:T(8,128)(2,1)S(1)} %get-tuple-element.24), channel_id=1, source_target_pairs={{0,2},{1,3},{2,0},{3,1},{4,6},{5,7},{6,4},{7,5},{8,10},{9,11},{10,... | collective-permute-start | bytes 208904 | tf_op jit(solution)/shard_map/ppermute | solution.py:242
  26.7 1.8 %collective-permute-start.4 = (bf16[272,128]{1,0:T(8,128)(2,1)S(1)}, bf16[272,128]{1,0:T(8,128)(2,1)S(1)}, u32[]{:S(2)}, u32[]{:S(2)}) collective-permute-start(bf16[272,128]{1,0:T(8,128)(2,1)S(1)} %get-tuple-element.25), channel_id=1, source_target_pairs={{0,3},{1,0},{2,1},{3,2},{4,7},{5,4},{6,5},{7,6},{8,11},{9,8},{10,9... | collective-permute-start | bytes 208904 | tf_op jit(solution)/shard_map/ppermute | solution.py:242
  28.5 0.5 collective-permute-start.2
  29.0 0.0 collective-permute-done.3.second
  29.0 2.4 %collective-permute-done.4.third = bf16[272,128]{1,0:T(8,128)(2,1)S(1)} collective-permute-done((bf16[272,128]{1,0:T(8,128)(2,1)S(1)}, bf16[272,128]{1,0:T(8,128)(2,1)S(1)}, u32[]{:S(2)}, u32[]{:S(2)}) %collective-permute-start.4) | collective-permute-done | bytes 69664 | tf_op jit(solution)/shard_map/ppermute | solution.py:242
  31.5 1.4 %collective-permute-done.2.first = bf16[272,128]{1,0:T(8,128)(2,1)S(1)} collective-permute-done((bf16[272,128]{1,0:T(8,128)(2,1)S(1)}, bf16[272,128]{1,0:T(8,128)(2,1)S(1)}, u32[]{:S(2)}, u32[]{:S(2)}) %collective-permute-start.2) | collective-permute-done | bytes 69664 | tf_op jit(solution)/shard_map/ppermute | solution.py:242
  33.0 4.2 %collective-permute-start.6 = (bf16[272,128]{1,0:T(8,128)(2,1)S(1)}, bf16[272,128]{1,0:T(8,128)(2,1)S(1)}, u32[]{:S(2)}, u32[]{:S(2)}) collective-permute-start(bf16[272,128]{1,0:T(8,128)(2,1)S(1)} %get-tuple-element.27), channel_id=1, source_target_pairs={{0,8},{1,9},{2,10},{3,11},{4,12},{5,13},{6,14},{7,15},{8,0},{9,1},... | collective-permute-start | bytes 208904 | tf_op jit(solution)/shard_map/ppermute | solution.py:242
  37.2 0.5 collective-permute-start.7
  37.7 0.9 %collective-permute-start.5 = (bf16[272,128]{1,0:T(8,128)(2,1)S(1)}, bf16[272,128]{1,0:T(8,128)(2,1)S(1)}, u32[]{:S(2)}, u32[]{:S(2)}) collective-permute-start(bf16[272,128]{1,0:T(8,128)(2,1)S(1)} %get-tuple-element.26.own), channel_id=1, source_target_pairs={{0,4},{1,5},{2,6},{3,7},{4,8},{5,9},{6,10},{7,11},{8,12},{9,13},{1... | collective-permute-start | bytes 208904 | tf_op jit(solution)/shard_map/ppermute | solution.py:242
  38.6 0.2 collective-permute-done.6.second
  38.9 1.8 %collective-permute-done.7.third = bf16[272,128]{1,0:T(8,128)(2,1)S(1)} collective-permute-done((bf16[272,128]{1,0:T(8,128)(2,1)S(1)}, bf16[272,128]{1,0:T(8,128)(2,1)S(1)}, u32[]{:S(2)}, u32[]{:S(2)}) %collective-permute-start.7) | collective-permute-done | bytes 69664 | tf_op jit(solution)/shard_map/ppermute | solution.py:242
  40.6 2.2 %collective-permute-done.5.first = bf16[272,128]{1,0:T(8,128)(2,1)S(1)} collective-permute-done((bf16[272,128]{1,0:T(8,128)(2,1)S(1)}, bf16[272,128]{1,0:T(8,128)(2,1)S(1)}, u32[]{:S(2)}, u32[]{:S(2)}) %collective-permute-start.5) | collective-permute-done | bytes 69664 | tf_op jit(solution)/shard_map/ppermute | solution.py:242
  42.9 2.8 %collective-permute-start.9 = (bf16[272,128]{1,0:T(8,128)(2,1)S(1)}, bf16[272,128]{1,0:T(8,128)(2,1)S(1)}, u32[]{:S(2)}, u32[]{:S(2)}) collective-permute-start(bf16[272,128]{1,0:T(8,128)(2,1)S(1)} %get-tuple-element.30), channel_id=1, source_target_pairs={{0,64},{16,80},{32,96},{48,112},{64,0},{80,16},{96,32},{112,48},{1... | collective-permute-start | bytes 208904 | tf_op jit(solution)/shard_map/ppermute | solution.py:242
  45.7 0.9 %collective-permute-start.10 = (bf16[272,128]{1,0:T(8,128)(2,1)S(1)}, bf16[272,128]{1,0:T(8,128)(2,1)S(1)}, u32[]{:S(2)}, u32[]{:S(2)}) collective-permute-start(bf16[272,128]{1,0:T(8,128)(2,1)S(1)} %get-tuple-element.31), channel_id=1, source_target_pairs={{0,96},{16,112},{32,0},{48,16},{64,32},{80,48},{96,64},{112,80},{1... | collective-permute-start | bytes 208904 | tf_op jit(solution)/shard_map/ppermute | solution.py:242
  46.5 0.6 collective-permute-start.8
  47.1 0.5 collective-permute-done.9
  47.6 1.2 %collective-permute-done.10 = bf16[272,128]{1,0:T(8,128)(2,1)S(1)} collective-permute-done((bf16[272,128]{1,0:T(8,128)(2,1)S(1)}, bf16[272,128]{1,0:T(8,128)(2,1)S(1)}, u32[]{:S(2)}, u32[]{:S(2)}) %collective-permute-start.10) | collective-permute-done | bytes 69664 | tf_op jit(solution)/shard_map/ppermute | solution.py:242
  48.8 2.1 %collective-permute-done.8 = bf16[272,128]{1,0:T(8,128)(2,1)S(1)} collective-permute-done((bf16[272,128]{1,0:T(8,128)(2,1)S(1)}, bf16[272,128]{1,0:T(8,128)(2,1)S(1)}, u32[]{:S(2)}, u32[]{:S(2)}) %collective-permute-start.8) | collective-permute-done | bytes 69664 | tf_op jit(solution)/shard_map/ppermute | solution.py:242
  51.0 5.7 %collective-permute-start.11 = (bf16[4,272,128]{2,1,0:T(8,128)(2,1)S(1)}, bf16[4,272,128]{2,1,0:T(8,128)(2,1)S(1)}, u32[]{:S(2)}, u32[]{:S(2)}) collective-permute-start(bf16[4,272,128]{2,1,0:T(8,128)(2,1)S(1)} %pad_maximum_fusion.along), channel_id=1, source_target_pairs={{0,16},{16,0},{32,48},{48,32},{64,80},{80,64},{96,112},{112,96},{1... | collective-permute-start | bytes 835592 | tf_op jit(solution)/shard_map/ppermute | solution.py:321
  56.6 1.2 %collective-permute-done.11.other = bf16[4,272,128]{2,1,0:T(8,128)(2,1)S(1)} collective-permute-done((bf16[4,272,128]{2,1,0:T(8,128)(2,1)S(1)}, bf16[4,272,128]{2,1,0:T(8,128)(2,1)S(1)}, u32[]{:S(2)}, u32[]{:S(2)}) %collective-permute-start.11) | collective-permute-done | bytes 278560 | tf_op jit(solution)/shard_map/ppermute | solution.py:321
  57.8 9.0 %backward_chain.1 = (f32[16,256]{1,0:T(8,128)}, f32[7,256,256]{2,1,0:T(8,128)}, f32[256,256]{1,0:T(8,128)}) custom-call(bf16[4,272,128]{2,1,0:T(8,128)(2,1)S(1)} %pad_maximum_fusion.along, bf16[4,272,128]{2,1,0:T(8,128)(2,1)S(1)} %collective-permute-done.11.other, f32[8,256,256]{2,1,0:T(8,128)S(1)} %get-tuple-element.32.before, ...), custom_call_target="tpu_custom_call" | custom-call | tf_op jit(solution)/shard_map/backward_chain/pallas_call | solution.py:324
  (3 shorter events, 0.1 us)
Async XLA Ops:
  0.6 17.2 %copy-start.5 = (s32[1,2,1024]{2,1,0:T(2,128)S(1)}, s32[1,2,1024]{2,1,0:T(2,128)}, u32[]{:S(2)}) copy-start(s32[1,2,1024]{2,1,0:T(2,128)} %param.11) | copy-start | bytes 24580
  0.6 17.1 %collective-permute-start.1 = (bf16[1024,256]{1,0:T(8,128)(2,1)}, bf16[1024,256]{1,0:T(8,128)(2,1)S(1)}, u32[]{:S(2)}, u32[]{:S(2)}) collective-permute-start(bf16[1024,256]{1,0:T(8,128)(2,1)} %bitcast.11), channel_id=1, source_target_pairs={{1,0},{2,1},{3,2},{4,3},{5,4},{6,5},{7,6},{8,7},{9,8},{10,9},{11,1... | collective-permute-start | bytes 1572872 | tf_op jit(solution)/shard_map/ppermute | solution.py:280
  1.9 15.8 %collective-permute-start = (bf16[1024,256]{1,0:T(8,128)(2,1)}, bf16[1024,256]{1,0:T(8,128)(2,1)S(1)}, u32[]{:S(2)}, u32[]{:S(2)}) collective-permute-start(bf16[1024,256]{1,0:T(8,128)(2,1)} %bitcast.12), channel_id=1, source_target_pairs={{0,1},{1,2},{2,3},{3,4},{4,5},{5,6},{6,7},{7,8},{8,9},{9,10},{10,1... | collective-permute-start | bytes 1572872 | tf_op jit(solution)/shard_map/ppermute | solution.py:279
  7.4 1.2 %copy-start = (f32[4,256,256]{2,1,0:T(8,128)S(1)}, f32[4,256,256]{2,1,0:T(8,128)}, u32[]{:S(2)}) copy-start(f32[4,256,256]{2,1,0:T(8,128)} %mats.1) | copy-start | bytes 3145732
  8.6 1.1 %copy-start.2 = (f32[3,256,256]{2,1,0:T(8,128)S(1)}, f32[3,256,256]{2,1,0:T(8,128)}, u32[]{:S(2)}) copy-start(f32[3,256,256]{2,1,0:T(8,128)} %bias.1) | copy-start | bytes 2359300
  9.8 0.9 %copy-start.4 = (f32[256,256]{1,0:T(8,128)S(1)}, f32[256,256]{1,0:T(8,128)}, u32[]{:S(2)}) copy-start(f32[256,256]{1,0:T(8,128)} %start.1) | copy-start | bytes 786436
  10.7 7.1 %copy-start.1 = (bf16[1,8,4,128,128]{4,3,2,1,0:T(8,128)(2,1)S(1)}, bf16[1,8,4,128,128]{4,3,2,1,0:T(8,128)(2,1)}, u32[]{:S(2)}) copy-start(bf16[1,8,4,128,128]{4,3,2,1,0:T(8,128)(2,1)} %param.10) | copy-start | bytes 3145732
  10.7 7.1 %copy-start.3 = (bf16[1,1024,256]{2,1,0:T(8,128)(2,1)S(1)}, bf16[1,1024,256]{2,1,0:T(8,128)(2,1)}, u32[]{:S(2)}) copy-start(bf16[1,1024,256]{2,1,0:T(8,128)(2,1)} %param.8) | copy-start | bytes 1572868
  10.7 7.1 %copy-start.6 = (s32[1,2,1024]{2,1,0:T(2,128)S(1)}, s32[1,2,1024]{2,1,0:T(2,128)}, u32[]{:S(2)}) copy-start(s32[1,2,1024]{2,1,0:T(2,128)} %param.12) | copy-start | bytes 24580
  23.4 5.6 %collective-permute-start.3 = (bf16[272,128]{1,0:T(8,128)(2,1)S(1)}, bf16[272,128]{1,0:T(8,128)(2,1)S(1)}, u32[]{:S(2)}, u32[]{:S(2)}) collective-permute-start(bf16[272,128]{1,0:T(8,128)(2,1)S(1)} %get-tuple-element.24), channel_id=1, source_target_pairs={{0,2},{1,3},{2,0},{3,1},{4,6},{5,7},{6,4},{7,5},{8,10},{9,11},{10,... | collective-permute-start | bytes 208904 | tf_op jit(solution)/shard_map/ppermute | solution.py:242
  26.7 4.7 %collective-permute-start.4 = (bf16[272,128]{1,0:T(8,128)(2,1)S(1)}, bf16[272,128]{1,0:T(8,128)(2,1)S(1)}, u32[]{:S(2)}, u32[]{:S(2)}) collective-permute-start(bf16[272,128]{1,0:T(8,128)(2,1)S(1)} %get-tuple-element.25), channel_id=1, source_target_pairs={{0,3},{1,0},{2,1},{3,2},{4,7},{5,4},{6,5},{7,6},{8,11},{9,8},{10,9... | collective-permute-start | bytes 208904 | tf_op jit(solution)/shard_map/ppermute | solution.py:242
  28.5 4.4 %collective-permute-start.2 = (bf16[272,128]{1,0:T(8,128)(2,1)S(1)}, bf16[272,128]{1,0:T(8,128)(2,1)S(1)}, u32[]{:S(2)}, u32[]{:S(2)}) collective-permute-start(bf16[272,128]{1,0:T(8,128)(2,1)S(1)} %get-tuple-element.23.own), channel_id=1, source_target_pairs={{0,1},{1,2},{2,3},{3,0},{4,5},{5,6},{6,7},{7,4},{8,9},{9,10},{10,1... | collective-permute-start | bytes 208904 | tf_op jit(solution)/shard_map/ppermute | solution.py:242
  33.0 5.9 %collective-permute-start.6 = (bf16[272,128]{1,0:T(8,128)(2,1)S(1)}, bf16[272,128]{1,0:T(8,128)(2,1)S(1)}, u32[]{:S(2)}, u32[]{:S(2)}) collective-permute-start(bf16[272,128]{1,0:T(8,128)(2,1)S(1)} %get-tuple-element.27), channel_id=1, source_target_pairs={{0,8},{1,9},{2,10},{3,11},{4,12},{5,13},{6,14},{7,15},{8,0},{9,1},... | collective-permute-start | bytes 208904 | tf_op jit(solution)/shard_map/ppermute | solution.py:242
  37.2 3.5 %collective-permute-start.7 = (bf16[272,128]{1,0:T(8,128)(2,1)S(1)}, bf16[272,128]{1,0:T(8,128)(2,1)S(1)}, u32[]{:S(2)}, u32[]{:S(2)}) collective-permute-start(bf16[272,128]{1,0:T(8,128)(2,1)S(1)} %get-tuple-element.28), channel_id=1, source_target_pairs={{0,12},{1,13},{2,14},{3,15},{4,0},{5,1},{6,2},{7,3},{8,4},{9,5},{1... | collective-permute-start | bytes 208904 | tf_op jit(solution)/shard_map/ppermute | solution.py:242
  37.7 5.1 %collective-permute-start.5 = (bf16[272,128]{1,0:T(8,128)(2,1)S(1)}, bf16[272,128]{1,0:T(8,128)(2,1)S(1)}, u32[]{:S(2)}, u32[]{:S(2)}) collective-permute-start(bf16[272,128]{1,0:T(8,128)(2,1)S(1)} %get-tuple-element.26.own), channel_id=1, source_target_pairs={{0,4},{1,5},{2,6},{3,7},{4,8},{5,9},{6,10},{7,11},{8,12},{9,13},{1... | collective-permute-start | bytes 208904 | tf_op jit(solution)/shard_map/ppermute | solution.py:242
  42.9 4.7 %collective-permute-start.9 = (bf16[272,128]{1,0:T(8,128)(2,1)S(1)}, bf16[272,128]{1,0:T(8,128)(2,1)S(1)}, u32[]{:S(2)}, u32[]{:S(2)}) collective-permute-start(bf16[272,128]{1,0:T(8,128)(2,1)S(1)} %get-tuple-element.30), channel_id=1, source_target_pairs={{0,64},{16,80},{32,96},{48,112},{64,0},{80,16},{96,32},{112,48},{1... | collective-permute-start | bytes 208904 | tf_op jit(solution)/shard_map/ppermute | solution.py:242
  45.7 3.2 %collective-permute-start.10 = (bf16[272,128]{1,0:T(8,128)(2,1)S(1)}, bf16[272,128]{1,0:T(8,128)(2,1)S(1)}, u32[]{:S(2)}, u32[]{:S(2)}) collective-permute-start(bf16[272,128]{1,0:T(8,128)(2,1)S(1)} %get-tuple-element.31), channel_id=1, source_target_pairs={{0,96},{16,112},{32,0},{48,16},{64,32},{80,48},{96,64},{112,80},{1... | collective-permute-start | bytes 208904 | tf_op jit(solution)/shard_map/ppermute | solution.py:242
  46.5 4.4 %collective-permute-start.8 = (bf16[272,128]{1,0:T(8,128)(2,1)S(1)}, bf16[272,128]{1,0:T(8,128)(2,1)S(1)}, u32[]{:S(2)}, u32[]{:S(2)}) collective-permute-start(bf16[272,128]{1,0:T(8,128)(2,1)S(1)} %get-tuple-element.29), channel_id=1, source_target_pairs={{0,32},{16,48},{32,64},{48,80},{64,96},{80,112},{96,0},{112,16},{1... | collective-permute-start | bytes 208904 | tf_op jit(solution)/shard_map/ppermute | solution.py:242
  51.0 6.9 %collective-permute-start.11 = (bf16[4,272,128]{2,1,0:T(8,128)(2,1)S(1)}, bf16[4,272,128]{2,1,0:T(8,128)(2,1)S(1)}, u32[]{:S(2)}, u32[]{:S(2)}) collective-permute-start(bf16[4,272,128]{2,1,0:T(8,128)(2,1)S(1)} %pad_maximum_fusion.along), channel_id=1, source_target_pairs={{0,16},{16,0},{32,48},{48,32},{64,80},{80,64},{96,112},{112,96},{1... | collective-permute-start | bytes 835592 | tf_op jit(solution)/shard_map/ppermute | solution.py:321

commit v2 on v1

v2 whole, which is shorter than its diff:
```python
import functools

import jax
import jax.numpy as jnp
from jax import lax
from jax.experimental import pallas as pl
from jax.experimental.pallas import tpu as pltpu
from jax.sharding import PartitionSpec as P

HALO = 1024
RING = 4
PACK_EXTRA = 16
F32 = jnp.float32
BF16 = jnp.bfloat16
INNER = (((1,), (0,)), ((), ()))
LANES = (((1,), (1,)), ((), ()))
ROWS = (((0,), (0,)), ((), ()))


def split(value):
    high = value.astype(BF16)
    return high, (value - high.astype(F32)).astype(BF16)


def dot(left, right, dims=INNER):
    return lax.dot_general(left, right, dims, preferred_element_type=F32)


def dot3(left, right, dims=INNER):
    return (
        dot(left[0], right[0], dims) + dot(left[0], right[1], dims) + dot(left[1], right[0], dims)
    )


def sigmoid(value):
    return 0.5 * jnp.tanh(0.5 * value) + 0.5


def forward_kernel(
    start_hbm,
    mats_hbm,
    bias_hbm,
    keep,
    gate_slope,
    proposal_slope,
    reset_slope,
    reset,
    low,
    weights_wide,
    reset_wide,
    turned_high,
    turned_low,
    score_matrix,
    start,
    mats,
    bias,
    mats_high,
    mats_low,
    sems,
):
    steps, width = low.shape[0], low.shape[1]
    copies = [pltpu.make_async_copy(start_hbm, start, sems.at[0])]
    copies += [
        pltpu.make_async_copy(mats_hbm.at[k], mats.at[k], sems.at[1 + k]) for k in range(4)
    ]
    copies += [
        pltpu.make_async_copy(bias_hbm.at[k], bias.at[k], sems.at[5 + k]) for k in range(3)
    ]
    for copy in copies:
        copy.start()
    for copy in copies[:5]:
        copy.wait()
    for k in range(4):
        mats_high[k], mats_low[k] = split(mats[k])
    for copy in copies[5:]:
        copy.wait()

    def gate(k, parts):
        return dot3((mats_high[k], mats_low[k]), parts)

    weight = start[...]
    for t in range(steps):
        parts = split(weight)
        r = sigmoid(gate(1, parts) + bias[1])
        mixed = r * weight
        mixed_parts = split(mixed)
        u_in = gate(0, parts)
        c_in = gate(2, parts)
        u = sigmoid(u_in + bias[0])
        c = jnp.tanh(c_in + gate(3, mixed_parts) + bias[2])
        rest = 1.0 - u
        keep[t] = rest
        reset[t] = r
        gate_slope[t] = (c - weight) * (u * rest)
        proposal_slope[t] = u * (1.0 - c * c)
        reset_slope[t] = mixed * (1.0 - r)
        lanes = pl.ds(t * width, width)
        weights_wide[:, lanes] = parts[0]
        reset_wide[:, lanes] = mixed_parts[0]
        weight = rest * weight + u * c
        low[t] = weight.astype(BF16)
    for k in range(4):
        turned_high[k] = mats_high[k].T
        turned_low[k] = mats_low[k].T
    own = low[lax.axis_index("snap")]
    score_matrix[...] = dot(own, own, LANES).astype(BF16)


def edge_kernel(
    factor,
    ids,
    own,
    even_side,
    odd_side,
    tiles,
    pos,
    neg,
    score_matrix,
    *refs,
):
    *outs, extended, aggregated, picked = refs
    rows, width = own.shape
    side = tiles.shape[1]
    blocks = rows // side
    per_block = ids.shape[1]
    node, ends = lax.axis_index("node"), lax.axis_size("node") - 1
    odd = lax.rem(node, 2)
    inside = (node > 0) & (node < ends)
    far = jnp.where(inside, odd_side[...], jnp.zeros_like(odd_side))
    extended[pl.ds(2 * blocks * (1 - odd), blocks)] = even_side[...].reshape(blocks, side, width)
    extended[pl.ds(blocks, blocks)] = own[...].reshape(blocks, side, width)
    extended[pl.ds(2 * blocks * odd, blocks)] = far.reshape(blocks, side, width)
    for b in range(blocks):
        total = jnp.zeros((side, width), F32)
        for k in range(0, per_block, 2):
            tile = jnp.concatenate([tiles[b * per_block + k], tiles[b * per_block + k + 1]], axis=1)
            source = jnp.concatenate([extended[ids[b, k]], extended[ids[b, k + 1]]], axis=0)
            total = total + dot(tile, source)
        aggregated[pl.ds(b * side, side), :] = total.astype(BF16)

    edges = pos.shape[1]
    chunk = 512
    lane = lax.broadcasted_iota(jnp.int32, (chunk, side), 1)
    for c in range(4 * edges // chunk):
        end, offset = divmod(c * chunk, edges)
        source = (pos, neg)[end // 2]
        turned = [
            jnp.broadcast_to(
                source[pl.ds(end % 2, 1), pl.ds(offset + part * side, side)], (side, side)
            ).T
            for part in range(chunk // side)
        ]
        index = jnp.concatenate(turned, axis=0)
        onehot = jnp.concatenate(
            [(index == lane + part * side).astype(F32).astype(BF16) for part in range(rows // side)],
            axis=1,
        )
        picked[pl.ds(c * chunk, chunk), :] = dot(onehot, aggregated[...]).astype(BF16)

    half = jnp.zeros((width, width), F32)
    for sign in (0, 1):
        first = picked[pl.ds(2 * sign * edges, edges), :]
        second = picked[pl.ds((2 * sign + 1) * edges, edges), :]
        score = jnp.sum(dot(first, score_matrix[...]) * second.astype(F32), axis=1, keepdims=True)
        score = score * (1.0 / width)
        if sign == 0:
            slope = sigmoid(-score) * (-factor)
        else:
            slope = sigmoid(score) * factor
        scaled = split(slope * first.astype(F32))
        half = half + dot(scaled[0], second, ROWS) + dot(scaled[1], second, ROWS)
    full = half + half.T
    quarter = width // 2
    upper = full[:quarter, :quarter]
    lower = full[quarter:, quarter:]
    i = lax.broadcasted_iota(jnp.int32, (quarter, quarter), 0)
    j = lax.broadcasted_iota(jnp.int32, (quarter, quarter), 1)
    diagonal = jnp.sum(jnp.where(i == j, lower, 0.0), axis=0, keepdims=True)
    corner = full[:quarter, quarter:].astype(BF16)
    mixed = jnp.where(i <= j, upper, lower).astype(BF16)
    extra = jnp.broadcast_to(diagonal, (PACK_EXTRA, quarter)).astype(BF16)
    for packed in outs:
        packed[pl.ds(0, quarter), :] = corner
        packed[pl.ds(quarter, quarter), :] = mixed
        packed[pl.ds(2 * quarter, PACK_EXTRA), :] = extra


def backward_kernel(
    along,
    other,
    keep,
    gate_slope,
    proposal_slope,
    reset_slope,
    reset,
    low,
    weights_wide,
    reset_wide,
    turned_high,
    turned_low,
    adjoint_rows,
    grads,
    initial_grad,
    adjoints,
    local,
):
    steps, width = low.shape[0], low.shape[1]
    quarter = width // 2
    place, node = lax.axis_index("snap"), lax.axis_index("node")
    x, core = lax.div(place, 2), lax.rem(place, 2)
    i = lax.broadcasted_iota(jnp.int32, (quarter, quarter), 0)
    j = lax.broadcasted_iota(jnp.int32, (quarter, quarter), 1)

    for t in range(steps):
        turn = lax.rem(x - t // 2 + RING, RING)
        piece = jnp.where(core == t % 2, along[turn], other[turn])
        corner = piece[:quarter]
        mixed = piece[quarter : 2 * quarter].astype(F32)
        diagonal = piece[2 * quarter :].astype(F32)[0:1]
        turned = mixed.T
        upper = jnp.where(i <= j, mixed, turned).astype(BF16)
        lower = jnp.where(i > j, mixed, jnp.where(i < j, turned, diagonal)).astype(BF16)
        whole = jnp.concatenate(
            [
                jnp.concatenate([upper, corner], axis=1),
                jnp.concatenate([corner.T, lower], axis=1),
            ],
            axis=0,
        )
        local[t] = dot(whole, low[t])

    def gate(k, parts):
        return dot3((turned_high[k], turned_low[k]), parts)

    grads[...] = jnp.zeros_like(grads)

    def step(s, carry):
        t = steps - 1 - s
        g = local[t] + carry
        adjoints[t] = g
        d2 = g * proposal_slope[t]
        d2_parts = split(d2)
        mixed = gate(3, d2_parts)
        d0 = g * gate_slope[t]
        d0_parts = split(d0)
        fresh = g * keep[t] + (gate(0, d0_parts) + gate(2, d2_parts))
        d1 = mixed * reset_slope[t]
        d1_parts = split(d1)
        fresh = fresh + mixed * reset[t] + gate(1, d1_parts)
        lanes = pl.ds(pl.multiple_of(t * width, width), width)
        before = weights_wide[:, lanes]
        grads[0] += dot(d0_parts[0], before, LANES)
        grads[1] += dot(d1_parts[0], before, LANES)
        grads[2] += dot(d2_parts[0], before, LANES)
        grads[3] += dot(d2_parts[0], reset_wide[:, lanes], LANES)
        grads[4] += d0
        grads[5] += d1
        grads[6] += d2
        return fresh

    initial_grad[...] = lax.fori_loop(0, steps, step, jnp.zeros((width, width), F32))
    share = adjoint_rows.shape[0]
    start = pl.multiple_of(node * share, share)
    adjoint_rows[...] = adjoints[place, pl.ds(start, share), :]


def params(megabytes):
    return pltpu.CompilerParams(vmem_limit_bytes=megabytes * 2**20)


VMEM = pl.BlockSpec(memory_space=pltpu.VMEM)
SMEM = pl.BlockSpec(memory_space=pltpu.SMEM)
HBM = pl.BlockSpec(memory_space=pltpu.HBM)


def ring_parts(copies, axis, stride, count):
    size = lax.axis_size(axis)
    span = stride * count
    parts = []
    for turn in sorted(range(1, count), key=lambda k: -min(k, count - k)):
        route = [(i, i - i % span + (i % span + turn * stride) % span) for i in range(size)]
        parts.append(lax.ppermute(copies[turn], axis, route))
    return parts


def sum_kernel(own, first, second, third, *copies):
    total = (own[...].astype(F32) + first[...].astype(F32)) + (
        second[...].astype(F32) + third[...].astype(F32)
    )
    total = total.astype(BF16)
    for copy in copies:
        copy[...] = total


def ring_sum(copies, axis, stride, count):
    parts = ring_parts(copies, axis, stride, count)
    like = jax.ShapeDtypeStruct(copies[0].shape, BF16)
    return pl.pallas_call(
        sum_kernel,
        out_shape=[like] * RING,
        in_specs=[VMEM] * RING,
        out_specs=[VMEM] * RING,
        compiler_params=params(4),
        name="ring_sum",
    )(copies[0], *parts)


def body(
    features, tile_ids, tile_values, pos_edges, neg_edges, initial_weight, gate_mats, gate_bias
):
    snap_count = lax.axis_size("snap")
    node_count = lax.axis_size("node")
    own = features[0]
    rows, width = own.shape
    side = tile_values.shape[-1]
    square = (snap_count, width, width)

    even_pairs = [(i, i ^ 1) for i in range(node_count)]
    odd_pairs = [(i, (i - 1 + 2 * (i % 2)) % node_count) for i in range(node_count)]
    even_side = lax.ppermute(own, "node", even_pairs)
    odd_side = lax.ppermute(own, "node", odd_pairs)

    wide = jax.ShapeDtypeStruct(square, F32)
    thin = jax.ShapeDtypeStruct(square, BF16)
    long = jax.ShapeDtypeStruct((width, snap_count * width), BF16)
    mats = jax.ShapeDtypeStruct((4, width, width), BF16)
    *states, score_matrix = pl.pallas_call(
        forward_kernel,
        out_shape=[wide] * 5
        + [thin, long, long, mats, mats, jax.ShapeDtypeStruct((width, width), BF16)],
        in_specs=[HBM] * 3,
        out_specs=[VMEM] * 11,
        scratch_shapes=[
            pltpu.VMEM((width, width), F32),
            pltpu.VMEM((4, width, width), F32),
            pltpu.VMEM((3, width, width), F32),
            pltpu.VMEM((4, width, width), BF16),
            pltpu.VMEM((4, width, width), BF16),
            pltpu.SemaphoreType.DMA((8,)),
        ],
        compiler_params=params(16),
        name="forward_chain",
    )(
        *(
            pltpu.with_memory_space_constraint(array, pltpu.HBM)
            for array in (initial_weight, gate_mats, gate_bias)
        )
    )

    factor = float(rows * node_count) ** (-0.5)
    pack_rows = width + PACK_EXTRA
    copies = pl.pallas_call(
        functools.partial(edge_kernel, factor),
        out_shape=[jax.ShapeDtypeStruct((pack_rows, width // 2), BF16)] * RING,
        in_specs=[SMEM] + [VMEM] * 7,
        out_specs=[VMEM] * RING,
        scratch_shapes=[
            pltpu.VMEM(((rows + 2 * HALO) // side, side, width), BF16),
            pltpu.VMEM((rows, width), BF16),
            pltpu.VMEM((4 * pos_edges.shape[-1], width), BF16),
        ],
        compiler_params=params(16),
        name="edge_products",
    )(
        tile_ids[0],
        own,
        even_side,
        odd_side,
        tile_values.reshape(-1, side, side),
        pos_edges[0],
        neg_edges[0],
        score_matrix,
    )

    copies = ring_sum(copies, "node", 1, RING)
    copies = ring_sum(copies, "node", RING, node_count // RING)
    far, near, back = ring_parts(copies, "snap", 2, snap_count // 2)
    along = jnp.stack([copies[0], near, far, back])
    other = lax.ppermute(along, "snap", [(i, i ^ 1) for i in range(snap_count)])

    share = width // node_count
    adjoint_rows, grads, initial_grad = pl.pallas_call(
        backward_kernel,
        out_shape=[
            jax.ShapeDtypeStruct((share, width), F32),
            jax.ShapeDtypeStruct((7, width, width), F32),
            jax.ShapeDtypeStruct((width, width), F32),
        ],
        in_specs=[VMEM] * 12,
        out_specs=[VMEM] * 3,
        scratch_shapes=[pltpu.VMEM(square, F32)] * 2,
        compiler_params=params(16),
        name="backward_chain",
    )(along, other, *states)
    return adjoint_rows[None], grads, initial_grad


def solution(mesh):
    placed = (
        P("snap", "node", None),
        P("snap", "node", None),
        P("snap", "node", None, None, None),
        P("snap", None, "node"),
        P("snap", None, "node"),
        P(),
        P(),
        P(),
    )
    return jax.shard_map(
        body,
        mesh=mesh,
        in_specs=placed,
        out_specs=(P("snap", "node", None), P(), P()),
        check_vma=False,
    )
```

time: 67.1 us -> 61.2 us (0.912)
  local copies, waits for them, and re-layouts: 4.08 us -> 0.77 us
  starting transfers between devices: 27.3 us -> 25.4 us
  waiting for transfers between devices: 13 us -> 12.1 us
    unnamed x14 -> x8, local copies, waits for them, and re-layouts: 3.32 us -> 0.02 us
    ppermute x11, starting transfers between devices: 21.6 us -> 19.3 us  [the longest x9 12.1 us: ring_parts(): parts.append(lax.ppermute(copies[turn], axis, route))]
    ppermute x11, waiting for transfers between devices: 11.8 us -> 10.9 us  [the longest x9 6.87 us: ring_parts(): parts.append(lax.ppermute(copies[turn], axis, route))]
    pallas_call x3, Pallas kernels: 7.12 us -> 7.97 us  [the longest x1 7.89 us: body(): pl.pallas_call(forward_kernel, out_shape=[wide] * 5 + [thin, long, long,...]
  transfers between devices with their start and end apart: 12 -> 12, of which waited for: 9 -> 10; matrix products, arithmetic and copies ran while one was open for 1% -> 1% of each run, Pallas kernels for 11% -> 13%
where the time goes in v2:
time: 61.2 us; the launch traced here: 61.1 us
  starting transfers between devices  25.4 us (42%)
  Pallas kernels  22 us (36%)
  waiting for transfers between devices  12.1 us (20%)
  local copies, waits for them, and re-layouts  0.77 us (1%)
  between operations  0.72 us (1%)
    ppermute x9, starting transfers between devices, ring_parts(): parts.append(lax.ppermute(copies[turn], axis, route))  12.1 us
    pallas_call x1, Pallas kernels, body(): pl.pallas_call(backward_kernel, out_shape=[jax.ShapeDtypeStruct((share, w...  8.6 us
    pallas_call x1, Pallas kernels, body(): pl.pallas_call(forward_kernel, out_shape=[wide] * 5 + [thin, long, long,...  7.89 us
    ppermute x1, starting transfers between devices, body(): odd_side = lax.ppermute(own, 'node', odd_pairs)  7.12 us
    ppermute x9, waiting for transfers between devices, ring_parts(): parts.append(lax.ppermute(copies[turn], axis, route))  6.87 us
    ppermute x1, starting transfers between devices, body(): other = lax.ppermute(along, 'snap', [(i, i ^ 1) for i in range(snap_count)])  6.19 us
    pallas_call x1, Pallas kernels, body(): pl.pallas_call(functools.partial(edge_kernel, factor), out_shape=[jax.Sha...  5.45 us
    ppermute x1, waiting for transfers between devices, body(): odd_side = lax.ppermute(own, 'node', odd_pairs)  3.21 us
  transfers between devices with their start and end apart: 12, of which 10 were waited for; matrix products, arithmetic and copies ran while one was open for 1% of the time, Pallas kernels for 13%

profile of v2, /device:TPU:1, one launch (start us, length us, event | category | flops | bytes accessed | tf_op | source)
XLA Modules:
  0.0 61.1 jit_solution(16955583711236390731)
XLA Ops:
  0.6 0.0 copy-start.1
  0.6 0.0 copy-start.3
  0.7 0.0 copy-start.2
  0.7 0.0 copy-start
  0.7 7.1 %collective-permute-start.1 = (bf16[1024,256]{1,0:T(8,128)(2,1)}, bf16[1024,256]{1,0:T(8,128)(2,1)S(1)}, u32[]{:S(2)}, u32[]{:S(2)}) collective-permute-start(bf16[1024,256]{1,0:T(8,128)(2,1)} %bitcast.11), channel_id=1, source_target_pairs={{0,15},{1,2},{2,1},{3,4},{4,3},{5,6},{6,5},{7,8},{8,7},{9,10},{10,... | collective-permute-start | bytes 1572872 | tf_op jit(solution)/shard_map/ppermute | solution.py:321
  7.8 0.0 collective-permute-start
  7.8 0.8 %copy.11.ids = s32[8,4]{1,0:T(8,128)S(1)} copy(s32[8,4]{0,1:T(4,128)} %bitcast.20) | data formatting | bytes 256 | tf_op jit(solution)/shard_map/squeeze | solution.py:365
  8.5 7.9 %forward_chain.1 = (f32[8,256,256]{2,1,0:T(8,128)S(1)}, f32[8,256,256]{2,1,0:T(8,128)S(1)}, f32[8,256,256]{2,1,0:T(8,128)S(1)}, f32[8,256,256]{2,1,0:T(8,128)S(1...) custom-call(f32[256,256]{1,0:T(8,128)} %start_hbm.1, ...), custom_call_target="tpu_custom_call" | custom-call | tf_op jit(solution)/shard_map/forward_chain/pallas_call | solution.py:327
  16.4 3.2 %collective-permute-done.1.odd_side = bf16[1024,256]{1,0:T(8,128)(2,1)S(1)} collective-permute-done((bf16[1024,256]{1,0:T(8,128)(2,1)}, bf16[1024,256]{1,0:T(8,128)(2,1)S(1)}, u32[]{:S(2)}, u32[]{:S(2)}) %collective-permute-start.1) | collective-permute-done | bytes 524320 | tf_op jit(solution)/shard_map/ppermute | solution.py:321
  19.6 0.8 %collective-permute-done.even_side = bf16[1024,256]{1,0:T(8,128)(2,1)S(1)} collective-permute-done((bf16[1024,256]{1,0:T(8,128)(2,1)}, bf16[1024,256]{1,0:T(8,128)(2,1)S(1)}, u32[]{:S(2)}, u32[]{:S(2)}) %collective-permute-start) | collective-permute-done | bytes 524320 | tf_op jit(solution)/shard_map/ppermute | solution.py:320
  20.5 0.0 copy-done.1
  20.5 0.0 copy-done.3
  20.5 0.0 copy-done.2
  20.5 0.0 copy-done
  20.5 5.5 %edge_products.1 = (bf16[272,128]{1,0:T(8,128)(2,1)S(1)}, bf16[272,128]{1,0:T(8,128)(2,1)S(1)}, bf16[272,128]{1,0:T(8,128)(2,1)S(1)}, bf16[272,128]{1,0:T(8,128)(2,1)S(1)}) custom-call(s32[8,4]{1,0:T(8,128)S(1)} %copy.11.ids, bf16[1024,256]{1,0:T(8,128)(2,1)S(1)} %bitcast.13, bf16[1024,256]{1,0:T(8,128)(2,1)S(1)} %collective-permute-done.even_side, ...), custom_call_target="tpu_custom_call" | custom-call | tf_op jit(solution)/shard_map/edge_products/pallas_call | solution.py:352
  25.9 0.1 collective-permute-start.2
  26.0 0.4 collective-permute-start.3
  26.5 2.3 %collective-permute-start.4 = (bf16[272,128]{1,0:T(8,128)(2,1)S(1)}, bf16[272,128]{1,0:T(8,128)(2,1)S(1)}, u32[]{:S(2)}, u32[]{:S(2)}) collective-permute-start(bf16[272,128]{1,0:T(8,128)(2,1)S(1)} %get-tuple-element.33), channel_id=1, source_target_pairs={{0,3},{1,0},{2,1},{3,2},{4,7},{5,4},{6,5},{7,6},{8,11},{9,8},{10,9... | collective-permute-start | bytes 208904 | tf_op jit(solution)/shard_map/ppermute | solution.py:282
  28.8 2.0 %collective-permute-done.2.first = bf16[272,128]{1,0:T(8,128)(2,1)S(1)} collective-permute-done((bf16[272,128]{1,0:T(8,128)(2,1)S(1)}, bf16[272,128]{1,0:T(8,128)(2,1)S(1)}, u32[]{:S(2)}, u32[]{:S(2)}) %collective-permute-start.2) | collective-permute-done | bytes 69664 | tf_op jit(solution)/shard_map/ppermute | solution.py:282
  30.8 0.4 collective-permute-done.3.second
  31.2 0.0 collective-permute-done.4.third
  31.3 1.7 %collective-permute-start.5 = (bf16[272,128]{1,0:T(8,128)(2,1)S(1)}, bf16[272,128]{1,0:T(8,128)(2,1)S(1)}, u32[]{:S(2)}, u32[]{:S(2)}) collective-permute-start(bf16[272,128]{1,0:T(8,128)(2,1)S(1)} %get-tuple-element.35), channel_id=1, source_target_pairs={{0,8},{1,9},{2,10},{3,11},{4,12},{5,13},{6,14},{7,15},{8,0},{9,1},... | collective-permute-start | bytes 208904 | tf_op jit(solution)/shard_map/ppermute | solution.py:282
  33.0 1.9 %collective-permute-start.6 = (bf16[272,128]{1,0:T(8,128)(2,1)S(1)}, bf16[272,128]{1,0:T(8,128)(2,1)S(1)}, u32[]{:S(2)}, u32[]{:S(2)}) collective-permute-start(bf16[272,128]{1,0:T(8,128)(2,1)S(1)} %get-tuple-element.36), channel_id=1, source_target_pairs={{0,4},{1,5},{2,6},{3,7},{4,8},{5,9},{6,10},{7,11},{8,12},{9,13},{1... | collective-permute-start | bytes 208904 | tf_op jit(solution)/shard_map/ppermute | solution.py:282
  35.0 0.7 %collective-permute-start.7 = (bf16[272,128]{1,0:T(8,128)(2,1)S(1)}, bf16[272,128]{1,0:T(8,128)(2,1)S(1)}, u32[]{:S(2)}, u32[]{:S(2)}) collective-permute-start(bf16[272,128]{1,0:T(8,128)(2,1)S(1)} %get-tuple-element.37), channel_id=1, source_target_pairs={{0,12},{1,13},{2,14},{3,15},{4,0},{5,1},{6,2},{7,3},{8,4},{9,5},{1... | collective-permute-start | bytes 208904 | tf_op jit(solution)/shard_map/ppermute | solution.py:282
  35.7 0.3 collective-permute-done.5.first
  36.0 1.4 %collective-permute-done.6.second = bf16[272,128]{1,0:T(8,128)(2,1)S(1)} collective-permute-done((bf16[272,128]{1,0:T(8,128)(2,1)S(1)}, bf16[272,128]{1,0:T(8,128)(2,1)S(1)}, u32[]{:S(2)}, u32[]{:S(2)}) %collective-permute-start.6) | collective-permute-done | bytes 69664 | tf_op jit(solution)/shard_map/ppermute | solution.py:282
  37.4 0.7 %collective-permute-done.7.third = bf16[272,128]{1,0:T(8,128)(2,1)S(1)} collective-permute-done((bf16[272,128]{1,0:T(8,128)(2,1)S(1)}, bf16[272,128]{1,0:T(8,128)(2,1)S(1)}, u32[]{:S(2)}, u32[]{:S(2)}) %collective-permute-start.7) | collective-permute-done | bytes 69664 | tf_op jit(solution)/shard_map/ppermute | solution.py:282
  38.2 1.3 %collective-permute-start.8 = (bf16[272,128]{1,0:T(8,128)(2,1)S(1)}, bf16[272,128]{1,0:T(8,128)(2,1)S(1)}, u32[]{:S(2)}, u32[]{:S(2)}) collective-permute-start(bf16[272,128]{1,0:T(8,128)(2,1)S(1)} %get-tuple-element.39), channel_id=1, source_target_pairs={{0,32},{16,48},{32,64},{48,80},{64,96},{80,112},{96,0},{112,16},{1... | collective-permute-start | bytes 208904 | tf_op jit(solution)/shard_map/ppermute | solution.py:282
  39.5 2.4 %collective-permute-start.9 = (bf16[272,128]{1,0:T(8,128)(2,1)S(1)}, bf16[272,128]{1,0:T(8,128)(2,1)S(1)}, u32[]{:S(2)}, u32[]{:S(2)}) collective-permute-start(bf16[272,128]{1,0:T(8,128)(2,1)S(1)} %get-tuple-element.40), channel_id=1, source_target_pairs={{0,64},{16,80},{32,96},{48,112},{64,0},{80,16},{96,32},{112,48},{1... | collective-permute-start | bytes 208904 | tf_op jit(solution)/shard_map/ppermute | solution.py:282
  41.9 1.2 %collective-permute-start.10 = (bf16[272,128]{1,0:T(8,128)(2,1)S(1)}, bf16[272,128]{1,0:T(8,128)(2,1)S(1)}, u32[]{:S(2)}, u32[]{:S(2)}) collective-permute-start(bf16[272,128]{1,0:T(8,128)(2,1)S(1)} %get-tuple-element.41), channel_id=1, source_target_pairs={{0,96},{16,112},{32,0},{48,16},{64,32},{80,48},{96,64},{112,80},{1... | collective-permute-start | bytes 208904 | tf_op jit(solution)/shard_map/ppermute | solution.py:282
  43.1 0.0 collective-permute-done.8
  43.1 1.3 %collective-permute-done.9 = bf16[272,128]{1,0:T(8,128)(2,1)S(1)} collective-permute-done((bf16[272,128]{1,0:T(8,128)(2,1)S(1)}, bf16[272,128]{1,0:T(8,128)(2,1)S(1)}, u32[]{:S(2)}, u32[]{:S(2)}) %collective-permute-start.9) | collective-permute-done | bytes 69664 | tf_op jit(solution)/shard_map/ppermute | solution.py:282
  44.3 0.7 %collective-permute-done.10 = bf16[272,128]{1,0:T(8,128)(2,1)S(1)} collective-permute-done((bf16[272,128]{1,0:T(8,128)(2,1)S(1)}, bf16[272,128]{1,0:T(8,128)(2,1)S(1)}, u32[]{:S(2)}, u32[]{:S(2)}) %collective-permute-start.10) | collective-permute-done | bytes 69664 | tf_op jit(solution)/shard_map/ppermute | solution.py:282
  45.1 6.2 %collective-permute-start.11 = (bf16[4,272,128]{2,1,0:T(8,128)(2,1)S(1)}, bf16[4,272,128]{2,1,0:T(8,128)(2,1)S(1)}, u32[]{:S(2)}, u32[]{:S(2)}) collective-permute-start(bf16[4,272,128]{2,1,0:T(8,128)(2,1)S(1)} %pad_maximum_fusion.along), channel_id=1, source_target_pairs={{0,16},{16,0},{32,48},{48,32},{64,80},{80,64},{96,112},{112,96},{1... | collective-permute-start | bytes 835592 | tf_op jit(solution)/shard_map/ppermute | solution.py:379
  51.3 1.2 %collective-permute-done.11.other = bf16[4,272,128]{2,1,0:T(8,128)(2,1)S(1)} collective-permute-done((bf16[4,272,128]{2,1,0:T(8,128)(2,1)S(1)}, bf16[4,272,128]{2,1,0:T(8,128)(2,1)S(1)}, u32[]{:S(2)}, u32[]{:S(2)}) %collective-permute-start.11) | collective-permute-done | bytes 278560 | tf_op jit(solution)/shard_map/ppermute | solution.py:379
  52.5 8.6 %backward_chain.1 = (f32[16,256]{1,0:T(8,128)}, f32[7,256,256]{2,1,0:T(8,128)}, f32[256,256]{1,0:T(8,128)}) custom-call(bf16[4,272,128]{2,1,0:T(8,128)(2,1)S(1)} %pad_maximum_fusion.along, bf16[4,272,128]{2,1,0:T(8,128)(2,1)S(1)} %collective-permute-done.11.other, f32[8,256,256]{2,1,0:T(8,128)S(1)} %get-tuple-element.42.keep, ...), custom_call_target="tpu_custom_call" | custom-call | tf_op jit(solution)/shard_map/backward_chain/pallas_call | solution.py:382
  (3 shorter events, 0.1 us)
Async XLA Ops:
  0.6 19.8 %copy-start.1 = (bf16[1,1024,256]{2,1,0:T(8,128)(2,1)S(1)}, bf16[1,1024,256]{2,1,0:T(8,128)(2,1)}, u32[]{:S(2)}) copy-start(bf16[1,1024,256]{2,1,0:T(8,128)(2,1)} %param.8) | copy-start | bytes 1572868
  0.6 19.8 %copy-start.3 = (s32[1,2,1024]{2,1,0:T(2,128)S(1)}, s32[1,2,1024]{2,1,0:T(2,128)}, u32[]{:S(2)}) copy-start(s32[1,2,1024]{2,1,0:T(2,128)} %param.12) | copy-start | bytes 24580
  0.7 19.8 %copy-start.2 = (s32[1,2,1024]{2,1,0:T(2,128)S(1)}, s32[1,2,1024]{2,1,0:T(2,128)}, u32[]{:S(2)}) copy-start(s32[1,2,1024]{2,1,0:T(2,128)} %param.11) | copy-start | bytes 24580
  0.7 19.8 %copy-start = (bf16[1,8,4,128,128]{4,3,2,1,0:T(8,128)(2,1)S(1)}, bf16[1,8,4,128,128]{4,3,2,1,0:T(8,128)(2,1)}, u32[]{:S(2)}) copy-start(bf16[1,8,4,128,128]{4,3,2,1,0:T(8,128)(2,1)} %param.10) | copy-start | bytes 3145732
  0.7 19.0 %collective-permute-start.1 = (bf16[1024,256]{1,0:T(8,128)(2,1)}, bf16[1024,256]{1,0:T(8,128)(2,1)S(1)}, u32[]{:S(2)}, u32[]{:S(2)}) collective-permute-start(bf16[1024,256]{1,0:T(8,128)(2,1)} %bitcast.11), channel_id=1, source_target_pairs={{0,15},{1,2},{2,1},{3,4},{4,3},{5,6},{6,5},{7,8},{8,7},{9,10},{10,... | collective-permute-start | bytes 1572872 | tf_op jit(solution)/shard_map/ppermute | solution.py:321
  7.8 12.7 %collective-permute-start = (bf16[1024,256]{1,0:T(8,128)(2,1)}, bf16[1024,256]{1,0:T(8,128)(2,1)S(1)}, u32[]{:S(2)}, u32[]{:S(2)}) collective-permute-start(bf16[1024,256]{1,0:T(8,128)(2,1)} %bitcast.12), channel_id=1, source_target_pairs={{0,1},{1,0},{2,3},{3,2},{4,5},{5,4},{6,7},{7,6},{8,9},{9,8},{10,11... | collective-permute-start | bytes 1572872 | tf_op jit(solution)/shard_map/ppermute | solution.py:320
  25.9 4.9 %collective-permute-start.2 = (bf16[272,128]{1,0:T(8,128)(2,1)S(1)}, bf16[272,128]{1,0:T(8,128)(2,1)S(1)}, u32[]{:S(2)}, u32[]{:S(2)}) collective-permute-start(bf16[272,128]{1,0:T(8,128)(2,1)S(1)} %get-tuple-element.31), channel_id=1, source_target_pairs={{0,2},{1,3},{2,0},{3,1},{4,6},{5,7},{6,4},{7,5},{8,10},{9,11},{10,... | collective-permute-start | bytes 208904 | tf_op jit(solution)/shard_map/ppermute | solution.py:282
  26.0 5.2 %collective-permute-start.3 = (bf16[272,128]{1,0:T(8,128)(2,1)S(1)}, bf16[272,128]{1,0:T(8,128)(2,1)S(1)}, u32[]{:S(2)}, u32[]{:S(2)}) collective-permute-start(bf16[272,128]{1,0:T(8,128)(2,1)S(1)} %get-tuple-element.32), channel_id=1, source_target_pairs={{0,1},{1,2},{2,3},{3,0},{4,5},{5,6},{6,7},{7,4},{8,9},{9,10},{10,1... | collective-permute-start | bytes 208904 | tf_op jit(solution)/shard_map/ppermute | solution.py:282
  26.5 4.8 %collective-permute-start.4 = (bf16[272,128]{1,0:T(8,128)(2,1)S(1)}, bf16[272,128]{1,0:T(8,128)(2,1)S(1)}, u32[]{:S(2)}, u32[]{:S(2)}) collective-permute-start(bf16[272,128]{1,0:T(8,128)(2,1)S(1)} %get-tuple-element.33), channel_id=1, source_target_pairs={{0,3},{1,0},{2,1},{3,2},{4,7},{5,4},{6,5},{7,6},{8,11},{9,8},{10,9... | collective-permute-start | bytes 208904 | tf_op jit(solution)/shard_map/ppermute | solution.py:282
  31.3 4.7 %collective-permute-start.5 = (bf16[272,128]{1,0:T(8,128)(2,1)S(1)}, bf16[272,128]{1,0:T(8,128)(2,1)S(1)}, u32[]{:S(2)}, u32[]{:S(2)}) collective-permute-start(bf16[272,128]{1,0:T(8,128)(2,1)S(1)} %get-tuple-element.35), channel_id=1, source_target_pairs={{0,8},{1,9},{2,10},{3,11},{4,12},{5,13},{6,14},{7,15},{8,0},{9,1},... | collective-permute-start | bytes 208904 | tf_op jit(solution)/shard_map/ppermute | solution.py:282
  33.0 4.4 %collective-permute-start.6 = (bf16[272,128]{1,0:T(8,128)(2,1)S(1)}, bf16[272,128]{1,0:T(8,128)(2,1)S(1)}, u32[]{:S(2)}, u32[]{:S(2)}) collective-permute-start(bf16[272,128]{1,0:T(8,128)(2,1)S(1)} %get-tuple-element.36), channel_id=1, source_target_pairs={{0,4},{1,5},{2,6},{3,7},{4,8},{5,9},{6,10},{7,11},{8,12},{9,13},{1... | collective-permute-start | bytes 208904 | tf_op jit(solution)/shard_map/ppermute | solution.py:282
  35.0 3.2 %collective-permute-start.7 = (bf16[272,128]{1,0:T(8,128)(2,1)S(1)}, bf16[272,128]{1,0:T(8,128)(2,1)S(1)}, u32[]{:S(2)}, u32[]{:S(2)}) collective-permute-start(bf16[272,128]{1,0:T(8,128)(2,1)S(1)} %get-tuple-element.37), channel_id=1, source_target_pairs={{0,12},{1,13},{2,14},{3,15},{4,0},{5,1},{6,2},{7,3},{8,4},{9,5},{1... | collective-permute-start | bytes 208904 | tf_op jit(solution)/shard_map/ppermute | solution.py:282
  38.2 4.9 %collective-permute-start.8 = (bf16[272,128]{1,0:T(8,128)(2,1)S(1)}, bf16[272,128]{1,0:T(8,128)(2,1)S(1)}, u32[]{:S(2)}, u32[]{:S(2)}) collective-permute-start(bf16[272,128]{1,0:T(8,128)(2,1)S(1)} %get-tuple-element.39), channel_id=1, source_target_pairs={{0,32},{16,48},{32,64},{48,80},{64,96},{80,112},{96,0},{112,16},{1... | collective-permute-start | bytes 208904 | tf_op jit(solution)/shard_map/ppermute | solution.py:282
  39.5 4.9 %collective-permute-start.9 = (bf16[272,128]{1,0:T(8,128)(2,1)S(1)}, bf16[272,128]{1,0:T(8,128)(2,1)S(1)}, u32[]{:S(2)}, u32[]{:S(2)}) collective-permute-start(bf16[272,128]{1,0:T(8,128)(2,1)S(1)} %get-tuple-element.40), channel_id=1, source_target_pairs={{0,64},{16,80},{32,96},{48,112},{64,0},{80,16},{96,32},{112,48},{1... | collective-permute-start | bytes 208904 | tf_op jit(solution)/shard_map/ppermute | solution.py:282
  41.9 3.2 %collective-permute-start.10 = (bf16[272,128]{1,0:T(8,128)(2,1)S(1)}, bf16[272,128]{1,0:T(8,128)(2,1)S(1)}, u32[]{:S(2)}, u32[]{:S(2)}) collective-permute-start(bf16[272,128]{1,0:T(8,128)(2,1)S(1)} %get-tuple-element.41), channel_id=1, source_target_pairs={{0,96},{16,112},{32,0},{48,16},{64,32},{80,48},{96,64},{112,80},{1... | collective-permute-start | bytes 208904 | tf_op jit(solution)/shard_map/ppermute | solution.py:282
  45.1 7.4 %collective-permute-start.11 = (bf16[4,272,128]{2,1,0:T(8,128)(2,1)S(1)}, bf16[4,272,128]{2,1,0:T(8,128)(2,1)S(1)}, u32[]{:S(2)}, u32[]{:S(2)}) collective-permute-start(bf16[4,272,128]{2,1,0:T(8,128)(2,1)S(1)} %pad_maximum_fusion.along), channel_id=1, source_target_pairs={{0,16},{16,0},{32,48},{48,32},{64,80},{80,64},{96,112},{112,96},{1... | collective-permute-start | bytes 835592 | tf_op jit(solution)/shard_map/ppermute | solution.py:379

commit v3 on v2

--- a/solution.py
+++ b/solution.py
@@ -36,29 +36,7 @@
     return 0.5 * jnp.tanh(0.5 * value) + 0.5
 
 
-def forward_kernel(
-    start_hbm,
-    mats_hbm,
-    bias_hbm,
-    keep,
-    gate_slope,
-    proposal_slope,
-    reset_slope,
-    reset,
-    low,
-    weights_wide,
-    reset_wide,
-    turned_high,
-    turned_low,
-    score_matrix,
-    start,
-    mats,
-    bias,
-    mats_high,
-    mats_low,
-    sems,
-):
-    steps, width = low.shape[0], low.shape[1]
+def load_gates(start_hbm, mats_hbm, bias_hbm, start, mats, bias, mats_high, mats_low, sems):
     copies = [pltpu.make_async_copy(start_hbm, start, sems.at[0])]
     copies += [
         pltpu.make_async_copy(mats_hbm.at[k], mats.at[k], sems.at[1 + k]) for k in range(4)
@@ -75,35 +53,87 @@
     for copy in copies[5:]:
         copy.wait()
 
+
+def gate_step(weight, bias, mats_high, mats_low):
     def gate(k, parts):
         return dot3((mats_high[k], mats_low[k]), parts)
 
+    parts = split(weight)
+    r = sigmoid(gate(1, parts) + bias[1])
+    mixed = r * weight
+    mixed_parts = split(mixed)
+    u_in = gate(0, parts)
+    c_in = gate(2, parts)
+    u = sigmoid(u_in + bias[0])
+    c = jnp.tanh(c_in + gate(3, mixed_parts) + bias[2])
+    return u, r, c, mixed, (1.0 - u) * weight + u * c
+
+
+def write_score_matrix(low, score_matrix):
+    own = low[lax.axis_index("snap")]
+    score_matrix[...] = dot(own, own, LANES).astype(BF16)
+
+
+def early_kernel(start_hbm, mats_hbm, bias_hbm, score_matrix, low, *scratch):
+    start, mats, bias, mats_high, mats_low, sems = scratch
+
+    @pl.when(lax.rem(lax.axis_index("snap"), 2) == 1)
+    def _():
+        load_gates(start_hbm, mats_hbm, bias_hbm, *scratch)
+        weight = start[...]
+        for t in range(low.shape[0]):
+            weight = gate_step(weight, bias, mats_high, mats_low)[-1]
+            low[t] = weight.astype(BF16)
+        write_score_matrix(low, score_matrix)
+
+
+def late_kernel(
+    start_hbm,
+    mats_hbm,
+    bias_hbm,
+    early_score_matrix,
+    keep,
+    gate_slope,
+    proposal_slope,
+    reset_slope,
+    reset,
+    low,
+    weights_wide,
+    reset_wide,
+    turned_high,
+    turned_low,
+    score_matrix,
+    *scratch,
+):
+    start, mats, bias, mats_high, mats_low, sems = scratch
+    steps, width = low.shape[0], low.shape[1]
+    odd = lax.rem(lax.axis_index("snap"), 2) == 1
+    load_gates(start_hbm, mats_hbm, bias_hbm, *scratch)
     weight = start[...]
     for t in range(steps):
-        parts = split(weight)
-        r = sigmoid(gate(1, parts) + bias[1])
-        mixed = r * weight
-        mixed_parts = split(mixed)
-        u_in = gate(0, parts)
-        c_in = gate(2, parts)
-        u = sigmoid(u_in + bias[0])
-        c = jnp.tanh(c_in + gate(3, mixed_parts) + bias[2])
-        rest = 1.0 - u
-        keep[t] = rest
+        u, r, c, mixed, fresh = gate_step(weight, bias, mats_high, mats_low)
+        keep[t] = 1.0 - u
         reset[t] = r
-        gate_slope[t] = (c - weight) * (u * rest)
+        gate_slope[t] = (c - weight) * (u * (1.0 - u))
         proposal_slope[t] = u * (1.0 - c * c)
         reset_slope[t] = mixed * (1.0 - r)
         lanes = pl.ds(t * width, width)
-        weights_wide[:, lanes] = parts[0]
-        reset_wide[:, lanes] = mixed_parts[0]
-        weight = rest * weight + u * c
+        weights_wide[:, lanes] = weight.astype(BF16)
+        reset_wide[:, lanes] = mixed.astype(BF16)
+        weight = fresh
         low[t] = weight.astype(BF16)
     for k in range(4):
         turned_high[k] = mats_high[k].T
-        turned_low[k] = mats_low[k].T
-    own = low[lax.axis_index("snap")]
-    score_matrix[...] = dot(own, own, LANES).astype(BF16)
+    for k in range(2):
+        turned_low[k] = mats_low[k + 2].T
+
+    @pl.when(odd)
+    def _():
+        score_matrix[...] = early_score_matrix[...]
+
+    @pl.when(jnp.logical_not(odd))
+    def _():
+        write_score_matrix(low, score_matrix)
 
 
 def edge_kernel(
@@ -185,8 +215,37 @@
         packed[pl.ds(2 * quarter, PACK_EXTRA), :] = extra
 
 
+def local_gradient(pieces, low, core, s, out):
+    width = low.shape[1]
+    quarter = width // 2
+    i = lax.broadcasted_iota(jnp.int32, (quarter, quarter), 0)
+    j = lax.broadcasted_iota(jnp.int32, (quarter, quarter), 1)
+    x = lax.div(lax.axis_index("snap"), 2)
+    piece = pieces[lax.rem(x - s + RING, RING)]
+    corner = piece[:quarter]
+    mixed = piece[quarter : 2 * quarter].astype(F32)
+    diagonal = piece[2 * quarter :].astype(F32)[0:1]
+    turned = mixed.T
+    upper = jnp.where(i <= j, mixed, turned).astype(BF16)
+    lower = jnp.where(i > j, mixed, jnp.where(i < j, turned, diagonal)).astype(BF16)
+    whole = jnp.concatenate(
+        [
+            jnp.concatenate([upper, corner], axis=1),
+            jnp.concatenate([corner.T, lower], axis=1),
+        ],
+        axis=0,
+    )
+    out[s] = dot(whole, low[2 * s + core])
+
+
+def local_kernel(along, low, mine):
+    core = lax.rem(lax.axis_index("snap"), 2)
+    for s in range(mine.shape[0]):
+        local_gradient(along, low, core, s, mine)
+
+
 def backward_kernel(
-    along,
+    mine,
     other,
     keep,
     gate_slope,
@@ -202,55 +261,39 @@
     grads,
     initial_grad,
     adjoints,
-    local,
+    others,
 ):
     steps, width = low.shape[0], low.shape[1]
-    quarter = width // 2
     place, node = lax.axis_index("snap"), lax.axis_index("node")
-    x, core = lax.div(place, 2), lax.rem(place, 2)
-    i = lax.broadcasted_iota(jnp.int32, (quarter, quarter), 0)
-    j = lax.broadcasted_iota(jnp.int32, (quarter, quarter), 1)
-
-    for t in range(steps):
-        turn = lax.rem(x - t // 2 + RING, RING)
-        piece = jnp.where(core == t % 2, along[turn], other[turn])
-        corner = piece[:quarter]
-        mixed = piece[quarter : 2 * quarter].astype(F32)
-        diagonal = piece[2 * quarter :].astype(F32)[0:1]
-        turned = mixed.T
-        upper = jnp.where(i <= j, mixed, turned).astype(BF16)
-        lower = jnp.where(i > j, mixed, jnp.where(i < j, turned, diagonal)).astype(BF16)
-        whole = jnp.concatenate(
-            [
-                jnp.concatenate([upper, corner], axis=1),
-                jnp.concatenate([corner.T, lower], axis=1),
-            ],
-            axis=0,
-        )
-        local[t] = dot(whole, low[t])
+    core = lax.rem(place, 2)
+    for s in range(steps // 2):
+        local_gradient(other, low, 1 - core, s, others)
 
     def gate(k, parts):
-        return dot3((turned_high[k], turned_low[k]), parts)
+        return dot3((turned_high[k], turned_low[k - 2]), parts)
+
+    def gate_once(k, part):
+        return dot(turned_high[k], part)
 
     grads[...] = jnp.zeros_like(grads)
 
     def step(s, carry):
         t = steps - 1 - s
-        g = local[t] + carry
+        g = jnp.where(lax.rem(t, 2) == core, mine[lax.div(t, 2)], others[lax.div(t, 2)]) + carry
         adjoints[t] = g
         d2 = g * proposal_slope[t]
         d2_parts = split(d2)
         mixed = gate(3, d2_parts)
         d0 = g * gate_slope[t]
-        d0_parts = split(d0)
-        fresh = g * keep[t] + (gate(0, d0_parts) + gate(2, d2_parts))
+        d0_high = d0.astype(BF16)
+        fresh = g * keep[t] + (gate_once(0, d0_high) + gate(2, d2_parts))
         d1 = mixed * reset_slope[t]
-        d1_parts = split(d1)
-        fresh = fresh + mixed * reset[t] + gate(1, d1_parts)
+        d1_high = d1.astype(BF16)
+        fresh = fresh + mixed * reset[t] + gate_once(1, d1_high)
         lanes = pl.ds(pl.multiple_of(t * width, width), width)
         before = weights_wide[:, lanes]
-        grads[0] += dot(d0_parts[0], before, LANES)
-        grads[1] += dot(d1_parts[0], before, LANES)
+        grads[0] += dot(d0_high, before, LANES)
+        grads[1] += dot(d1_high, before, LANES)
         grads[2] += dot(d2_parts[0], before, LANES)
         grads[3] += dot(d2_parts[0], reset_wide[:, lanes], LANES)
         grads[4] += d0
@@ -315,37 +358,47 @@
     side = tile_values.shape[-1]
     square = (snap_count, width, width)
 
+    sources = [
+        pltpu.with_memory_space_constraint(array, pltpu.HBM)
+        for array in (initial_weight, gate_mats, gate_bias)
+    ]
+    gate_scratch = [
+        pltpu.VMEM((width, width), F32),
+        pltpu.VMEM((4, width, width), F32),
+        pltpu.VMEM((3, width, width), F32),
+        pltpu.VMEM((4, width, width), BF16),
+        pltpu.VMEM((4, width, width), BF16),
+        pltpu.SemaphoreType.DMA((8,)),
+    ]
+    flat = jax.ShapeDtypeStruct((width, width), BF16)
+    early_score_matrix = pl.pallas_call(
+        early_kernel,
+        out_shape=flat,
+        in_specs=[HBM] * 3,
+        out_specs=VMEM,
+        scratch_shapes=[pltpu.VMEM(square, BF16)] + gate_scratch,
+        compiler_params=params(10),
+        name="forward_early",
+    )(*sources)
+    own, early_score_matrix = lax.optimization_barrier((own, early_score_matrix))
     even_pairs = [(i, i ^ 1) for i in range(node_count)]
     odd_pairs = [(i, (i - 1 + 2 * (i % 2)) % node_count) for i in range(node_count)]
     even_side = lax.ppermute(own, "node", even_pairs)
     odd_side = lax.ppermute(own, "node", odd_pairs)
 
     wide = jax.ShapeDtypeStruct(square, F32)
-    thin = jax.ShapeDtypeStruct(square, BF16)
     long = jax.ShapeDtypeStruct((width, snap_count * width), BF16)
-    mats = jax.ShapeDtypeStruct((4, width, width), BF16)
+    outs = [wide] * 5 + [jax.ShapeDtypeStruct(square, BF16), long, long]
+    outs += [jax.ShapeDtypeStruct((k, width, width), BF16) for k in (4, 2)] + [flat]
     *states, score_matrix = pl.pallas_call(
-        forward_kernel,
-        out_shape=[wide] * 5
-        + [thin, long, long, mats, mats, jax.ShapeDtypeStruct((width, width), BF16)],
-        in_specs=[HBM] * 3,
-        out_specs=[VMEM] * 11,
-        scratch_shapes=[
-            pltpu.VMEM((width, width), F32),
-            pltpu.VMEM((4, width, width), F32),
-            pltpu.VMEM((3, width, width), F32),
-            pltpu.VMEM((4, width, width), BF16),
-            pltpu.VMEM((4, width, width), BF16),
-            pltpu.SemaphoreType.DMA((8,)),
-        ],
-        compiler_params=params(16),
-        name="forward_chain",
-    )(
-        *(
-            pltpu.with_memory_space_constraint(array, pltpu.HBM)
-            for array in (initial_weight, gate_mats, gate_bias)
-        )
-    )
+        late_kernel,
+        out_shape=outs,
+        in_specs=[HBM] * 3 + [VMEM],
+        out_specs=[VMEM] * len(outs),
+        scratch_shapes=gate_scratch,
+        compiler_params=params(10),
+        name="forward_late",
+    )(*sources, early_score_matrix)
 
     factor = float(rows * node_count) ** (-0.5)
     pack_rows = width + PACK_EXTRA
@@ -378,6 +431,16 @@
     along = jnp.stack([copies[0], near, far, back])
     other = lax.ppermute(along, "snap", [(i, i ^ 1) for i in range(snap_count)])
 
+    half = (snap_count // 2, width, width)
+    mine = pl.pallas_call(
+        local_kernel,
+        out_shape=jax.ShapeDtypeStruct(half, F32),
+        in_specs=[VMEM] * 2,
+        out_specs=VMEM,
+        compiler_params=params(8),
+        name="local_gradients",
+    )(along, states[5])
+
     share = width // node_count
     adjoint_rows, grads, initial_grad = pl.pallas_call(
         backward_kernel,
@@ -388,10 +451,10 @@
         ],
         in_specs=[VMEM] * 12,
         out_specs=[VMEM] * 3,
-        scratch_shapes=[pltpu.VMEM(square, F32)] * 2,
+        scratch_shapes=[pltpu.VMEM(square, F32), pltpu.VMEM(half, F32)],
         compiler_params=params(16),
         name="backward_chain",
-    )(along, other, *states)
+    )(mine, other, *states)
     return adjoint_rows[None], grads, initial_grad
 
 

time: 61.2 us -> 56.8 us (0.928)
  Pallas kernels: 22 us -> 28.4 us
  starting transfers between devices: 25.4 us -> 19.4 us
  waiting for transfers between devices: 12.1 us -> 7.98 us
  local copies, waits for them, and re-layouts: 0.77 us -> 0.1 us
    pallas_call x1 -> x3, Pallas kernels: 7.89 us -> 15.7 us  [the longest x1 7.84 us: body(): pl.pallas_call(late_kernel, out_shape=outs, in_specs=[HBM] * 3 + [VMEM],...]
    ppermute x1, starting transfers between devices: 6.19 us -> 0.47 us  [body(): other = lax.ppermute(along, 'snap', [(i, i ^ 1) for i in range(snap_count)])]
    ppermute x1, waiting for transfers between devices: 3.21 us -> 0.01 us  [body(): odd_side = lax.ppermute(own, 'node', odd_pairs)]
    pallas_call x1, Pallas kernels: 8.6 us -> 7.18 us  [body(): pl.pallas_call(backward_kernel, out_shape=[jax.ShapeDtypeStruct((share, w...]
    squeeze x1, local copies, waits for them, and re-layouts: 0.76 us -> 0.08 us  [body(): tile_ids[0]]
  transfers between devices with their start and end apart: 12 -> 12, of which waited for: 10 -> 8; matrix products, arithmetic and copies ran while one was open for 1% -> 0% of each run, Pallas kernels for 13% -> 14%
where the time goes in v3:
time: 56.8 us; the launch traced here: 56.7 us
  Pallas kernels  28.4 us (50%)
  starting transfers between devices  19.4 us (34%)
  waiting for transfers between devices  7.98 us (14%)
  between operations  0.75 us (1%)
    ppermute x9, starting transfers between devices, ring_parts(): parts.append(lax.ppermute(copies[turn], axis, route))  11.8 us
    pallas_call x1, Pallas kernels, body(): pl.pallas_call(late_kernel, out_shape=outs, in_specs=[HBM] * 3 + [VMEM],...  7.84 us
    pallas_call x1, Pallas kernels, body(): pl.pallas_call(early_kernel, out_shape=flat, in_specs=[HBM] * 3, out_spec...  7.48 us
    pallas_call x1, Pallas kernels, body(): pl.pallas_call(backward_kernel, out_shape=[jax.ShapeDtypeStruct((share, w...  7.18 us
    ppermute x1, starting transfers between devices, body(): odd_side = lax.ppermute(own, 'node', odd_pairs)  7.11 us
    ppermute x9, waiting for transfers between devices, ring_parts(): parts.append(lax.ppermute(copies[turn], axis, route))  6.62 us
    pallas_call x1, Pallas kernels, body(): pl.pallas_call(functools.partial(edge_kernel, factor), out_shape=[jax.Sha...  5.45 us
  transfers between devices with their start and end apart: 12, of which 8 were waited for; matrix products, arithmetic and copies ran while one was open for 0% of the time, Pallas kernels for 14%

profile of v3, /device:TPU:1, one launch (start us, length us, event | category | flops | bytes accessed | tf_op | source)
XLA Modules:
  0.0 56.7 jit_solution(3185647805003476392)
XLA Ops:
  0.6 0.0 copy-start.1
  0.6 0.0 copy-start.4
  0.7 0.0 copy-start.3
  0.7 0.0 copy-start.2
  0.7 0.0 copy-start
  0.7 7.5 %forward_early.1.early_score_matrix = bf16[256,256]{1,0:T(8,128)(2,1)S(1)} custom-call(f32[256,256]{1,0:T(8,128)} %start_hbm.3, f32[4,256,256]{2,1,0:T(8,128)} %mats_hbm.3, f32[3,256,256]{2,1,0:T(8,128)} %bias_hbm.3), custom_call_target="tpu_custom_call" | custom-call | tf_op jit(solution)/shard_map/forward_early/pallas_call | solution.py:374
  8.2 0.0 copy-done.1
  8.2 7.1 %collective-permute-start.1 = (bf16[1024,256]{1,0:T(8,128)(2,1)S(1)}, bf16[1024,256]{1,0:T(8,128)(2,1)S(1)}, u32[]{:S(2)}, u32[]{:S(2)}) collective-permute-start(bf16[1024,256]{1,0:T(8,128)(2,1)S(1)} %bitcast.11), channel_id=1, source_target_pairs={{0,15},{1,2},{2,1},{3,4},{4,3},{5,6},{6,5},{7,8},{8,7},{9,10},{10,... | collective-permute-start | bytes 1572872 | tf_op jit(solution)/shard_map/ppermute | solution.py:387
  15.3 0.0 collective-permute-start
  15.3 0.0 copy-done.4
  15.3 0.1 copy.11.ids
  15.4 7.8 %forward_late.1 = (f32[8,256,256]{2,1,0:T(8,128)S(1)}, f32[8,256,256]{2,1,0:T(8,128)S(1)}, f32[8,256,256]{2,1,0:T(8,128)S(1)}, f32[8,256,256]{2,1,0:T(8,128)S(1)...) custom-call(f32[256,256]{1,0:T(8,128)} %start_hbm.3, ...), custom_call_target="tpu_custom_call" | custom-call | tf_op jit(solution)/shard_map/forward_late/pallas_call | solution.py:393
  23.2 0.0 collective-permute-done.1.odd_side
  23.2 0.5 collective-permute-done.even_side
  23.8 0.0 copy-done.3
  23.8 0.0 copy-done.2
  23.8 0.0 copy-done
  23.8 5.4 %edge_products.1 = (bf16[272,128]{1,0:T(8,128)(2,1)S(1)}, bf16[272,128]{1,0:T(8,128)(2,1)S(1)}, bf16[272,128]{1,0:T(8,128)(2,1)S(1)}, bf16[272,128]{1,0:T(8,128)(2,1)S(1)}) custom-call(s32[8,4]{1,0:T(8,128)S(1)} %copy.11.ids, bf16[1024,256]{1,0:T(8,128)(2,1)S(1)} %bitcast.13, bf16[1024,256]{1,0:T(8,128)(2,1)S(1)} %collective-permute-done.even_side, ...), custom_call_target="tpu_custom_call" | custom-call | tf_op jit(solution)/shard_map/edge_products/pallas_call | solution.py:405
  29.2 0.1 collective-permute-start.2
  29.3 1.0 %collective-permute-start.3 = (bf16[272,128]{1,0:T(8,128)(2,1)S(1)}, bf16[272,128]{1,0:T(8,128)(2,1)S(1)}, u32[]{:S(2)}, u32[]{:S(2)}) collective-permute-start(bf16[272,128]{1,0:T(8,128)(2,1)S(1)} %get-tuple-element.36), channel_id=1, source_target_pairs={{0,1},{1,2},{2,3},{3,0},{4,5},{5,6},{6,7},{7,4},{8,9},{9,10},{10,1... | collective-permute-start | bytes 208904 | tf_op jit(solution)/shard_map/ppermute | solution.py:325
  30.4 2.3 %collective-permute-start.4 = (bf16[272,128]{1,0:T(8,128)(2,1)S(1)}, bf16[272,128]{1,0:T(8,128)(2,1)S(1)}, u32[]{:S(2)}, u32[]{:S(2)}) collective-permute-start(bf16[272,128]{1,0:T(8,128)(2,1)S(1)} %get-tuple-element.37), channel_id=1, source_target_pairs={{0,3},{1,0},{2,1},{3,2},{4,7},{5,4},{6,5},{7,6},{8,11},{9,8},{10,9... | collective-permute-start | bytes 208904 | tf_op jit(solution)/shard_map/ppermute | solution.py:325
  32.7 1.4 %collective-permute-done.2.first = bf16[272,128]{1,0:T(8,128)(2,1)S(1)} collective-permute-done((bf16[272,128]{1,0:T(8,128)(2,1)S(1)}, bf16[272,128]{1,0:T(8,128)(2,1)S(1)}, u32[]{:S(2)}, u32[]{:S(2)}) %collective-permute-start.2) | collective-permute-done | bytes 69664 | tf_op jit(solution)/shard_map/ppermute | solution.py:325
  34.0 0.7 %collective-permute-done.3.second = bf16[272,128]{1,0:T(8,128)(2,1)S(1)} collective-permute-done((bf16[272,128]{1,0:T(8,128)(2,1)S(1)}, bf16[272,128]{1,0:T(8,128)(2,1)S(1)}, u32[]{:S(2)}, u32[]{:S(2)}) %collective-permute-start.3) | collective-permute-done | bytes 69664 | tf_op jit(solution)/shard_map/ppermute | solution.py:325
  34.7 0.0 collective-permute-done.4.third
  34.8 0.8 %collective-permute-start.5 = (bf16[272,128]{1,0:T(8,128)(2,1)S(1)}, bf16[272,128]{1,0:T(8,128)(2,1)S(1)}, u32[]{:S(2)}, u32[]{:S(2)}) collective-permute-start(bf16[272,128]{1,0:T(8,128)(2,1)S(1)} %get-tuple-element.39), channel_id=1, source_target_pairs={{0,8},{1,9},{2,10},{3,11},{4,12},{5,13},{6,14},{7,15},{8,0},{9,1},... | collective-permute-start | bytes 208904 | tf_op jit(solution)/shard_map/ppermute | solution.py:325
  35.6 1.5 %collective-permute-start.6 = (bf16[272,128]{1,0:T(8,128)(2,1)S(1)}, bf16[272,128]{1,0:T(8,128)(2,1)S(1)}, u32[]{:S(2)}, u32[]{:S(2)}) collective-permute-start(bf16[272,128]{1,0:T(8,128)(2,1)S(1)} %get-tuple-element.40), channel_id=1, source_target_pairs={{0,4},{1,5},{2,6},{3,7},{4,8},{5,9},{6,10},{7,11},{8,12},{9,13},{1... | collective-permute-start | bytes 208904 | tf_op jit(solution)/shard_map/ppermute | solution.py:325
  37.1 1.2 %collective-permute-start.7 = (bf16[272,128]{1,0:T(8,128)(2,1)S(1)}, bf16[272,128]{1,0:T(8,128)(2,1)S(1)}, u32[]{:S(2)}, u32[]{:S(2)}) collective-permute-start(bf16[272,128]{1,0:T(8,128)(2,1)S(1)} %get-tuple-element.41), channel_id=1, source_target_pairs={{0,12},{1,13},{2,14},{3,15},{4,0},{5,1},{6,2},{7,3},{8,4},{9,5},{1... | collective-permute-start | bytes 208904 | tf_op jit(solution)/shard_map/ppermute | solution.py:325
  38.3 1.3 %collective-permute-done.5.first = bf16[272,128]{1,0:T(8,128)(2,1)S(1)} collective-permute-done((bf16[272,128]{1,0:T(8,128)(2,1)S(1)}, bf16[272,128]{1,0:T(8,128)(2,1)S(1)}, u32[]{:S(2)}, u32[]{:S(2)}) %collective-permute-start.5) | collective-permute-done | bytes 69664 | tf_op jit(solution)/shard_map/ppermute | solution.py:325
  39.6 0.7 %collective-permute-done.6.second = bf16[272,128]{1,0:T(8,128)(2,1)S(1)} collective-permute-done((bf16[272,128]{1,0:T(8,128)(2,1)S(1)}, bf16[272,128]{1,0:T(8,128)(2,1)S(1)}, u32[]{:S(2)}, u32[]{:S(2)}) %collective-permute-start.6) | collective-permute-done | bytes 69664 | tf_op jit(solution)/shard_map/ppermute | solution.py:325
  40.3 0.0 collective-permute-done.7.third
  40.3 1.3 %collective-permute-start.8 = (bf16[272,128]{1,0:T(8,128)(2,1)S(1)}, bf16[272,128]{1,0:T(8,128)(2,1)S(1)}, u32[]{:S(2)}, u32[]{:S(2)}) collective-permute-start(bf16[272,128]{1,0:T(8,128)(2,1)S(1)} %get-tuple-element.43), channel_id=1, source_target_pairs={{0,32},{16,48},{32,64},{48,80},{64,96},{80,112},{96,0},{112,16},{1... | collective-permute-start | bytes 208904 | tf_op jit(solution)/shard_map/ppermute | solution.py:325
  41.6 2.4 %collective-permute-start.9 = (bf16[272,128]{1,0:T(8,128)(2,1)S(1)}, bf16[272,128]{1,0:T(8,128)(2,1)S(1)}, u32[]{:S(2)}, u32[]{:S(2)}) collective-permute-start(bf16[272,128]{1,0:T(8,128)(2,1)S(1)} %get-tuple-element.44), channel_id=1, source_target_pairs={{0,64},{16,80},{32,96},{48,112},{64,0},{80,16},{96,32},{112,48},{1... | collective-permute-start | bytes 208904 | tf_op jit(solution)/shard_map/ppermute | solution.py:325
  44.0 1.2 %collective-permute-start.10 = (bf16[272,128]{1,0:T(8,128)(2,1)S(1)}, bf16[272,128]{1,0:T(8,128)(2,1)S(1)}, u32[]{:S(2)}, u32[]{:S(2)}) collective-permute-start(bf16[272,128]{1,0:T(8,128)(2,1)S(1)} %get-tuple-element.45), channel_id=1, source_target_pairs={{0,96},{16,112},{32,0},{48,16},{64,32},{80,48},{96,64},{112,80},{1... | collective-permute-start | bytes 208904 | tf_op jit(solution)/shard_map/ppermute | solution.py:325
  45.2 0.0 collective-permute-done.8
  45.2 2.0 %collective-permute-done.9 = bf16[272,128]{1,0:T(8,128)(2,1)S(1)} collective-permute-done((bf16[272,128]{1,0:T(8,128)(2,1)S(1)}, bf16[272,128]{1,0:T(8,128)(2,1)S(1)}, u32[]{:S(2)}, u32[]{:S(2)}) %collective-permute-start.9) | collective-permute-done | bytes 69664 | tf_op jit(solution)/shard_map/ppermute | solution.py:325
  47.2 0.5 collective-permute-done.10
  47.8 0.5 collective-permute-start.11
  48.3 0.4 local_gradients.1.mine
  48.7 0.8 %collective-permute-done.11.other = bf16[4,272,128]{2,1,0:T(8,128)(2,1)S(1)} collective-permute-done((bf16[4,272,128]{2,1,0:T(8,128)(2,1)S(1)}, bf16[4,272,128]{2,1,0:T(8,128)(2,1)S(1)}, u32[]{:S(2)}, u32[]{:S(2)}) %collective-permute-start.11) | collective-permute-done | bytes 278560 | tf_op jit(solution)/shard_map/ppermute | solution.py:432
  49.5 7.2 %backward_chain.1 = (f32[16,256]{1,0:T(8,128)}, f32[7,256,256]{2,1,0:T(8,128)}, f32[256,256]{1,0:T(8,128)}) custom-call(f32[4,256,256]{2,1,0:T(8,128)S(1)} %local_gradients.1.mine, bf16[4,272,128]{2,1,0:T(8,128)(2,1)S(1)} %collective-permute-done.11.other, f32[8,256,256]{2,1,0:T(8,128)S(1)} %get-tuple-element.47.keep, ...), custom_call_target="tpu_custom_call" | custom-call | tf_op jit(solution)/shard_map/backward_chain/pallas_call | solution.py:445
  (3 shorter events, 0.1 us)
Async XLA Ops:
  0.6 7.5 %copy-start.1 = (bf16[1,1024,256]{2,1,0:T(8,128)(2,1)S(1)}, bf16[1,1024,256]{2,1,0:T(8,128)(2,1)}, u32[]{:S(2)}) copy-start(bf16[1,1024,256]{2,1,0:T(8,128)(2,1)} %param.8) | copy-start | bytes 1572868
  0.6 14.7 %copy-start.4 = (s32[1,8,4]{1,2,0:T(4,128)S(1)}, s32[1,8,4]{1,2,0:T(4,128)}, u32[]{:S(2)}) copy-start(s32[1,8,4]{1,2,0:T(4,128)} %param.9) | copy-start | bytes 388
  0.7 23.1 %copy-start.3 = (s32[1,2,1024]{2,1,0:T(2,128)S(1)}, s32[1,2,1024]{2,1,0:T(2,128)}, u32[]{:S(2)}) copy-start(s32[1,2,1024]{2,1,0:T(2,128)} %param.12) | copy-start | bytes 24580
  0.7 23.1 %copy-start.2 = (s32[1,2,1024]{2,1,0:T(2,128)S(1)}, s32[1,2,1024]{2,1,0:T(2,128)}, u32[]{:S(2)}) copy-start(s32[1,2,1024]{2,1,0:T(2,128)} %param.11) | copy-start | bytes 24580
  0.7 23.1 %copy-start = (bf16[1,8,4,128,128]{4,3,2,1,0:T(8,128)(2,1)S(1)}, bf16[1,8,4,128,128]{4,3,2,1,0:T(8,128)(2,1)}, u32[]{:S(2)}) copy-start(bf16[1,8,4,128,128]{4,3,2,1,0:T(8,128)(2,1)} %param.10) | copy-start | bytes 3145732
  8.2 15.1 %collective-permute-start.1 = (bf16[1024,256]{1,0:T(8,128)(2,1)S(1)}, bf16[1024,256]{1,0:T(8,128)(2,1)S(1)}, u32[]{:S(2)}, u32[]{:S(2)}) collective-permute-start(bf16[1024,256]{1,0:T(8,128)(2,1)S(1)} %bitcast.11), channel_id=1, source_target_pairs={{0,15},{1,2},{2,1},{3,4},{4,3},{5,6},{6,5},{7,8},{8,7},{9,10},{10,... | collective-permute-start | bytes 1572872 | tf_op jit(solution)/shard_map/ppermute | solution.py:387
  15.3 8.5 %collective-permute-start = (bf16[1024,256]{1,0:T(8,128)(2,1)S(1)}, bf16[1024,256]{1,0:T(8,128)(2,1)S(1)}, u32[]{:S(2)}, u32[]{:S(2)}) collective-permute-start(bf16[1024,256]{1,0:T(8,128)(2,1)S(1)} %bitcast.12), channel_id=1, source_target_pairs={{0,1},{1,0},{2,3},{3,2},{4,5},{5,4},{6,7},{7,6},{8,9},{9,8},{10,11... | collective-permute-start | bytes 1572872 | tf_op jit(solution)/shard_map/ppermute | solution.py:386
  29.2 4.8 %collective-permute-start.2 = (bf16[272,128]{1,0:T(8,128)(2,1)S(1)}, bf16[272,128]{1,0:T(8,128)(2,1)S(1)}, u32[]{:S(2)}, u32[]{:S(2)}) collective-permute-start(bf16[272,128]{1,0:T(8,128)(2,1)S(1)} %get-tuple-element.35), channel_id=1, source_target_pairs={{0,2},{1,3},{2,0},{3,1},{4,6},{5,7},{6,4},{7,5},{8,10},{9,11},{10,... | collective-permute-start | bytes 208904 | tf_op jit(solution)/shard_map/ppermute | solution.py:325
  29.3 5.4 %collective-permute-start.3 = (bf16[272,128]{1,0:T(8,128)(2,1)S(1)}, bf16[272,128]{1,0:T(8,128)(2,1)S(1)}, u32[]{:S(2)}, u32[]{:S(2)}) collective-permute-start(bf16[272,128]{1,0:T(8,128)(2,1)S(1)} %get-tuple-element.36), channel_id=1, source_target_pairs={{0,1},{1,2},{2,3},{3,0},{4,5},{5,6},{6,7},{7,4},{8,9},{9,10},{10,1... | collective-permute-start | bytes 208904 | tf_op jit(solution)/shard_map/ppermute | solution.py:325
  30.4 4.4 %collective-permute-start.4 = (bf16[272,128]{1,0:T(8,128)(2,1)S(1)}, bf16[272,128]{1,0:T(8,128)(2,1)S(1)}, u32[]{:S(2)}, u32[]{:S(2)}) collective-permute-start(bf16[272,128]{1,0:T(8,128)(2,1)S(1)} %get-tuple-element.37), channel_id=1, source_target_pairs={{0,3},{1,0},{2,1},{3,2},{4,7},{5,4},{6,5},{7,6},{8,11},{9,8},{10,9... | collective-permute-start | bytes 208904 | tf_op jit(solution)/shard_map/ppermute | solution.py:325
  34.8 4.8 %collective-permute-start.5 = (bf16[272,128]{1,0:T(8,128)(2,1)S(1)}, bf16[272,128]{1,0:T(8,128)(2,1)S(1)}, u32[]{:S(2)}, u32[]{:S(2)}) collective-permute-start(bf16[272,128]{1,0:T(8,128)(2,1)S(1)} %get-tuple-element.39), channel_id=1, source_target_pairs={{0,8},{1,9},{2,10},{3,11},{4,12},{5,13},{6,14},{7,15},{8,0},{9,1},... | collective-permute-start | bytes 208904 | tf_op jit(solution)/shard_map/ppermute | solution.py:325
  35.6 4.7 %collective-permute-start.6 = (bf16[272,128]{1,0:T(8,128)(2,1)S(1)}, bf16[272,128]{1,0:T(8,128)(2,1)S(1)}, u32[]{:S(2)}, u32[]{:S(2)}) collective-permute-start(bf16[272,128]{1,0:T(8,128)(2,1)S(1)} %get-tuple-element.40), channel_id=1, source_target_pairs={{0,4},{1,5},{2,6},{3,7},{4,8},{5,9},{6,10},{7,11},{8,12},{9,13},{1... | collective-permute-start | bytes 208904 | tf_op jit(solution)/shard_map/ppermute | solution.py:325
  37.1 3.2 %collective-permute-start.7 = (bf16[272,128]{1,0:T(8,128)(2,1)S(1)}, bf16[272,128]{1,0:T(8,128)(2,1)S(1)}, u32[]{:S(2)}, u32[]{:S(2)}) collective-permute-start(bf16[272,128]{1,0:T(8,128)(2,1)S(1)} %get-tuple-element.41), channel_id=1, source_target_pairs={{0,12},{1,13},{2,14},{3,15},{4,0},{5,1},{6,2},{7,3},{8,4},{9,5},{1... | collective-permute-start | bytes 208904 | tf_op jit(solution)/shard_map/ppermute | solution.py:325
  40.3 4.9 %collective-permute-start.8 = (bf16[272,128]{1,0:T(8,128)(2,1)S(1)}, bf16[272,128]{1,0:T(8,128)(2,1)S(1)}, u32[]{:S(2)}, u32[]{:S(2)}) collective-permute-start(bf16[272,128]{1,0:T(8,128)(2,1)S(1)} %get-tuple-element.43), channel_id=1, source_target_pairs={{0,32},{16,48},{32,64},{48,80},{64,96},{80,112},{96,0},{112,16},{1... | collective-permute-start | bytes 208904 | tf_op jit(solution)/shard_map/ppermute | solution.py:325
  41.6 5.6 %collective-permute-start.9 = (bf16[272,128]{1,0:T(8,128)(2,1)S(1)}, bf16[272,128]{1,0:T(8,128)(2,1)S(1)}, u32[]{:S(2)}, u32[]{:S(2)}) collective-permute-start(bf16[272,128]{1,0:T(8,128)(2,1)S(1)} %get-tuple-element.44), channel_id=1, source_target_pairs={{0,64},{16,80},{32,96},{48,112},{64,0},{80,16},{96,32},{112,48},{1... | collective-permute-start | bytes 208904 | tf_op jit(solution)/shard_map/ppermute | solution.py:325
  44.0 3.7 %collective-permute-start.10 = (bf16[272,128]{1,0:T(8,128)(2,1)S(1)}, bf16[272,128]{1,0:T(8,128)(2,1)S(1)}, u32[]{:S(2)}, u32[]{:S(2)}) collective-permute-start(bf16[272,128]{1,0:T(8,128)(2,1)S(1)} %get-tuple-element.45), channel_id=1, source_target_pairs={{0,96},{16,112},{32,0},{48,16},{64,32},{80,48},{96,64},{112,80},{1... | collective-permute-start | bytes 208904 | tf_op jit(solution)/shard_map/ppermute | solution.py:325
  47.8 1.7 %collective-permute-start.11 = (bf16[4,272,128]{2,1,0:T(8,128)(2,1)S(1)}, bf16[4,272,128]{2,1,0:T(8,128)(2,1)S(1)}, u32[]{:S(2)}, u32[]{:S(2)}) collective-permute-start(bf16[4,272,128]{2,1,0:T(8,128)(2,1)S(1)} %pad_maximum_fusion.along), channel_id=1, source_target_pairs={{0,16},{16,0},{32,48},{48,32},{64,80},{80,64},{96,112},{112,96},{1... | collective-permute-start | bytes 835592 | tf_op jit(solution)/shard_map/ppermute | solution.py:432

commit v4 on v3

--- a/solution.py
+++ b/solution.py
@@ -9,6 +9,7 @@
 
 HALO = 1024
 RING = 4
+STRIDE = 3
 PACK_EXTRA = 16
 F32 = jnp.float32
 BF16 = jnp.bfloat16
@@ -59,13 +60,14 @@
         return dot3((mats_high[k], mats_low[k]), parts)
 
     parts = split(weight)
-    r = sigmoid(gate(1, parts) + bias[1])
+    r = sigmoid(dot(mats_high[1], parts[0]) + bias[1])
     mixed = r * weight
     mixed_parts = split(mixed)
+    c_in = gate(2, parts)
+    c_in = c_in + gate(3, mixed_parts)
     u_in = gate(0, parts)
-    c_in = gate(2, parts)
     u = sigmoid(u_in + bias[0])
-    c = jnp.tanh(c_in + gate(3, mixed_parts) + bias[2])
+    c = jnp.tanh(c_in + bias[2])
     return u, r, c, mixed, (1.0 - u) * weight + u * c
 
 
@@ -74,7 +76,7 @@
     score_matrix[...] = dot(own, own, LANES).astype(BF16)
 
 
-def early_kernel(start_hbm, mats_hbm, bias_hbm, score_matrix, low, *scratch):
+def early_kernel(start_hbm, mats_hbm, bias_hbm, before, score_matrix, low, *scratch):
     start, mats, bias, mats_high, mats_low, sems = scratch
 
     @pl.when(lax.rem(lax.axis_index("snap"), 2) == 1)
@@ -82,6 +84,8 @@
         load_gates(start_hbm, mats_hbm, bias_hbm, *scratch)
         weight = start[...]
         for t in range(low.shape[0]):
+            if t > 0 and t % STRIDE == 0:
+                before[t // STRIDE - 1] = weight
             weight = gate_step(weight, bias, mats_high, mats_low)[-1]
             low[t] = weight.astype(BF16)
         write_score_matrix(low, score_matrix)
@@ -91,6 +95,7 @@
     start_hbm,
     mats_hbm,
     bias_hbm,
+    before,
     early_score_matrix,
     keep,
     gate_slope,
@@ -109,8 +114,8 @@
     steps, width = low.shape[0], low.shape[1]
     odd = lax.rem(lax.axis_index("snap"), 2) == 1
     load_gates(start_hbm, mats_hbm, bias_hbm, *scratch)
-    weight = start[...]
-    for t in range(steps):
+
+    def record(t, weight):
         u, r, c, mixed, fresh = gate_step(weight, bias, mats_high, mats_low)
         keep[t] = 1.0 - u
         reset[t] = r
@@ -120,20 +125,29 @@
         lanes = pl.ds(t * width, width)
         weights_wide[:, lanes] = weight.astype(BF16)
         reset_wide[:, lanes] = mixed.astype(BF16)
-        weight = fresh
-        low[t] = weight.astype(BF16)
+        low[t] = fresh.astype(BF16)
+        return fresh
+
+    @pl.when(odd)
+    def _():
+        weights = [start[...]] + [before[k] for k in range(before.shape[0])]
+        for s in range(STRIDE):
+            for k in range(len(weights)):
+                if k * STRIDE + s < steps:
+                    weights[k] = record(k * STRIDE + s, weights[k])
+        score_matrix[...] = early_score_matrix[...]
+
+    @pl.when(jnp.logical_not(odd))
+    def _():
+        weight = start[...]
+        for t in range(steps):
+            weight = record(t, weight)
+        write_score_matrix(low, score_matrix)
+
     for k in range(4):
         turned_high[k] = mats_high[k].T
     for k in range(2):
         turned_low[k] = mats_low[k + 2].T
-
-    @pl.when(odd)
-    def _():
-        score_matrix[...] = early_score_matrix[...]
-
-    @pl.when(jnp.logical_not(odd))
-    def _():
-        write_score_matrix(low, score_matrix)
 
 
 def edge_kernel(
@@ -153,6 +167,7 @@
     side = tiles.shape[1]
     blocks = rows // side
     per_block = ids.shape[1]
+    picks = ids[...]
     node, ends = lax.axis_index("node"), lax.axis_size("node") - 1
     odd = lax.rem(node, 2)
     inside = (node > 0) & (node < ends)
@@ -164,7 +179,7 @@
         total = jnp.zeros((side, width), F32)
         for k in range(0, per_block, 2):
             tile = jnp.concatenate([tiles[b * per_block + k], tiles[b * per_block + k + 1]], axis=1)
-            source = jnp.concatenate([extended[ids[b, k]], extended[ids[b, k + 1]]], axis=0)
+            source = jnp.concatenate([extended[picks[b, k]], extended[picks[b, k + 1]]], axis=0)
             total = total + dot(tile, source)
         aggregated[pl.ds(b * side, side), :] = total.astype(BF16)
 
@@ -197,8 +212,8 @@
             slope = sigmoid(-score) * (-factor)
         else:
             slope = sigmoid(score) * factor
-        scaled = split(slope * first.astype(F32))
-        half = half + dot(scaled[0], second, ROWS) + dot(scaled[1], second, ROWS)
+        scaled = (slope * first.astype(F32)).astype(BF16)
+        half = half + dot(scaled, second, ROWS)
     full = half + half.T
     quarter = width // 2
     upper = full[:quarter, :quarter]
@@ -312,7 +327,6 @@
 
 
 VMEM = pl.BlockSpec(memory_space=pltpu.VMEM)
-SMEM = pl.BlockSpec(memory_space=pltpu.SMEM)
 HBM = pl.BlockSpec(memory_space=pltpu.HBM)
 
 
@@ -370,49 +384,49 @@
         pltpu.VMEM((4, width, width), BF16),
         pltpu.SemaphoreType.DMA((8,)),
     ]
+    wide = jax.ShapeDtypeStruct(square, F32)
     flat = jax.ShapeDtypeStruct((width, width), BF16)
-    early_score_matrix = pl.pallas_call(
+    before, early_score_matrix = pl.pallas_call(
         early_kernel,
-        out_shape=flat,
+        out_shape=[jax.ShapeDtypeStruct(((snap_count - 1) // STRIDE, width, width), F32), flat],
         in_specs=[HBM] * 3,
-        out_specs=VMEM,
+        out_specs=[VMEM] * 2,
         scratch_shapes=[pltpu.VMEM(square, BF16)] + gate_scratch,
-        compiler_params=params(10),
+        compiler_params=params(7),
         name="forward_early",
     )(*sources)
-    own, early_score_matrix = lax.optimization_barrier((own, early_score_matrix))
+    own, before = lax.optimization_barrier((own, before))
     even_pairs = [(i, i ^ 1) for i in range(node_count)]
     odd_pairs = [(i, (i - 1 + 2 * (i % 2)) % node_count) for i in range(node_count)]
     even_side = lax.ppermute(own, "node", even_pairs)
     odd_side = lax.ppermute(own, "node", odd_pairs)
 
-    wide = jax.ShapeDtypeStruct(square, F32)
     long = jax.ShapeDtypeStruct((width, snap_count * width), BF16)
     outs = [wide] * 5 + [jax.ShapeDtypeStruct(square, BF16), long, long]
     outs += [jax.ShapeDtypeStruct((k, width, width), BF16) for k in (4, 2)] + [flat]
     *states, score_matrix = pl.pallas_call(
         late_kernel,
         out_shape=outs,
-        in_specs=[HBM] * 3 + [VMEM],
+        in_specs=[HBM] * 3 + [VMEM] * 2,
         out_specs=[VMEM] * len(outs),
         scratch_shapes=gate_scratch,
-        compiler_params=params(10),
+        compiler_params=params(7),
         name="forward_late",
-    )(*sources, early_score_matrix)
+    )(*sources, before, early_score_matrix)
 
     factor = float(rows * node_count) ** (-0.5)
     pack_rows = width + PACK_EXTRA
     copies = pl.pallas_call(
         functools.partial(edge_kernel, factor),
         out_shape=[jax.ShapeDtypeStruct((pack_rows, width // 2), BF16)] * RING,
-        in_specs=[SMEM] + [VMEM] * 7,
+        in_specs=[VMEM] * 8,
         out_specs=[VMEM] * RING,
         scratch_shapes=[
             pltpu.VMEM(((rows + 2 * HALO) // side, side, width), BF16),
             pltpu.VMEM((rows, width), BF16),
             pltpu.VMEM((4 * pos_edges.shape[-1], width), BF16),
         ],
-        compiler_params=params(16),
+        compiler_params=params(9),
         name="edge_products",
     )(
         tile_ids[0],
@@ -452,7 +466,7 @@
         in_specs=[VMEM] * 12,
         out_specs=[VMEM] * 3,
         scratch_shapes=[pltpu.VMEM(square, F32), pltpu.VMEM(half, F32)],
-        compiler_params=params(16),
+        compiler_params=params(9),
         name="backward_chain",
     )(mine, other, *states)
     return adjoint_rows[None], grads, initial_grad

time: 56.8 us -> 56.3 us (level)
  Pallas kernels: 28.4 us -> 24.2 us
  waiting for transfers between devices: 7.98 us -> 12 us
    pallas_call x2, Pallas kernels: 15.3 us -> 12.3 us  [the longest x1 6.91 us: body(): pl.pallas_call(early_kernel, out_shape=[jax.ShapeDtypeStruct(((snap_count...]
    ppermute x1, waiting for transfers between devices: 0.01 us -> 1.52 us  [body(): odd_side = lax.ppermute(own, 'node', odd_pairs)]
    ppermute x1, waiting for transfers between devices: 0.54 us -> 2.02 us  [body(): even_side = lax.ppermute(own, 'node', even_pairs)]
    pallas_call x1, Pallas kernels: 5.45 us -> 4.24 us  [body(): pl.pallas_call(functools.partial(edge_kernel, factor), out_shape=[jax.Sha...]
    ppermute x9, waiting for transfers between devices: 6.62 us -> 7.62 us  [ring_parts(): parts.append(lax.ppermute(copies[turn], axis, route))]
    ppermute x9, starting transfers between devices: 11.8 us -> 11 us  [ring_parts(): parts.append(lax.ppermute(copies[turn], axis, route))]
  transfers between devices with their start and end apart: 12 -> 12, of which waited for: 8 -> 10; matrix products, arithmetic and copies ran while one was open for 0% -> 0% of each run, Pallas kernels for 14% -> 10%
where the time goes in v4:
time: 56.3 us; the launch traced here: 56.1 us
  Pallas kernels  24.2 us (43%)
  starting transfers between devices  19 us (34%)
  waiting for transfers between devices  12 us (21%)
  between operations  0.75 us (1%)
    ppermute x9, starting transfers between devices, ring_parts(): parts.append(lax.ppermute(copies[turn], axis, route))  11 us
    ppermute x9, waiting for transfers between devices, ring_parts(): parts.append(lax.ppermute(copies[turn], axis, route))  7.62 us
    pallas_call x1, Pallas kernels, body(): pl.pallas_call(backward_kernel, out_shape=[jax.ShapeDtypeStruct((share, w...  7.25 us
    ppermute x1, starting transfers between devices, body(): odd_side = lax.ppermute(own, 'node', odd_pairs)  7.12 us
    pallas_call x1, Pallas kernels, body(): pl.pallas_call(early_kernel, out_shape=[jax.ShapeDtypeStruct(((snap_count...  6.91 us
    pallas_call x1, Pallas kernels, body(): pl.pallas_call(late_kernel, out_shape=outs, in_specs=[HBM] * 3 + [VMEM] *...  5.41 us
    pallas_call x1, Pallas kernels, body(): pl.pallas_call(functools.partial(edge_kernel, factor), out_shape=[jax.Sha...  4.24 us
    ppermute x1, waiting for transfers between devices, body(): even_side = lax.ppermute(own, 'node', even_pairs)  2.02 us
  transfers between devices with their start and end apart: 12, of which 10 were waited for; matrix products, arithmetic and copies ran while one was open for 0% of the time, Pallas kernels for 10%

profile of v4, /device:TPU:1, one launch (start us, length us, event | category | flops | bytes accessed | tf_op | source)
XLA Modules:
  0.0 56.1 jit_solution(15146655486071005850)
XLA Ops:
  0.6 0.0 copy-start.1
  0.6 0.0 copy-start.4
  0.7 0.0 copy-start.3
  0.7 0.0 copy-start.2
  0.7 0.0 copy-start
  0.7 6.9 %forward_early.1 = (f32[2,256,256]{2,1,0:T(8,128)S(1)}, bf16[256,256]{1,0:T(8,128)(2,1)S(1)}) custom-call(f32[256,256]{1,0:T(8,128)} %start_hbm.3, f32[4,256,256]{2,1,0:T(8,128)} %mats_hbm.3, f32[3,256,256]{2,1,0:T(8,128)} %bias_hbm.3), custom_call_target="tpu_custom_call" | custom-call | tf_op jit(solution)/shard_map/forward_early/pallas_call | solution.py:389
  7.6 0.0 copy-done.1
  7.6 7.1 %collective-permute-start.1 = (bf16[1024,256]{1,0:T(8,128)(2,1)S(1)}, bf16[1024,256]{1,0:T(8,128)(2,1)S(1)}, u32[]{:S(2)}, u32[]{:S(2)}) collective-permute-start(bf16[1024,256]{1,0:T(8,128)(2,1)S(1)} %bitcast.11), channel_id=1, source_target_pairs={{0,15},{1,2},{2,1},{3,4},{4,3},{5,6},{6,5},{7,8},{8,7},{9,10},{10,... | collective-permute-start | bytes 1572872 | tf_op jit(solution)/shard_map/ppermute | solution.py:402
  14.7 0.0 collective-permute-start
  14.7 0.0 copy-done.4
  14.7 0.1 copy.11.ids
  14.8 5.4 %forward_late.1 = (f32[8,256,256]{2,1,0:T(8,128)S(1)}, f32[8,256,256]{2,1,0:T(8,128)S(1)}, f32[8,256,256]{2,1,0:T(8,128)S(1)}, f32[8,256,256]{2,1,0:T(8,128)S(1)...) custom-call(f32[256,256]{1,0:T(8,128)} %start_hbm.3, ...), custom_call_target="tpu_custom_call" | custom-call | tf_op jit(solution)/shard_map/forward_late/pallas_call | solution.py:407
  20.2 1.5 %collective-permute-done.1.odd_side = bf16[1024,256]{1,0:T(8,128)(2,1)S(1)} collective-permute-done((bf16[1024,256]{1,0:T(8,128)(2,1)S(1)}, bf16[1024,256]{1,0:T(8,128)(2,1)S(1)}, u32[]{:S(2)}, u32[]{:S(2)}) %collective-permute-start.1) | collective-permute-done | bytes 524320 | tf_op jit(solution)/shard_map/ppermute | solution.py:402
  21.8 2.0 %collective-permute-done.even_side = bf16[1024,256]{1,0:T(8,128)(2,1)S(1)} collective-permute-done((bf16[1024,256]{1,0:T(8,128)(2,1)S(1)}, bf16[1024,256]{1,0:T(8,128)(2,1)S(1)}, u32[]{:S(2)}, u32[]{:S(2)}) %collective-permute-start) | collective-permute-done | bytes 524320 | tf_op jit(solution)/shard_map/ppermute | solution.py:401
  23.8 0.0 copy-done.3
  23.8 0.0 copy-done.2
  23.8 0.0 copy-done
  23.8 4.2 %edge_products.1 = (bf16[272,128]{1,0:T(8,128)(2,1)S(1)}, bf16[272,128]{1,0:T(8,128)(2,1)S(1)}, bf16[272,128]{1,0:T(8,128)(2,1)S(1)}, bf16[272,128]{1,0:T(8,128)(2,1)S(1)}) custom-call(s32[8,4]{1,0:T(8,128)S(1)} %copy.11.ids, bf16[1024,256]{1,0:T(8,128)(2,1)S(1)} %bitcast.13, bf16[1024,256]{1,0:T(8,128)(2,1)S(1)} %collective-permute-done.even_side, ...), custom_call_target="tpu_custom_call" | custom-call | tf_op jit(solution)/shard_map/edge_products/pallas_call | solution.py:419
  28.0 0.1 collective-permute-start.2
  28.1 0.1 collective-permute-start.3
  28.2 2.7 %collective-permute-start.4 = (bf16[272,128]{1,0:T(8,128)(2,1)S(1)}, bf16[272,128]{1,0:T(8,128)(2,1)S(1)}, u32[]{:S(2)}, u32[]{:S(2)}) collective-permute-start(bf16[272,128]{1,0:T(8,128)(2,1)S(1)} %get-tuple-element.41), channel_id=1, source_target_pairs={{0,3},{1,0},{2,1},{3,2},{4,7},{5,4},{6,5},{7,6},{8,11},{9,8},{10,9... | collective-permute-start | bytes 208904 | tf_op jit(solution)/shard_map/ppermute | solution.py:339
  30.9 2.0 %collective-permute-done.2.first = bf16[272,128]{1,0:T(8,128)(2,1)S(1)} collective-permute-done((bf16[272,128]{1,0:T(8,128)(2,1)S(1)}, bf16[272,128]{1,0:T(8,128)(2,1)S(1)}, u32[]{:S(2)}, u32[]{:S(2)}) %collective-permute-start.2) | collective-permute-done | bytes 69664 | tf_op jit(solution)/shard_map/ppermute | solution.py:339
  32.9 0.4 collective-permute-done.3.second
  33.3 0.0 collective-permute-done.4.third
  33.4 0.6 %collective-permute-start.5 = (bf16[272,128]{1,0:T(8,128)(2,1)S(1)}, bf16[272,128]{1,0:T(8,128)(2,1)S(1)}, u32[]{:S(2)}, u32[]{:S(2)}) collective-permute-start(bf16[272,128]{1,0:T(8,128)(2,1)S(1)} %get-tuple-element.43), channel_id=1, source_target_pairs={{0,8},{1,9},{2,10},{3,11},{4,12},{5,13},{6,14},{7,15},{8,0},{9,1},... | collective-permute-start | bytes 208904 | tf_op jit(solution)/shard_map/ppermute | solution.py:339
  33.9 1.9 %collective-permute-start.6 = (bf16[272,128]{1,0:T(8,128)(2,1)S(1)}, bf16[272,128]{1,0:T(8,128)(2,1)S(1)}, u32[]{:S(2)}, u32[]{:S(2)}) collective-permute-start(bf16[272,128]{1,0:T(8,128)(2,1)S(1)} %get-tuple-element.44), channel_id=1, source_target_pairs={{0,4},{1,5},{2,6},{3,7},{4,8},{5,9},{6,10},{7,11},{8,12},{9,13},{1... | collective-permute-start | bytes 208904 | tf_op jit(solution)/shard_map/ppermute | solution.py:339
  35.9 0.7 %collective-permute-start.7 = (bf16[272,128]{1,0:T(8,128)(2,1)S(1)}, bf16[272,128]{1,0:T(8,128)(2,1)S(1)}, u32[]{:S(2)}, u32[]{:S(2)}) collective-permute-start(bf16[272,128]{1,0:T(8,128)(2,1)S(1)} %get-tuple-element.45), channel_id=1, source_target_pairs={{0,12},{1,13},{2,14},{3,15},{4,0},{5,1},{6,2},{7,3},{8,4},{9,5},{1... | collective-permute-start | bytes 208904 | tf_op jit(solution)/shard_map/ppermute | solution.py:339
  36.6 1.5 %collective-permute-done.5.first = bf16[272,128]{1,0:T(8,128)(2,1)S(1)} collective-permute-done((bf16[272,128]{1,0:T(8,128)(2,1)S(1)}, bf16[272,128]{1,0:T(8,128)(2,1)S(1)}, u32[]{:S(2)}, u32[]{:S(2)}) %collective-permute-start.5) | collective-permute-done | bytes 69664 | tf_op jit(solution)/shard_map/ppermute | solution.py:339
  38.2 0.7 %collective-permute-done.6.second = bf16[272,128]{1,0:T(8,128)(2,1)S(1)} collective-permute-done((bf16[272,128]{1,0:T(8,128)(2,1)S(1)}, bf16[272,128]{1,0:T(8,128)(2,1)S(1)}, u32[]{:S(2)}, u32[]{:S(2)}) %collective-permute-start.6) | collective-permute-done | bytes 69664 | tf_op jit(solution)/shard_map/ppermute | solution.py:339
  38.9 0.2 collective-permute-done.7.third
  39.1 1.3 %collective-permute-start.8 = (bf16[272,128]{1,0:T(8,128)(2,1)S(1)}, bf16[272,128]{1,0:T(8,128)(2,1)S(1)}, u32[]{:S(2)}, u32[]{:S(2)}) collective-permute-start(bf16[272,128]{1,0:T(8,128)(2,1)S(1)} %get-tuple-element.47), channel_id=1, source_target_pairs={{0,32},{16,48},{32,64},{48,80},{64,96},{80,112},{96,0},{112,16},{1... | collective-permute-start | bytes 208904 | tf_op jit(solution)/shard_map/ppermute | solution.py:339
  40.4 2.5 %collective-permute-start.9 = (bf16[272,128]{1,0:T(8,128)(2,1)S(1)}, bf16[272,128]{1,0:T(8,128)(2,1)S(1)}, u32[]{:S(2)}, u32[]{:S(2)}) collective-permute-start(bf16[272,128]{1,0:T(8,128)(2,1)S(1)} %get-tuple-element.48), channel_id=1, source_target_pairs={{0,64},{16,80},{32,96},{48,112},{64,0},{80,16},{96,32},{112,48},{1... | collective-permute-start | bytes 208904 | tf_op jit(solution)/shard_map/ppermute | solution.py:339
  42.8 1.2 %collective-permute-start.10 = (bf16[272,128]{1,0:T(8,128)(2,1)S(1)}, bf16[272,128]{1,0:T(8,128)(2,1)S(1)}, u32[]{:S(2)}, u32[]{:S(2)}) collective-permute-start(bf16[272,128]{1,0:T(8,128)(2,1)S(1)} %get-tuple-element.49), channel_id=1, source_target_pairs={{0,96},{16,112},{32,0},{48,16},{64,32},{80,48},{96,64},{112,80},{1... | collective-permute-start | bytes 208904 | tf_op jit(solution)/shard_map/ppermute | solution.py:339
  44.0 0.3 collective-permute-done.8
  44.3 2.5 %collective-permute-done.9 = bf16[272,128]{1,0:T(8,128)(2,1)S(1)} collective-permute-done((bf16[272,128]{1,0:T(8,128)(2,1)S(1)}, bf16[272,128]{1,0:T(8,128)(2,1)S(1)}, u32[]{:S(2)}, u32[]{:S(2)}) %collective-permute-start.9) | collective-permute-done | bytes 69664 | tf_op jit(solution)/shard_map/ppermute | solution.py:339
  46.7 0.0 collective-permute-done.10
  46.8 0.9 %collective-permute-start.11 = (bf16[4,272,128]{2,1,0:T(8,128)(2,1)S(1)}, bf16[4,272,128]{2,1,0:T(8,128)(2,1)S(1)}, u32[]{:S(2)}, u32[]{:S(2)}) collective-permute-start(bf16[4,272,128]{2,1,0:T(8,128)(2,1)S(1)} %pad_maximum_fusion.along), channel_id=1, source_target_pairs={{0,16},{16,0},{32,48},{48,32},{64,80},{80,64},{96,112},{112,96},{1... | collective-permute-start | bytes 835592 | tf_op jit(solution)/shard_map/ppermute | solution.py:446
  47.7 0.4 local_gradients.1.mine
  48.0 0.8 %collective-permute-done.11.other = bf16[4,272,128]{2,1,0:T(8,128)(2,1)S(1)} collective-permute-done((bf16[4,272,128]{2,1,0:T(8,128)(2,1)S(1)}, bf16[4,272,128]{2,1,0:T(8,128)(2,1)S(1)}, u32[]{:S(2)}, u32[]{:S(2)}) %collective-permute-start.11) | collective-permute-done | bytes 278560 | tf_op jit(solution)/shard_map/ppermute | solution.py:446
  48.9 7.2 %backward_chain.1 = (f32[16,256]{1,0:T(8,128)}, f32[7,256,256]{2,1,0:T(8,128)}, f32[256,256]{1,0:T(8,128)}) custom-call(f32[4,256,256]{2,1,0:T(8,128)S(1)} %local_gradients.1.mine, bf16[4,272,128]{2,1,0:T(8,128)(2,1)S(1)} %collective-permute-done.11.other, f32[8,256,256]{2,1,0:T(8,128)S(1)} %get-tuple-element.51.keep, ...), custom_call_target="tpu_custom_call" | custom-call | tf_op jit(solution)/shard_map/backward_chain/pallas_call | solution.py:459
  (3 shorter events, 0.1 us)
Async XLA Ops:
  0.6 7.0 %copy-start.1 = (bf16[1,1024,256]{2,1,0:T(8,128)(2,1)S(1)}, bf16[1,1024,256]{2,1,0:T(8,128)(2,1)}, u32[]{:S(2)}) copy-start(bf16[1,1024,256]{2,1,0:T(8,128)(2,1)} %param.8) | copy-start | bytes 1572868
  0.6 14.1 %copy-start.4 = (s32[1,8,4]{1,2,0:T(4,128)S(1)}, s32[1,8,4]{1,2,0:T(4,128)}, u32[]{:S(2)}) copy-start(s32[1,8,4]{1,2,0:T(4,128)} %param.9) | copy-start | bytes 388
  0.7 23.1 %copy-start.3 = (s32[1,2,1024]{2,1,0:T(2,128)S(1)}, s32[1,2,1024]{2,1,0:T(2,128)}, u32[]{:S(2)}) copy-start(s32[1,2,1024]{2,1,0:T(2,128)} %param.12) | copy-start | bytes 24580
  0.7 23.1 %copy-start.2 = (s32[1,2,1024]{2,1,0:T(2,128)S(1)}, s32[1,2,1024]{2,1,0:T(2,128)}, u32[]{:S(2)}) copy-start(s32[1,2,1024]{2,1,0:T(2,128)} %param.11) | copy-start | bytes 24580
  0.7 23.1 %copy-start = (bf16[1,8,4,128,128]{4,3,2,1,0:T(8,128)(2,1)S(1)}, bf16[1,8,4,128,128]{4,3,2,1,0:T(8,128)(2,1)}, u32[]{:S(2)}) copy-start(bf16[1,8,4,128,128]{4,3,2,1,0:T(8,128)(2,1)} %param.10) | copy-start | bytes 3145732
  7.6 14.1 %collective-permute-start.1 = (bf16[1024,256]{1,0:T(8,128)(2,1)S(1)}, bf16[1024,256]{1,0:T(8,128)(2,1)S(1)}, u32[]{:S(2)}, u32[]{:S(2)}) collective-permute-start(bf16[1024,256]{1,0:T(8,128)(2,1)S(1)} %bitcast.11), channel_id=1, source_target_pairs={{0,15},{1,2},{2,1},{3,4},{4,3},{5,6},{6,5},{7,8},{8,7},{9,10},{10,... | collective-permute-start | bytes 1572872 | tf_op jit(solution)/shard_map/ppermute | solution.py:402
  14.7 9.0 %collective-permute-start = (bf16[1024,256]{1,0:T(8,128)(2,1)S(1)}, bf16[1024,256]{1,0:T(8,128)(2,1)S(1)}, u32[]{:S(2)}, u32[]{:S(2)}) collective-permute-start(bf16[1024,256]{1,0:T(8,128)(2,1)S(1)} %bitcast.12), channel_id=1, source_target_pairs={{0,1},{1,0},{2,3},{3,2},{4,5},{5,4},{6,7},{7,6},{8,9},{9,8},{10,11... | collective-permute-start | bytes 1572872 | tf_op jit(solution)/shard_map/ppermute | solution.py:401
  28.0 4.9 %collective-permute-start.2 = (bf16[272,128]{1,0:T(8,128)(2,1)S(1)}, bf16[272,128]{1,0:T(8,128)(2,1)S(1)}, u32[]{:S(2)}, u32[]{:S(2)}) collective-permute-start(bf16[272,128]{1,0:T(8,128)(2,1)S(1)} %get-tuple-element.39), channel_id=1, source_target_pairs={{0,2},{1,3},{2,0},{3,1},{4,6},{5,7},{6,4},{7,5},{8,10},{9,11},{10,... | collective-permute-start | bytes 208904 | tf_op jit(solution)/shard_map/ppermute | solution.py:339
  28.1 5.2 %collective-permute-start.3 = (bf16[272,128]{1,0:T(8,128)(2,1)S(1)}, bf16[272,128]{1,0:T(8,128)(2,1)S(1)}, u32[]{:S(2)}, u32[]{:S(2)}) collective-permute-start(bf16[272,128]{1,0:T(8,128)(2,1)S(1)} %get-tuple-element.40), channel_id=1, source_target_pairs={{0,1},{1,2},{2,3},{3,0},{4,5},{5,6},{6,7},{7,4},{8,9},{9,10},{10,1... | collective-permute-start | bytes 208904 | tf_op jit(solution)/shard_map/ppermute | solution.py:339
  28.2 5.1 %collective-permute-start.4 = (bf16[272,128]{1,0:T(8,128)(2,1)S(1)}, bf16[272,128]{1,0:T(8,128)(2,1)S(1)}, u32[]{:S(2)}, u32[]{:S(2)}) collective-permute-start(bf16[272,128]{1,0:T(8,128)(2,1)S(1)} %get-tuple-element.41), channel_id=1, source_target_pairs={{0,3},{1,0},{2,1},{3,2},{4,7},{5,4},{6,5},{7,6},{8,11},{9,8},{10,9... | collective-permute-start | bytes 208904 | tf_op jit(solution)/shard_map/ppermute | solution.py:339
  33.4 4.8 %collective-permute-start.5 = (bf16[272,128]{1,0:T(8,128)(2,1)S(1)}, bf16[272,128]{1,0:T(8,128)(2,1)S(1)}, u32[]{:S(2)}, u32[]{:S(2)}) collective-permute-start(bf16[272,128]{1,0:T(8,128)(2,1)S(1)} %get-tuple-element.43), channel_id=1, source_target_pairs={{0,8},{1,9},{2,10},{3,11},{4,12},{5,13},{6,14},{7,15},{8,0},{9,1},... | collective-permute-start | bytes 208904 | tf_op jit(solution)/shard_map/ppermute | solution.py:339
  33.9 4.9 %collective-permute-start.6 = (bf16[272,128]{1,0:T(8,128)(2,1)S(1)}, bf16[272,128]{1,0:T(8,128)(2,1)S(1)}, u32[]{:S(2)}, u32[]{:S(2)}) collective-permute-start(bf16[272,128]{1,0:T(8,128)(2,1)S(1)} %get-tuple-element.44), channel_id=1, source_target_pairs={{0,4},{1,5},{2,6},{3,7},{4,8},{5,9},{6,10},{7,11},{8,12},{9,13},{1... | collective-permute-start | bytes 208904 | tf_op jit(solution)/shard_map/ppermute | solution.py:339
  35.9 3.2 %collective-permute-start.7 = (bf16[272,128]{1,0:T(8,128)(2,1)S(1)}, bf16[272,128]{1,0:T(8,128)(2,1)S(1)}, u32[]{:S(2)}, u32[]{:S(2)}) collective-permute-start(bf16[272,128]{1,0:T(8,128)(2,1)S(1)} %get-tuple-element.45), channel_id=1, source_target_pairs={{0,12},{1,13},{2,14},{3,15},{4,0},{5,1},{6,2},{7,3},{8,4},{9,5},{1... | collective-permute-start | bytes 208904 | tf_op jit(solution)/shard_map/ppermute | solution.py:339
  39.1 5.2 %collective-permute-start.8 = (bf16[272,128]{1,0:T(8,128)(2,1)S(1)}, bf16[272,128]{1,0:T(8,128)(2,1)S(1)}, u32[]{:S(2)}, u32[]{:S(2)}) collective-permute-start(bf16[272,128]{1,0:T(8,128)(2,1)S(1)} %get-tuple-element.47), channel_id=1, source_target_pairs={{0,32},{16,48},{32,64},{48,80},{64,96},{80,112},{96,0},{112,16},{1... | collective-permute-start | bytes 208904 | tf_op jit(solution)/shard_map/ppermute | solution.py:339
  40.4 6.4 %collective-permute-start.9 = (bf16[272,128]{1,0:T(8,128)(2,1)S(1)}, bf16[272,128]{1,0:T(8,128)(2,1)S(1)}, u32[]{:S(2)}, u32[]{:S(2)}) collective-permute-start(bf16[272,128]{1,0:T(8,128)(2,1)S(1)} %get-tuple-element.48), channel_id=1, source_target_pairs={{0,64},{16,80},{32,96},{48,112},{64,0},{80,16},{96,32},{112,48},{1... | collective-permute-start | bytes 208904 | tf_op jit(solution)/shard_map/ppermute | solution.py:339
  42.8 3.9 %collective-permute-start.10 = (bf16[272,128]{1,0:T(8,128)(2,1)S(1)}, bf16[272,128]{1,0:T(8,128)(2,1)S(1)}, u32[]{:S(2)}, u32[]{:S(2)}) collective-permute-start(bf16[272,128]{1,0:T(8,128)(2,1)S(1)} %get-tuple-element.49), channel_id=1, source_target_pairs={{0,96},{16,112},{32,0},{48,16},{64,32},{80,48},{96,64},{112,80},{1... | collective-permute-start | bytes 208904 | tf_op jit(solution)/shard_map/ppermute | solution.py:339
  46.8 2.1 %collective-permute-start.11 = (bf16[4,272,128]{2,1,0:T(8,128)(2,1)S(1)}, bf16[4,272,128]{2,1,0:T(8,128)(2,1)S(1)}, u32[]{:S(2)}, u32[]{:S(2)}) collective-permute-start(bf16[4,272,128]{2,1,0:T(8,128)(2,1)S(1)} %pad_maximum_fusion.along), channel_id=1, source_target_pairs={{0,16},{16,0},{32,48},{48,32},{64,80},{80,64},{96,112},{112,96},{1... | collective-permute-start | bytes 835592 | tf_op jit(solution)/shard_map/ppermute | solution.py:446

commit v5 on v4

--- a/solution.py
+++ b/solution.py
@@ -10,6 +10,7 @@
 HALO = 1024
 RING = 4
 STRIDE = 3
+CHIPS_AT_ONCE = 2
 PACK_EXTRA = 16
 F32 = jnp.float32
 BF16 = jnp.bfloat16
@@ -292,9 +293,8 @@
 
     grads[...] = jnp.zeros_like(grads)
 
-    def step(s, carry):
-        t = steps - 1 - s
-        g = jnp.where(lax.rem(t, 2) == core, mine[lax.div(t, 2)], others[lax.div(t, 2)]) + carry
+    def step(t, local, carry):
+        g = local + carry
         adjoints[t] = g
         d2 = g * proposal_slope[t]
         d2_parts = split(d2)
@@ -316,7 +316,15 @@
         grads[6] += d2
         return fresh
 
-    initial_grad[...] = lax.fori_loop(0, steps, step, jnp.zeros((width, width), F32))
+    def steps_of_chips(turn, carry):
+        for k in range(CHIPS_AT_ONCE):
+            s = steps // 2 - 1 - (turn * CHIPS_AT_ONCE + k)
+            carry = step(2 * s + 1, jnp.where(core == 1, mine[s], others[s]), carry)
+            carry = step(2 * s, jnp.where(core == 0, mine[s], others[s]), carry)
+        return carry
+
+    turns = steps // (2 * CHIPS_AT_ONCE)
+    initial_grad[...] = lax.fori_loop(0, turns, steps_of_chips, jnp.zeros((width, width), F32))
     share = adjoint_rows.shape[0]
     start = pl.multiple_of(node * share, share)
     adjoint_rows[...] = adjoints[place, pl.ds(start, share), :]
@@ -395,11 +403,11 @@
         compiler_params=params(7),
         name="forward_early",
     )(*sources)
-    own, before = lax.optimization_barrier((own, before))
+    sent, before = lax.optimization_barrier((own, before))
     even_pairs = [(i, i ^ 1) for i in range(node_count)]
     odd_pairs = [(i, (i - 1 + 2 * (i % 2)) % node_count) for i in range(node_count)]
-    even_side = lax.ppermute(own, "node", even_pairs)
-    odd_side = lax.ppermute(own, "node", odd_pairs)
+    even_side = lax.ppermute(sent, "node", even_pairs)
+    odd_side = lax.ppermute(sent, "node", odd_pairs)
 
     long = jax.ShapeDtypeStruct((width, snap_count * width), BF16)
     outs = [wide] * 5 + [jax.ShapeDtypeStruct(square, BF16), long, long]

time: 56.3 us -> 55.9 us (level)
    pallas_call x1, Pallas kernels: 7.25 us -> 6.65 us  [body(): pl.pallas_call(backward_kernel, out_shape=[jax.ShapeDtypeStruct((share, w...]
where the time goes in v5:
time: 55.9 us; the launch traced here: 55.7 us
  Pallas kernels  23.7 us (42%)
  starting transfers between devices  19.2 us (34%)
  waiting for transfers between devices  12 us (21%)
  between operations  0.75 us (1%)
    ppermute x9, starting transfers between devices, ring_parts(): parts.append(lax.ppermute(copies[turn], axis, route))  11 us
    ppermute x9, waiting for transfers between devices, ring_parts(): parts.append(lax.ppermute(copies[turn], axis, route))  7.65 us
    ppermute x1, starting transfers between devices, body(): odd_side = lax.ppermute(sent, 'node', odd_pairs)  7.12 us
    pallas_call x1, Pallas kernels, body(): pl.pallas_call(early_kernel, out_shape=[jax.ShapeDtypeStruct(((snap_count...  6.91 us
    pallas_call x1, Pallas kernels, body(): pl.pallas_call(backward_kernel, out_shape=[jax.ShapeDtypeStruct((share, w...  6.65 us
    pallas_call x1, Pallas kernels, body(): pl.pallas_call(late_kernel, out_shape=outs, in_specs=[HBM] * 3 + [VMEM] *...  5.41 us
    pallas_call x1, Pallas kernels, body(): pl.pallas_call(functools.partial(edge_kernel, factor), out_shape=[jax.Sha...  4.24 us
    ppermute x1, waiting for transfers between devices, body(): even_side = lax.ppermute(sent, 'node', even_pairs)  2.02 us
  transfers between devices with their start and end apart: 12, of which 10 were waited for; matrix products, arithmetic and copies ran while one was open for 0% of the time, Pallas kernels for 10%

profile of v5, /device:TPU:1, one launch (start us, length us, event | category | flops | bytes accessed | tf_op | source)
XLA Modules:
  0.0 55.7 jit_solution(8946912455962291536)
XLA Ops:
  0.6 0.0 copy-start.1
  0.6 0.0 copy-start.4
  0.7 0.0 copy-start.3
  0.7 0.0 copy-start.2
  0.7 0.0 copy-start
  0.7 6.9 %forward_early.1 = (f32[2,256,256]{2,1,0:T(8,128)S(1)}, bf16[256,256]{1,0:T(8,128)(2,1)S(1)}) custom-call(f32[256,256]{1,0:T(8,128)} %start_hbm.3, f32[4,256,256]{2,1,0:T(8,128)} %mats_hbm.3, f32[3,256,256]{2,1,0:T(8,128)} %bias_hbm.3), custom_call_target="tpu_custom_call" | custom-call | tf_op jit(solution)/shard_map/forward_early/pallas_call | solution.py:397
  7.6 0.0 copy-done.1
  7.6 7.1 %collective-permute-start.1 = (bf16[1024,256]{1,0:T(8,128)(2,1)S(1)}, bf16[1024,256]{1,0:T(8,128)(2,1)S(1)}, u32[]{:S(2)}, u32[]{:S(2)}) collective-permute-start(bf16[1024,256]{1,0:T(8,128)(2,1)S(1)} %bitcast.11), channel_id=1, source_target_pairs={{0,15},{1,2},{2,1},{3,4},{4,3},{5,6},{6,5},{7,8},{8,7},{9,10},{10,... | collective-permute-start | bytes 1572872 | tf_op jit(solution)/shard_map/ppermute | solution.py:410
  14.7 0.0 collective-permute-start
  14.7 0.0 copy-done.4
  14.7 0.1 copy.11.ids
  14.8 5.4 %forward_late.1 = (f32[8,256,256]{2,1,0:T(8,128)S(1)}, f32[8,256,256]{2,1,0:T(8,128)S(1)}, f32[8,256,256]{2,1,0:T(8,128)S(1)}, f32[8,256,256]{2,1,0:T(8,128)S(1)...) custom-call(f32[256,256]{1,0:T(8,128)} %start_hbm.3, ...), custom_call_target="tpu_custom_call" | custom-call | tf_op jit(solution)/shard_map/forward_late/pallas_call | solution.py:415
  20.2 1.5 %collective-permute-done.1.odd_side = bf16[1024,256]{1,0:T(8,128)(2,1)S(1)} collective-permute-done((bf16[1024,256]{1,0:T(8,128)(2,1)S(1)}, bf16[1024,256]{1,0:T(8,128)(2,1)S(1)}, u32[]{:S(2)}, u32[]{:S(2)}) %collective-permute-start.1) | collective-permute-done | bytes 524320 | tf_op jit(solution)/shard_map/ppermute | solution.py:410
  21.8 2.0 %collective-permute-done.even_side = bf16[1024,256]{1,0:T(8,128)(2,1)S(1)} collective-permute-done((bf16[1024,256]{1,0:T(8,128)(2,1)S(1)}, bf16[1024,256]{1,0:T(8,128)(2,1)S(1)}, u32[]{:S(2)}, u32[]{:S(2)}) %collective-permute-start) | collective-permute-done | bytes 524320 | tf_op jit(solution)/shard_map/ppermute | solution.py:409
  23.8 0.0 copy-done.3
  23.8 0.0 copy-done.2
  23.8 0.0 copy-done
  23.8 4.2 %edge_products.1 = (bf16[272,128]{1,0:T(8,128)(2,1)S(1)}, bf16[272,128]{1,0:T(8,128)(2,1)S(1)}, bf16[272,128]{1,0:T(8,128)(2,1)S(1)}, bf16[272,128]{1,0:T(8,128)(2,1)S(1)}) custom-call(s32[8,4]{1,0:T(8,128)S(1)} %copy.11.ids, bf16[1024,256]{1,0:T(8,128)(2,1)S(1)} %bitcast.13, bf16[1024,256]{1,0:T(8,128)(2,1)S(1)} %collective-permute-done.even_side, ...), custom_call_target="tpu_custom_call" | custom-call | tf_op jit(solution)/shard_map/edge_products/pallas_call | solution.py:427
  28.0 0.1 collective-permute-start.2
  28.1 0.1 collective-permute-start.3
  28.2 2.7 %collective-permute-start.4 = (bf16[272,128]{1,0:T(8,128)(2,1)S(1)}, bf16[272,128]{1,0:T(8,128)(2,1)S(1)}, u32[]{:S(2)}, u32[]{:S(2)}) collective-permute-start(bf16[272,128]{1,0:T(8,128)(2,1)S(1)} %get-tuple-element.41), channel_id=1, source_target_pairs={{0,3},{1,0},{2,1},{3,2},{4,7},{5,4},{6,5},{7,6},{8,11},{9,8},{10,9... | collective-permute-start | bytes 208904 | tf_op jit(solution)/shard_map/ppermute | solution.py:347
  30.9 2.0 %collective-permute-done.2.first = bf16[272,128]{1,0:T(8,128)(2,1)S(1)} collective-permute-done((bf16[272,128]{1,0:T(8,128)(2,1)S(1)}, bf16[272,128]{1,0:T(8,128)(2,1)S(1)}, u32[]{:S(2)}, u32[]{:S(2)}) %collective-permute-start.2) | collective-permute-done | bytes 69664 | tf_op jit(solution)/shard_map/ppermute | solution.py:347
  32.9 0.4 collective-permute-done.3.second
  33.3 0.0 collective-permute-done.4.third
  33.4 0.6 %collective-permute-start.5 = (bf16[272,128]{1,0:T(8,128)(2,1)S(1)}, bf16[272,128]{1,0:T(8,128)(2,1)S(1)}, u32[]{:S(2)}, u32[]{:S(2)}) collective-permute-start(bf16[272,128]{1,0:T(8,128)(2,1)S(1)} %get-tuple-element.43), channel_id=1, source_target_pairs={{0,8},{1,9},{2,10},{3,11},{4,12},{5,13},{6,14},{7,15},{8,0},{9,1},... | collective-permute-start | bytes 208904 | tf_op jit(solution)/shard_map/ppermute | solution.py:347
  33.9 1.9 %collective-permute-start.6 = (bf16[272,128]{1,0:T(8,128)(2,1)S(1)}, bf16[272,128]{1,0:T(8,128)(2,1)S(1)}, u32[]{:S(2)}, u32[]{:S(2)}) collective-permute-start(bf16[272,128]{1,0:T(8,128)(2,1)S(1)} %get-tuple-element.44), channel_id=1, source_target_pairs={{0,4},{1,5},{2,6},{3,7},{4,8},{5,9},{6,10},{7,11},{8,12},{9,13},{1... | collective-permute-start | bytes 208904 | tf_op jit(solution)/shard_map/ppermute | solution.py:347
  35.9 0.7 %collective-permute-start.7 = (bf16[272,128]{1,0:T(8,128)(2,1)S(1)}, bf16[272,128]{1,0:T(8,128)(2,1)S(1)}, u32[]{:S(2)}, u32[]{:S(2)}) collective-permute-start(bf16[272,128]{1,0:T(8,128)(2,1)S(1)} %get-tuple-element.45), channel_id=1, source_target_pairs={{0,12},{1,13},{2,14},{3,15},{4,0},{5,1},{6,2},{7,3},{8,4},{9,5},{1... | collective-permute-start | bytes 208904 | tf_op jit(solution)/shard_map/ppermute | solution.py:347
  36.6 1.5 %collective-permute-done.5.first = bf16[272,128]{1,0:T(8,128)(2,1)S(1)} collective-permute-done((bf16[272,128]{1,0:T(8,128)(2,1)S(1)}, bf16[272,128]{1,0:T(8,128)(2,1)S(1)}, u32[]{:S(2)}, u32[]{:S(2)}) %collective-permute-start.5) | collective-permute-done | bytes 69664 | tf_op jit(solution)/shard_map/ppermute | solution.py:347
  38.2 0.7 %collective-permute-done.6.second = bf16[272,128]{1,0:T(8,128)(2,1)S(1)} collective-permute-done((bf16[272,128]{1,0:T(8,128)(2,1)S(1)}, bf16[272,128]{1,0:T(8,128)(2,1)S(1)}, u32[]{:S(2)}, u32[]{:S(2)}) %collective-permute-start.6) | collective-permute-done | bytes 69664 | tf_op jit(solution)/shard_map/ppermute | solution.py:347
  38.9 0.2 collective-permute-done.7.third
  39.1 1.3 %collective-permute-start.8 = (bf16[272,128]{1,0:T(8,128)(2,1)S(1)}, bf16[272,128]{1,0:T(8,128)(2,1)S(1)}, u32[]{:S(2)}, u32[]{:S(2)}) collective-permute-start(bf16[272,128]{1,0:T(8,128)(2,1)S(1)} %get-tuple-element.47), channel_id=1, source_target_pairs={{0,32},{16,48},{32,64},{48,80},{64,96},{80,112},{96,0},{112,16},{1... | collective-permute-start | bytes 208904 | tf_op jit(solution)/shard_map/ppermute | solution.py:347
  40.4 2.5 %collective-permute-start.9 = (bf16[272,128]{1,0:T(8,128)(2,1)S(1)}, bf16[272,128]{1,0:T(8,128)(2,1)S(1)}, u32[]{:S(2)}, u32[]{:S(2)}) collective-permute-start(bf16[272,128]{1,0:T(8,128)(2,1)S(1)} %get-tuple-element.48), channel_id=1, source_target_pairs={{0,64},{16,80},{32,96},{48,112},{64,0},{80,16},{96,32},{112,48},{1... | collective-permute-start | bytes 208904 | tf_op jit(solution)/shard_map/ppermute | solution.py:347
  42.8 1.1 %collective-permute-start.10 = (bf16[272,128]{1,0:T(8,128)(2,1)S(1)}, bf16[272,128]{1,0:T(8,128)(2,1)S(1)}, u32[]{:S(2)}, u32[]{:S(2)}) collective-permute-start(bf16[272,128]{1,0:T(8,128)(2,1)S(1)} %get-tuple-element.49), channel_id=1, source_target_pairs={{0,96},{16,112},{32,0},{48,16},{64,32},{80,48},{96,64},{112,80},{1... | collective-permute-start | bytes 208904 | tf_op jit(solution)/shard_map/ppermute | solution.py:347
  44.0 0.3 collective-permute-done.8
  44.3 2.5 %collective-permute-done.9 = bf16[272,128]{1,0:T(8,128)(2,1)S(1)} collective-permute-done((bf16[272,128]{1,0:T(8,128)(2,1)S(1)}, bf16[272,128]{1,0:T(8,128)(2,1)S(1)}, u32[]{:S(2)}, u32[]{:S(2)}) %collective-permute-start.9) | collective-permute-done | bytes 69664 | tf_op jit(solution)/shard_map/ppermute | solution.py:347
  46.7 0.0 collective-permute-done.10
  46.8 1.1 %collective-permute-start.11 = (bf16[4,272,128]{2,1,0:T(8,128)(2,1)S(1)}, bf16[4,272,128]{2,1,0:T(8,128)(2,1)S(1)}, u32[]{:S(2)}, u32[]{:S(2)}) collective-permute-start(bf16[4,272,128]{2,1,0:T(8,128)(2,1)S(1)} %pad_maximum_fusion.along), channel_id=1, source_target_pairs={{0,16},{16,0},{32,48},{48,32},{64,80},{80,64},{96,112},{112,96},{1... | collective-permute-start | bytes 835592 | tf_op jit(solution)/shard_map/ppermute | solution.py:454
  47.9 0.4 local_gradients.1.mine
  48.3 0.8 %collective-permute-done.11.other = bf16[4,272,128]{2,1,0:T(8,128)(2,1)S(1)} collective-permute-done((bf16[4,272,128]{2,1,0:T(8,128)(2,1)S(1)}, bf16[4,272,128]{2,1,0:T(8,128)(2,1)S(1)}, u32[]{:S(2)}, u32[]{:S(2)}) %collective-permute-start.11) | collective-permute-done | bytes 278560 | tf_op jit(solution)/shard_map/ppermute | solution.py:454
  49.1 6.7 %backward_chain.1 = (f32[16,256]{1,0:T(8,128)}, f32[7,256,256]{2,1,0:T(8,128)}, f32[256,256]{1,0:T(8,128)}) custom-call(f32[4,256,256]{2,1,0:T(8,128)S(1)} %local_gradients.1.mine, bf16[4,272,128]{2,1,0:T(8,128)(2,1)S(1)} %collective-permute-done.11.other, f32[8,256,256]{2,1,0:T(8,128)S(1)} %get-tuple-element.51.keep, ...), custom_call_target="tpu_custom_call" | custom-call | tf_op jit(solution)/shard_map/backward_chain/pallas_call | solution.py:467
  (3 shorter events, 0.1 us)
Async XLA Ops:
  0.6 7.0 %copy-start.1 = (bf16[1,1024,256]{2,1,0:T(8,128)(2,1)S(1)}, bf16[1,1024,256]{2,1,0:T(8,128)(2,1)}, u32[]{:S(2)}) copy-start(bf16[1,1024,256]{2,1,0:T(8,128)(2,1)} %param.8) | copy-start | bytes 1572868
  0.6 14.1 %copy-start.4 = (s32[1,8,4]{1,2,0:T(4,128)S(1)}, s32[1,8,4]{1,2,0:T(4,128)}, u32[]{:S(2)}) copy-start(s32[1,8,4]{1,2,0:T(4,128)} %param.9) | copy-start | bytes 388
  0.7 23.1 %copy-start.3 = (s32[1,2,1024]{2,1,0:T(2,128)S(1)}, s32[1,2,1024]{2,1,0:T(2,128)}, u32[]{:S(2)}) copy-start(s32[1,2,1024]{2,1,0:T(2,128)} %param.12) | copy-start | bytes 24580
  0.7 23.1 %copy-start.2 = (s32[1,2,1024]{2,1,0:T(2,128)S(1)}, s32[1,2,1024]{2,1,0:T(2,128)}, u32[]{:S(2)}) copy-start(s32[1,2,1024]{2,1,0:T(2,128)} %param.11) | copy-start | bytes 24580
  0.7 23.1 %copy-start = (bf16[1,8,4,128,128]{4,3,2,1,0:T(8,128)(2,1)S(1)}, bf16[1,8,4,128,128]{4,3,2,1,0:T(8,128)(2,1)}, u32[]{:S(2)}) copy-start(bf16[1,8,4,128,128]{4,3,2,1,0:T(8,128)(2,1)} %param.10) | copy-start | bytes 3145732
  7.6 14.1 %collective-permute-start.1 = (bf16[1024,256]{1,0:T(8,128)(2,1)S(1)}, bf16[1024,256]{1,0:T(8,128)(2,1)S(1)}, u32[]{:S(2)}, u32[]{:S(2)}) collective-permute-start(bf16[1024,256]{1,0:T(8,128)(2,1)S(1)} %bitcast.11), channel_id=1, source_target_pairs={{0,15},{1,2},{2,1},{3,4},{4,3},{5,6},{6,5},{7,8},{8,7},{9,10},{10,... | collective-permute-start | bytes 1572872 | tf_op jit(solution)/shard_map/ppermute | solution.py:410
  14.7 9.0 %collective-permute-start = (bf16[1024,256]{1,0:T(8,128)(2,1)S(1)}, bf16[1024,256]{1,0:T(8,128)(2,1)S(1)}, u32[]{:S(2)}, u32[]{:S(2)}) collective-permute-start(bf16[1024,256]{1,0:T(8,128)(2,1)S(1)} %bitcast.12), channel_id=1, source_target_pairs={{0,1},{1,0},{2,3},{3,2},{4,5},{5,4},{6,7},{7,6},{8,9},{9,8},{10,11... | collective-permute-start | bytes 1572872 | tf_op jit(solution)/shard_map/ppermute | solution.py:409
  28.0 4.9 %collective-permute-start.2 = (bf16[272,128]{1,0:T(8,128)(2,1)S(1)}, bf16[272,128]{1,0:T(8,128)(2,1)S(1)}, u32[]{:S(2)}, u32[]{:S(2)}) collective-permute-start(bf16[272,128]{1,0:T(8,128)(2,1)S(1)} %get-tuple-element.39), channel_id=1, source_target_pairs={{0,2},{1,3},{2,0},{3,1},{4,6},{5,7},{6,4},{7,5},{8,10},{9,11},{10,... | collective-permute-start | bytes 208904 | tf_op jit(solution)/shard_map/ppermute | solution.py:347
  28.1 5.2 %collective-permute-start.3 = (bf16[272,128]{1,0:T(8,128)(2,1)S(1)}, bf16[272,128]{1,0:T(8,128)(2,1)S(1)}, u32[]{:S(2)}, u32[]{:S(2)}) collective-permute-start(bf16[272,128]{1,0:T(8,128)(2,1)S(1)} %get-tuple-element.40), channel_id=1, source_target_pairs={{0,1},{1,2},{2,3},{3,0},{4,5},{5,6},{6,7},{7,4},{8,9},{9,10},{10,1... | collective-permute-start | bytes 208904 | tf_op jit(solution)/shard_map/ppermute | solution.py:347
  28.2 5.1 %collective-permute-start.4 = (bf16[272,128]{1,0:T(8,128)(2,1)S(1)}, bf16[272,128]{1,0:T(8,128)(2,1)S(1)}, u32[]{:S(2)}, u32[]{:S(2)}) collective-permute-start(bf16[272,128]{1,0:T(8,128)(2,1)S(1)} %get-tuple-element.41), channel_id=1, source_target_pairs={{0,3},{1,0},{2,1},{3,2},{4,7},{5,4},{6,5},{7,6},{8,11},{9,8},{10,9... | collective-permute-start | bytes 208904 | tf_op jit(solution)/shard_map/ppermute | solution.py:347
  33.4 4.8 %collective-permute-start.5 = (bf16[272,128]{1,0:T(8,128)(2,1)S(1)}, bf16[272,128]{1,0:T(8,128)(2,1)S(1)}, u32[]{:S(2)}, u32[]{:S(2)}) collective-permute-start(bf16[272,128]{1,0:T(8,128)(2,1)S(1)} %get-tuple-element.43), channel_id=1, source_target_pairs={{0,8},{1,9},{2,10},{3,11},{4,12},{5,13},{6,14},{7,15},{8,0},{9,1},... | collective-permute-start | bytes 208904 | tf_op jit(solution)/shard_map/ppermute | solution.py:347
  33.9 4.9 %collective-permute-start.6 = (bf16[272,128]{1,0:T(8,128)(2,1)S(1)}, bf16[272,128]{1,0:T(8,128)(2,1)S(1)}, u32[]{:S(2)}, u32[]{:S(2)}) collective-permute-start(bf16[272,128]{1,0:T(8,128)(2,1)S(1)} %get-tuple-element.44), channel_id=1, source_target_pairs={{0,4},{1,5},{2,6},{3,7},{4,8},{5,9},{6,10},{7,11},{8,12},{9,13},{1... | collective-permute-start | bytes 208904 | tf_op jit(solution)/shard_map/ppermute | solution.py:347
  35.9 3.2 %collective-permute-start.7 = (bf16[272,128]{1,0:T(8,128)(2,1)S(1)}, bf16[272,128]{1,0:T(8,128)(2,1)S(1)}, u32[]{:S(2)}, u32[]{:S(2)}) collective-permute-start(bf16[272,128]{1,0:T(8,128)(2,1)S(1)} %get-tuple-element.45), channel_id=1, source_target_pairs={{0,12},{1,13},{2,14},{3,15},{4,0},{5,1},{6,2},{7,3},{8,4},{9,5},{1... | collective-permute-start | bytes 208904 | tf_op jit(solution)/shard_map/ppermute | solution.py:347
  39.1 5.2 %collective-permute-start.8 = (bf16[272,128]{1,0:T(8,128)(2,1)S(1)}, bf16[272,128]{1,0:T(8,128)(2,1)S(1)}, u32[]{:S(2)}, u32[]{:S(2)}) collective-permute-start(bf16[272,128]{1,0:T(8,128)(2,1)S(1)} %get-tuple-element.47), channel_id=1, source_target_pairs={{0,32},{16,48},{32,64},{48,80},{64,96},{80,112},{96,0},{112,16},{1... | collective-permute-start | bytes 208904 | tf_op jit(solution)/shard_map/ppermute | solution.py:347
  40.4 6.4 %collective-permute-start.9 = (bf16[272,128]{1,0:T(8,128)(2,1)S(1)}, bf16[272,128]{1,0:T(8,128)(2,1)S(1)}, u32[]{:S(2)}, u32[]{:S(2)}) collective-permute-start(bf16[272,128]{1,0:T(8,128)(2,1)S(1)} %get-tuple-element.48), channel_id=1, source_target_pairs={{0,64},{16,80},{32,96},{48,112},{64,0},{80,16},{96,32},{112,48},{1... | collective-permute-start | bytes 208904 | tf_op jit(solution)/shard_map/ppermute | solution.py:347
  42.8 3.9 %collective-permute-start.10 = (bf16[272,128]{1,0:T(8,128)(2,1)S(1)}, bf16[272,128]{1,0:T(8,128)(2,1)S(1)}, u32[]{:S(2)}, u32[]{:S(2)}) collective-permute-start(bf16[272,128]{1,0:T(8,128)(2,1)S(1)} %get-tuple-element.49), channel_id=1, source_target_pairs={{0,96},{16,112},{32,0},{48,16},{64,32},{80,48},{96,64},{112,80},{1... | collective-permute-start | bytes 208904 | tf_op jit(solution)/shard_map/ppermute | solution.py:347
  46.8 2.3 %collective-permute-start.11 = (bf16[4,272,128]{2,1,0:T(8,128)(2,1)S(1)}, bf16[4,272,128]{2,1,0:T(8,128)(2,1)S(1)}, u32[]{:S(2)}, u32[]{:S(2)}) collective-permute-start(bf16[4,272,128]{2,1,0:T(8,128)(2,1)S(1)} %pad_maximum_fusion.along), channel_id=1, source_target_pairs={{0,16},{16,0},{32,48},{48,32},{64,80},{80,64},{96,112},{112,96},{1... | collective-permute-start | bytes 835592 | tf_op jit(solution)/shard_map/ppermute | solution.py:454

commit v6 on v5

--- a/solution.py
+++ b/solution.py
@@ -48,9 +48,9 @@
     ]
     for copy in copies:
         copy.start()
-    for copy in copies[:5]:
-        copy.wait()
+    copies[0].wait()
     for k in range(4):
+        copies[1 + k].wait()
         mats_high[k], mats_low[k] = split(mats[k])
     for copy in copies[5:]:
         copy.wait()
@@ -61,7 +61,7 @@
         return dot3((mats_high[k], mats_low[k]), parts)
 
     parts = split(weight)
-    r = sigmoid(dot(mats_high[1], parts[0]) + bias[1])
+    r = sigmoid(gate(1, parts) + bias[1])
     mixed = r * weight
     mixed_parts = split(mixed)
     c_in = gate(2, parts)
@@ -74,7 +74,7 @@
 
 def write_score_matrix(low, score_matrix):
     own = low[lax.axis_index("snap")]
-    score_matrix[...] = dot(own, own, LANES).astype(BF16)
+    score_matrix[0], score_matrix[1] = split(dot(own, own, LANES))
 
 
 def early_kernel(start_hbm, mats_hbm, bias_hbm, before, score_matrix, low, *scratch):
@@ -205,16 +205,18 @@
 
     half = jnp.zeros((width, width), F32)
     for sign in (0, 1):
-        first = picked[pl.ds(2 * sign * edges, edges), :]
-        second = picked[pl.ds((2 * sign + 1) * edges, edges), :]
-        score = jnp.sum(dot(first, score_matrix[...]) * second.astype(F32), axis=1, keepdims=True)
-        score = score * (1.0 / width)
-        if sign == 0:
-            slope = sigmoid(-score) * (-factor)
-        else:
-            slope = sigmoid(score) * factor
-        scaled = (slope * first.astype(F32)).astype(BF16)
-        half = half + dot(scaled, second, ROWS)
+        for c in range(edges // chunk):
+            first = picked[pl.ds(2 * sign * edges + c * chunk, chunk), :]
+            second = picked[pl.ds((2 * sign + 1) * edges + c * chunk, chunk), :]
+            ends = dot(first, score_matrix[0]) + dot(first, score_matrix[1])
+            ends = ends * second.astype(F32)
+            score = jnp.sum(ends, axis=1, keepdims=True) * (1.0 / width)
+            if sign == 0:
+                slope = sigmoid(-score) * (-factor)
+            else:
+                slope = sigmoid(score) * factor
+            scaled = (slope * first.astype(F32)).astype(BF16)
+            half = half + dot(scaled, second, ROWS)
     full = half + half.T
     quarter = width // 2
     upper = full[:quarter, :quarter]
@@ -299,18 +301,19 @@
         d2 = g * proposal_slope[t]
         d2_parts = split(d2)
         mixed = gate(3, d2_parts)
+        two = gate(2, d2_parts)
         d0 = g * gate_slope[t]
         d0_high = d0.astype(BF16)
-        fresh = g * keep[t] + (gate_once(0, d0_high) + gate(2, d2_parts))
-        d1 = mixed * reset_slope[t]
-        d1_high = d1.astype(BF16)
-        fresh = fresh + mixed * reset[t] + gate_once(1, d1_high)
         lanes = pl.ds(pl.multiple_of(t * width, width), width)
         before = weights_wide[:, lanes]
         grads[0] += dot(d0_high, before, LANES)
-        grads[1] += dot(d1_high, before, LANES)
         grads[2] += dot(d2_parts[0], before, LANES)
         grads[3] += dot(d2_parts[0], reset_wide[:, lanes], LANES)
+        d1 = mixed * reset_slope[t]
+        d1_high = d1.astype(BF16)
+        fresh = g * keep[t] + gate_once(0, d0_high) + two
+        fresh = fresh + mixed * reset[t] + gate_once(1, d1_high)
+        grads[1] += dot(d1_high, before, LANES)
         grads[4] += d0
         grads[5] += d1
         grads[6] += d2
@@ -393,7 +396,7 @@
         pltpu.SemaphoreType.DMA((8,)),
     ]
     wide = jax.ShapeDtypeStruct(square, F32)
-    flat = jax.ShapeDtypeStruct((width, width), BF16)
+    flat = jax.ShapeDtypeStruct((2, width, width), BF16)
     before, early_score_matrix = pl.pallas_call(
         early_kernel,
         out_shape=[jax.ShapeDtypeStruct(((snap_count - 1) // STRIDE, width, width), F32), flat],

time: 55.9 us -> 54.9 us (0.982)
  waiting for transfers between devices: 12 us -> 10.6 us
  Pallas kernels: 23.7 us -> 24.7 us
  starting transfers between devices: 19.2 us -> 18.5 us
    ppermute x1, waiting for transfers between devices: 1.52 us -> 0.42 us  [body(): odd_side = lax.ppermute(sent, 'node', odd_pairs)]
    pallas_call x1, Pallas kernels: 5.41 us -> 6.06 us  [body(): pl.pallas_call(late_kernel, out_shape=outs, in_specs=[HBM] * 3 + [VMEM] *...]
    ppermute x1, starting transfers between devices: 1.11 us -> 0.47 us  [body(): other = lax.ppermute(along, 'snap', [(i, i ^ 1) for i in range(snap_count)])]
    pallas_call x1, Pallas kernels: 6.91 us -> 7.48 us  [body(): pl.pallas_call(early_kernel, out_shape=[jax.ShapeDtypeStruct(((snap_count...]
  transfers between devices with their start and end apart: 12 -> 12, of which waited for: 10 -> 10; matrix products, arithmetic and copies ran while one was open for 0% -> 0% of each run, Pallas kernels for 10% -> 12%
where the time goes in v6:
time: 54.9 us; the launch traced here: 54.7 us
  Pallas kernels  24.7 us (45%)
  starting transfers between devices  18.5 us (34%)
  waiting for transfers between devices  10.6 us (19%)
  between operations  0.75 us (1%)
    ppermute x9, starting transfers between devices, ring_parts(): parts.append(lax.ppermute(copies[turn], axis, route))  11 us
    pallas_call x1, Pallas kernels, body(): pl.pallas_call(early_kernel, out_shape=[jax.ShapeDtypeStruct(((snap_count...  7.48 us
    ppermute x9, waiting for transfers between devices, ring_parts(): parts.append(lax.ppermute(copies[turn], axis, route))  7.45 us
    ppermute x1, starting transfers between devices, body(): odd_side = lax.ppermute(sent, 'node', odd_pairs)  7.11 us
    pallas_call x1, Pallas kernels, body(): pl.pallas_call(backward_kernel, out_shape=[jax.ShapeDtypeStruct((share, w...  6.51 us
    pallas_call x1, Pallas kernels, body(): pl.pallas_call(late_kernel, out_shape=outs, in_specs=[HBM] * 3 + [VMEM] *...  6.06 us
    pallas_call x1, Pallas kernels, body(): pl.pallas_call(functools.partial(edge_kernel, factor), out_shape=[jax.Sha...  4.18 us
    ppermute x1, waiting for transfers between devices, body(): even_side = lax.ppermute(sent, 'node', even_pairs)  1.91 us
  transfers between devices with their start and end apart: 12, of which 10 were waited for; matrix products, arithmetic and copies ran while one was open for 0% of the time, Pallas kernels for 12%

profile of v6, /device:TPU:1, one launch (start us, length us, event | category | flops | bytes accessed | tf_op | source)
XLA Modules:
  0.0 54.7 jit_solution(15567645414683944841)
XLA Ops:
  0.6 0.0 copy-start.1
  0.6 0.0 copy-start.4
  0.7 0.0 copy-start.3
  0.7 0.0 copy-start.2
  0.7 0.0 copy-start
  0.7 7.5 %forward_early.1 = (f32[2,256,256]{2,1,0:T(8,128)S(1)}, bf16[2,256,256]{2,1,0:T(8,128)(2,1)S(1)}) custom-call(f32[256,256]{1,0:T(8,128)} %start_hbm.3, f32[4,256,256]{2,1,0:T(8,128)} %mats_hbm.3, f32[3,256,256]{2,1,0:T(8,128)} %bias_hbm.3), custom_call_target="tpu_custom_call" | custom-call | tf_op jit(solution)/shard_map/forward_early/pallas_call | solution.py:400
  8.2 0.0 copy-done.1
  8.2 7.1 %collective-permute-start.1 = (bf16[1024,256]{1,0:T(8,128)(2,1)S(1)}, bf16[1024,256]{1,0:T(8,128)(2,1)S(1)}, u32[]{:S(2)}, u32[]{:S(2)}) collective-permute-start(bf16[1024,256]{1,0:T(8,128)(2,1)S(1)} %bitcast.11), channel_id=1, source_target_pairs={{0,15},{1,2},{2,1},{3,4},{4,3},{5,6},{6,5},{7,8},{8,7},{9,10},{10,... | collective-permute-start | bytes 1572872 | tf_op jit(solution)/shard_map/ppermute | solution.py:413
  15.3 0.0 collective-permute-start
  15.3 0.0 copy-done.4
  15.3 0.1 copy.11.ids
  15.4 6.1 %forward_late.1 = (f32[8,256,256]{2,1,0:T(8,128)S(1)}, f32[8,256,256]{2,1,0:T(8,128)S(1)}, f32[8,256,256]{2,1,0:T(8,128)S(1)}, f32[8,256,256]{2,1,0:T(8,128)S(1)...) custom-call(f32[256,256]{1,0:T(8,128)} %start_hbm.3, ...), custom_call_target="tpu_custom_call" | custom-call | tf_op jit(solution)/shard_map/forward_late/pallas_call | solution.py:418
  21.4 0.4 collective-permute-done.1.odd_side
  21.9 1.9 %collective-permute-done.even_side = bf16[1024,256]{1,0:T(8,128)(2,1)S(1)} collective-permute-done((bf16[1024,256]{1,0:T(8,128)(2,1)S(1)}, bf16[1024,256]{1,0:T(8,128)(2,1)S(1)}, u32[]{:S(2)}, u32[]{:S(2)}) %collective-permute-start) | collective-permute-done | bytes 524320 | tf_op jit(solution)/shard_map/ppermute | solution.py:412
  23.8 0.0 copy-done.3
  23.8 0.0 copy-done.2
  23.8 0.0 copy-done
  23.8 4.2 %edge_products.1 = (bf16[272,128]{1,0:T(8,128)(2,1)S(1)}, bf16[272,128]{1,0:T(8,128)(2,1)S(1)}, bf16[272,128]{1,0:T(8,128)(2,1)S(1)}, bf16[272,128]{1,0:T(8,128)(2,1)S(1)}) custom-call(s32[8,4]{1,0:T(8,128)S(1)} %copy.11.ids, bf16[1024,256]{1,0:T(8,128)(2,1)S(1)} %bitcast.13, bf16[1024,256]{1,0:T(8,128)(2,1)S(1)} %collective-permute-done.even_side, ...), custom_call_target="tpu_custom_call" | custom-call | tf_op jit(solution)/shard_map/edge_products/pallas_call | solution.py:430
  28.0 0.1 collective-permute-start.2
  28.1 0.1 collective-permute-start.3
  28.1 2.7 %collective-permute-start.4 = (bf16[272,128]{1,0:T(8,128)(2,1)S(1)}, bf16[272,128]{1,0:T(8,128)(2,1)S(1)}, u32[]{:S(2)}, u32[]{:S(2)}) collective-permute-start(bf16[272,128]{1,0:T(8,128)(2,1)S(1)} %get-tuple-element.41), channel_id=1, source_target_pairs={{0,3},{1,0},{2,1},{3,2},{4,7},{5,4},{6,5},{7,6},{8,11},{9,8},{10,9... | collective-permute-start | bytes 208904 | tf_op jit(solution)/shard_map/ppermute | solution.py:350
  30.8 2.0 %collective-permute-done.2.first = bf16[272,128]{1,0:T(8,128)(2,1)S(1)} collective-permute-done((bf16[272,128]{1,0:T(8,128)(2,1)S(1)}, bf16[272,128]{1,0:T(8,128)(2,1)S(1)}, u32[]{:S(2)}, u32[]{:S(2)}) %collective-permute-start.2) | collective-permute-done | bytes 69664 | tf_op jit(solution)/shard_map/ppermute | solution.py:350
  32.8 0.4 collective-permute-done.3.second
  33.3 0.0 collective-permute-done.4.third
  33.3 0.6 %collective-permute-start.5 = (bf16[272,128]{1,0:T(8,128)(2,1)S(1)}, bf16[272,128]{1,0:T(8,128)(2,1)S(1)}, u32[]{:S(2)}, u32[]{:S(2)}) collective-permute-start(bf16[272,128]{1,0:T(8,128)(2,1)S(1)} %get-tuple-element.43), channel_id=1, source_target_pairs={{0,8},{1,9},{2,10},{3,11},{4,12},{5,13},{6,14},{7,15},{8,0},{9,1},... | collective-permute-start | bytes 208904 | tf_op jit(solution)/shard_map/ppermute | solution.py:350
  33.9 2.0 %collective-permute-start.6 = (bf16[272,128]{1,0:T(8,128)(2,1)S(1)}, bf16[272,128]{1,0:T(8,128)(2,1)S(1)}, u32[]{:S(2)}, u32[]{:S(2)}) collective-permute-start(bf16[272,128]{1,0:T(8,128)(2,1)S(1)} %get-tuple-element.44), channel_id=1, source_target_pairs={{0,4},{1,5},{2,6},{3,7},{4,8},{5,9},{6,10},{7,11},{8,12},{9,13},{1... | collective-permute-start | bytes 208904 | tf_op jit(solution)/shard_map/ppermute | solution.py:350
  35.8 0.7 %collective-permute-start.7 = (bf16[272,128]{1,0:T(8,128)(2,1)S(1)}, bf16[272,128]{1,0:T(8,128)(2,1)S(1)}, u32[]{:S(2)}, u32[]{:S(2)}) collective-permute-start(bf16[272,128]{1,0:T(8,128)(2,1)S(1)} %get-tuple-element.45), channel_id=1, source_target_pairs={{0,12},{1,13},{2,14},{3,15},{4,0},{5,1},{6,2},{7,3},{8,4},{9,5},{1... | collective-permute-start | bytes 208904 | tf_op jit(solution)/shard_map/ppermute | solution.py:350
  36.6 1.5 %collective-permute-done.5.first = bf16[272,128]{1,0:T(8,128)(2,1)S(1)} collective-permute-done((bf16[272,128]{1,0:T(8,128)(2,1)S(1)}, bf16[272,128]{1,0:T(8,128)(2,1)S(1)}, u32[]{:S(2)}, u32[]{:S(2)}) %collective-permute-start.5) | collective-permute-done | bytes 69664 | tf_op jit(solution)/shard_map/ppermute | solution.py:350
  38.1 0.7 %collective-permute-done.6.second = bf16[272,128]{1,0:T(8,128)(2,1)S(1)} collective-permute-done((bf16[272,128]{1,0:T(8,128)(2,1)S(1)}, bf16[272,128]{1,0:T(8,128)(2,1)S(1)}, u32[]{:S(2)}, u32[]{:S(2)}) %collective-permute-start.6) | collective-permute-done | bytes 69664 | tf_op jit(solution)/shard_map/ppermute | solution.py:350
  38.8 0.2 collective-permute-done.7.third
  39.0 1.3 %collective-permute-start.8 = (bf16[272,128]{1,0:T(8,128)(2,1)S(1)}, bf16[272,128]{1,0:T(8,128)(2,1)S(1)}, u32[]{:S(2)}, u32[]{:S(2)}) collective-permute-start(bf16[272,128]{1,0:T(8,128)(2,1)S(1)} %get-tuple-element.47), channel_id=1, source_target_pairs={{0,32},{16,48},{32,64},{48,80},{64,96},{80,112},{96,0},{112,16},{1... | collective-permute-start | bytes 208904 | tf_op jit(solution)/shard_map/ppermute | solution.py:350
  40.3 2.5 %collective-permute-start.9 = (bf16[272,128]{1,0:T(8,128)(2,1)S(1)}, bf16[272,128]{1,0:T(8,128)(2,1)S(1)}, u32[]{:S(2)}, u32[]{:S(2)}) collective-permute-start(bf16[272,128]{1,0:T(8,128)(2,1)S(1)} %get-tuple-element.48), channel_id=1, source_target_pairs={{0,64},{16,80},{32,96},{48,112},{64,0},{80,16},{96,32},{112,48},{1... | collective-permute-start | bytes 208904 | tf_op jit(solution)/shard_map/ppermute | solution.py:350
  42.8 1.1 %collective-permute-start.10 = (bf16[272,128]{1,0:T(8,128)(2,1)S(1)}, bf16[272,128]{1,0:T(8,128)(2,1)S(1)}, u32[]{:S(2)}, u32[]{:S(2)}) collective-permute-start(bf16[272,128]{1,0:T(8,128)(2,1)S(1)} %get-tuple-element.49), channel_id=1, source_target_pairs={{0,96},{16,112},{32,0},{48,16},{64,32},{80,48},{96,64},{112,80},{1... | collective-permute-start | bytes 208904 | tf_op jit(solution)/shard_map/ppermute | solution.py:350
  43.9 0.0 collective-permute-done.8
  43.9 2.0 %collective-permute-done.9 = bf16[272,128]{1,0:T(8,128)(2,1)S(1)} collective-permute-done((bf16[272,128]{1,0:T(8,128)(2,1)S(1)}, bf16[272,128]{1,0:T(8,128)(2,1)S(1)}, u32[]{:S(2)}, u32[]{:S(2)}) %collective-permute-start.9) | collective-permute-done | bytes 69664 | tf_op jit(solution)/shard_map/ppermute | solution.py:350
  45.9 0.5 collective-permute-done.10
  46.5 0.5 collective-permute-start.11
  47.0 0.4 local_gradients.1.mine
  47.4 0.8 %collective-permute-done.11.other = bf16[4,272,128]{2,1,0:T(8,128)(2,1)S(1)} collective-permute-done((bf16[4,272,128]{2,1,0:T(8,128)(2,1)S(1)}, bf16[4,272,128]{2,1,0:T(8,128)(2,1)S(1)}, u32[]{:S(2)}, u32[]{:S(2)}) %collective-permute-start.11) | collective-permute-done | bytes 278560 | tf_op jit(solution)/shard_map/ppermute | solution.py:457
  48.2 6.5 %backward_chain.1 = (f32[16,256]{1,0:T(8,128)}, f32[7,256,256]{2,1,0:T(8,128)}, f32[256,256]{1,0:T(8,128)}) custom-call(f32[4,256,256]{2,1,0:T(8,128)S(1)} %local_gradients.1.mine, bf16[4,272,128]{2,1,0:T(8,128)(2,1)S(1)} %collective-permute-done.11.other, f32[8,256,256]{2,1,0:T(8,128)S(1)} %get-tuple-element.51.keep, ...), custom_call_target="tpu_custom_call" | custom-call | tf_op jit(solution)/shard_map/backward_chain/pallas_call | solution.py:470
  (3 shorter events, 0.1 us)
Async XLA Ops:
  0.6 7.5 %copy-start.1 = (bf16[1,1024,256]{2,1,0:T(8,128)(2,1)S(1)}, bf16[1,1024,256]{2,1,0:T(8,128)(2,1)}, u32[]{:S(2)}) copy-start(bf16[1,1024,256]{2,1,0:T(8,128)(2,1)} %param.8) | copy-start | bytes 1572868
  0.6 14.7 %copy-start.4 = (s32[1,8,4]{1,2,0:T(4,128)S(1)}, s32[1,8,4]{1,2,0:T(4,128)}, u32[]{:S(2)}) copy-start(s32[1,8,4]{1,2,0:T(4,128)} %param.9) | copy-start | bytes 388
  0.7 23.1 %copy-start.3 = (s32[1,2,1024]{2,1,0:T(2,128)S(1)}, s32[1,2,1024]{2,1,0:T(2,128)}, u32[]{:S(2)}) copy-start(s32[1,2,1024]{2,1,0:T(2,128)} %param.12) | copy-start | bytes 24580
  0.7 23.1 %copy-start.2 = (s32[1,2,1024]{2,1,0:T(2,128)S(1)}, s32[1,2,1024]{2,1,0:T(2,128)}, u32[]{:S(2)}) copy-start(s32[1,2,1024]{2,1,0:T(2,128)} %param.11) | copy-start | bytes 24580
  0.7 23.1 %copy-start = (bf16[1,8,4,128,128]{4,3,2,1,0:T(8,128)(2,1)S(1)}, bf16[1,8,4,128,128]{4,3,2,1,0:T(8,128)(2,1)}, u32[]{:S(2)}) copy-start(bf16[1,8,4,128,128]{4,3,2,1,0:T(8,128)(2,1)} %param.10) | copy-start | bytes 3145732
  8.2 13.7 %collective-permute-start.1 = (bf16[1024,256]{1,0:T(8,128)(2,1)S(1)}, bf16[1024,256]{1,0:T(8,128)(2,1)S(1)}, u32[]{:S(2)}, u32[]{:S(2)}) collective-permute-start(bf16[1024,256]{1,0:T(8,128)(2,1)S(1)} %bitcast.11), channel_id=1, source_target_pairs={{0,15},{1,2},{2,1},{3,4},{4,3},{5,6},{6,5},{7,8},{8,7},{9,10},{10,... | collective-permute-start | bytes 1572872 | tf_op jit(solution)/shard_map/ppermute | solution.py:413
  15.3 8.5 %collective-permute-start = (bf16[1024,256]{1,0:T(8,128)(2,1)S(1)}, bf16[1024,256]{1,0:T(8,128)(2,1)S(1)}, u32[]{:S(2)}, u32[]{:S(2)}) collective-permute-start(bf16[1024,256]{1,0:T(8,128)(2,1)S(1)} %bitcast.12), channel_id=1, source_target_pairs={{0,1},{1,0},{2,3},{3,2},{4,5},{5,4},{6,7},{7,6},{8,9},{9,8},{10,11... | collective-permute-start | bytes 1572872 | tf_op jit(solution)/shard_map/ppermute | solution.py:412
  28.0 4.9 %collective-permute-start.2 = (bf16[272,128]{1,0:T(8,128)(2,1)S(1)}, bf16[272,128]{1,0:T(8,128)(2,1)S(1)}, u32[]{:S(2)}, u32[]{:S(2)}) collective-permute-start(bf16[272,128]{1,0:T(8,128)(2,1)S(1)} %get-tuple-element.39), channel_id=1, source_target_pairs={{0,2},{1,3},{2,0},{3,1},{4,6},{5,7},{6,4},{7,5},{8,10},{9,11},{10,... | collective-permute-start | bytes 208904 | tf_op jit(solution)/shard_map/ppermute | solution.py:350
  28.1 5.2 %collective-permute-start.3 = (bf16[272,128]{1,0:T(8,128)(2,1)S(1)}, bf16[272,128]{1,0:T(8,128)(2,1)S(1)}, u32[]{:S(2)}, u32[]{:S(2)}) collective-permute-start(bf16[272,128]{1,0:T(8,128)(2,1)S(1)} %get-tuple-element.40), channel_id=1, source_target_pairs={{0,1},{1,2},{2,3},{3,0},{4,5},{5,6},{6,7},{7,4},{8,9},{9,10},{10,1... | collective-permute-start | bytes 208904 | tf_op jit(solution)/shard_map/ppermute | solution.py:350
  28.1 5.1 %collective-permute-start.4 = (bf16[272,128]{1,0:T(8,128)(2,1)S(1)}, bf16[272,128]{1,0:T(8,128)(2,1)S(1)}, u32[]{:S(2)}, u32[]{:S(2)}) collective-permute-start(bf16[272,128]{1,0:T(8,128)(2,1)S(1)} %get-tuple-element.41), channel_id=1, source_target_pairs={{0,3},{1,0},{2,1},{3,2},{4,7},{5,4},{6,5},{7,6},{8,11},{9,8},{10,9... | collective-permute-start | bytes 208904 | tf_op jit(solution)/shard_map/ppermute | solution.py:350
  33.3 4.8 %collective-permute-start.5 = (bf16[272,128]{1,0:T(8,128)(2,1)S(1)}, bf16[272,128]{1,0:T(8,128)(2,1)S(1)}, u32[]{:S(2)}, u32[]{:S(2)}) collective-permute-start(bf16[272,128]{1,0:T(8,128)(2,1)S(1)} %get-tuple-element.43), channel_id=1, source_target_pairs={{0,8},{1,9},{2,10},{3,11},{4,12},{5,13},{6,14},{7,15},{8,0},{9,1},... | collective-permute-start | bytes 208904 | tf_op jit(solution)/shard_map/ppermute | solution.py:350
  33.9 4.9 %collective-permute-start.6 = (bf16[272,128]{1,0:T(8,128)(2,1)S(1)}, bf16[272,128]{1,0:T(8,128)(2,1)S(1)}, u32[]{:S(2)}, u32[]{:S(2)}) collective-permute-start(bf16[272,128]{1,0:T(8,128)(2,1)S(1)} %get-tuple-element.44), channel_id=1, source_target_pairs={{0,4},{1,5},{2,6},{3,7},{4,8},{5,9},{6,10},{7,11},{8,12},{9,13},{1... | collective-permute-start | bytes 208904 | tf_op jit(solution)/shard_map/ppermute | solution.py:350
  35.8 3.2 %collective-permute-start.7 = (bf16[272,128]{1,0:T(8,128)(2,1)S(1)}, bf16[272,128]{1,0:T(8,128)(2,1)S(1)}, u32[]{:S(2)}, u32[]{:S(2)}) collective-permute-start(bf16[272,128]{1,0:T(8,128)(2,1)S(1)} %get-tuple-element.45), channel_id=1, source_target_pairs={{0,12},{1,13},{2,14},{3,15},{4,0},{5,1},{6,2},{7,3},{8,4},{9,5},{1... | collective-permute-start | bytes 208904 | tf_op jit(solution)/shard_map/ppermute | solution.py:350
  39.0 4.9 %collective-permute-start.8 = (bf16[272,128]{1,0:T(8,128)(2,1)S(1)}, bf16[272,128]{1,0:T(8,128)(2,1)S(1)}, u32[]{:S(2)}, u32[]{:S(2)}) collective-permute-start(bf16[272,128]{1,0:T(8,128)(2,1)S(1)} %get-tuple-element.47), channel_id=1, source_target_pairs={{0,32},{16,48},{32,64},{48,80},{64,96},{80,112},{96,0},{112,16},{1... | collective-permute-start | bytes 208904 | tf_op jit(solution)/shard_map/ppermute | solution.py:350
  40.3 5.6 %collective-permute-start.9 = (bf16[272,128]{1,0:T(8,128)(2,1)S(1)}, bf16[272,128]{1,0:T(8,128)(2,1)S(1)}, u32[]{:S(2)}, u32[]{:S(2)}) collective-permute-start(bf16[272,128]{1,0:T(8,128)(2,1)S(1)} %get-tuple-element.48), channel_id=1, source_target_pairs={{0,64},{16,80},{32,96},{48,112},{64,0},{80,16},{96,32},{112,48},{1... | collective-permute-start | bytes 208904 | tf_op jit(solution)/shard_map/ppermute | solution.py:350
  42.8 3.7 %collective-permute-start.10 = (bf16[272,128]{1,0:T(8,128)(2,1)S(1)}, bf16[272,128]{1,0:T(8,128)(2,1)S(1)}, u32[]{:S(2)}, u32[]{:S(2)}) collective-permute-start(bf16[272,128]{1,0:T(8,128)(2,1)S(1)} %get-tuple-element.49), channel_id=1, source_target_pairs={{0,96},{16,112},{32,0},{48,16},{64,32},{80,48},{96,64},{112,80},{1... | collective-permute-start | bytes 208904 | tf_op jit(solution)/shard_map/ppermute | solution.py:350
  46.5 1.7 %collective-permute-start.11 = (bf16[4,272,128]{2,1,0:T(8,128)(2,1)S(1)}, bf16[4,272,128]{2,1,0:T(8,128)(2,1)S(1)}, u32[]{:S(2)}, u32[]{:S(2)}) collective-permute-start(bf16[4,272,128]{2,1,0:T(8,128)(2,1)S(1)} %pad_maximum_fusion.along), channel_id=1, source_target_pairs={{0,16},{16,0},{32,48},{48,32},{64,80},{80,64},{96,112},{112,96},{1... | collective-permute-start | bytes 835592 | tf_op jit(solution)/shard_map/ppermute | solution.py:457

commit v7 on v6

--- a/solution.py
+++ b/solution.py
@@ -46,18 +46,23 @@
     copies += [
         pltpu.make_async_copy(bias_hbm.at[k], bias.at[k], sems.at[5 + k]) for k in range(3)
     ]
-    for copy in copies:
-        copy.start()
+    for k in (0, 2, 6, 3, 4, 1, 5, 7):
+        copies[k].start()
     copies[0].wait()
-    for k in range(4):
+
+    def arrive(k):
         copies[1 + k].wait()
         mats_high[k], mats_low[k] = split(mats[k])
-    for copy in copies[5:]:
-        copy.wait()
-
-
-def gate_step(weight, bias, mats_high, mats_low):
+        if k < 3:
+            copies[5 + k].wait()
+
+    return arrive
+
+
+def gate_step(weight, bias, mats_high, mats_low, arrive):
     def gate(k, parts):
+        if arrive is not None:
+            arrive(k)
         return dot3((mats_high[k], mats_low[k]), parts)
 
     parts = split(weight)
@@ -82,12 +87,12 @@
 
     @pl.when(lax.rem(lax.axis_index("snap"), 2) == 1)
     def _():
-        load_gates(start_hbm, mats_hbm, bias_hbm, *scratch)
+        arrive = load_gates(start_hbm, mats_hbm, bias_hbm, *scratch)
         weight = start[...]
         for t in range(low.shape[0]):
             if t > 0 and t % STRIDE == 0:
                 before[t // STRIDE - 1] = weight
-            weight = gate_step(weight, bias, mats_high, mats_low)[-1]
+            weight = gate_step(weight, bias, mats_high, mats_low, arrive if t == 0 else None)[-1]
             low[t] = weight.astype(BF16)
         write_score_matrix(low, score_matrix)
 
@@ -114,10 +119,10 @@
     start, mats, bias, mats_high, mats_low, sems = scratch
     steps, width = low.shape[0], low.shape[1]
     odd = lax.rem(lax.axis_index("snap"), 2) == 1
-    load_gates(start_hbm, mats_hbm, bias_hbm, *scratch)
-
-    def record(t, weight):
-        u, r, c, mixed, fresh = gate_step(weight, bias, mats_high, mats_low)
+
+    def record(t, weight, arrive):
+        first = arrive if t == 0 else None
+        u, r, c, mixed, fresh = gate_step(weight, bias, mats_high, mats_low, first)
         keep[t] = 1.0 - u
         reset[t] = r
         gate_slope[t] = (c - weight) * (u * (1.0 - u))
@@ -131,18 +136,20 @@
 
     @pl.when(odd)
     def _():
+        arrive = load_gates(start_hbm, mats_hbm, bias_hbm, *scratch)
         weights = [start[...]] + [before[k] for k in range(before.shape[0])]
         for s in range(STRIDE):
             for k in range(len(weights)):
                 if k * STRIDE + s < steps:
-                    weights[k] = record(k * STRIDE + s, weights[k])
+                    weights[k] = record(k * STRIDE + s, weights[k], arrive)
         score_matrix[...] = early_score_matrix[...]
 
     @pl.when(jnp.logical_not(odd))
     def _():
+        arrive = load_gates(start_hbm, mats_hbm, bias_hbm, *scratch)
         weight = start[...]
         for t in range(steps):
-            weight = record(t, weight)
+            weight = record(t, weight, arrive)
         write_score_matrix(low, score_matrix)
 
     for k in range(4):

time: 54.9 us -> 54.5 us (level)
  waiting for transfers between devices: 10.6 us -> 9.58 us
  Pallas kernels: 24.7 us -> 25.5 us
  transfers between devices with their start and end apart: 12 -> 12, of which waited for: 10 -> 10; matrix products, arithmetic and copies ran while one was open for 0% -> 0% of each run, Pallas kernels for 12% -> 13%
where the time goes in v7:
time: 54.5 us; the launch traced here: 54.4 us
  Pallas kernels  25.5 us (47%)
  starting transfers between devices  18.4 us (34%)
  waiting for transfers between devices  9.58 us (18%)
  between operations  0.76 us (1%)
    ppermute x9, starting transfers between devices, ring_parts(): parts.append(lax.ppermute(copies[turn], axis, route))  11.1 us
    pallas_call x1, Pallas kernels, body(): pl.pallas_call(early_kernel, out_shape=[jax.ShapeDtypeStruct(((snap_count...  7.82 us
    ppermute x1, starting transfers between devices, body(): odd_side = lax.ppermute(sent, 'node', odd_pairs)  7.11 us
    ppermute x9, waiting for transfers between devices, ring_parts(): parts.append(lax.ppermute(copies[turn], axis, route))  6.96 us
    pallas_call x1, Pallas kernels, body(): pl.pallas_call(late_kernel, out_shape=outs, in_specs=[HBM] * 3 + [VMEM] *...  6.54 us
    pallas_call x1, Pallas kernels, body(): pl.pallas_call(backward_kernel, out_shape=[jax.ShapeDtypeStruct((share, w...  6.52 us
    pallas_call x1, Pallas kernels, body(): pl.pallas_call(functools.partial(edge_kernel, factor), out_shape=[jax.Sha...  4.18 us
    ppermute x1, waiting for transfers between devices, body(): even_side = lax.ppermute(sent, 'node', even_pairs)  1.5 us
  transfers between devices with their start and end apart: 12, of which 10 were waited for; matrix products, arithmetic and copies ran while one was open for 0% of the time, Pallas kernels for 13%

profile of v7, /device:TPU:1, one launch (start us, length us, event | category | flops | bytes accessed | tf_op | source)
XLA Modules:
  0.0 54.4 jit_solution(6213706947460242445)
XLA Ops:
  0.6 0.0 copy-start.1
  0.6 0.0 copy-start.4
  0.7 0.0 copy-start.3
  0.7 0.0 copy-start.2
  0.7 0.0 copy-start
  0.7 7.8 %forward_early.1 = (f32[2,256,256]{2,1,0:T(8,128)S(1)}, bf16[2,256,256]{2,1,0:T(8,128)(2,1)S(1)}) custom-call(f32[256,256]{1,0:T(8,128)} %start_hbm.3, f32[4,256,256]{2,1,0:T(8,128)} %mats_hbm.3, f32[3,256,256]{2,1,0:T(8,128)} %bias_hbm.3), custom_call_target="tpu_custom_call" | custom-call | tf_op jit(solution)/shard_map/forward_early/pallas_call | solution.py:407
  8.5 0.0 copy-done.1
  8.5 7.1 %collective-permute-start.1 = (bf16[1024,256]{1,0:T(8,128)(2,1)S(1)}, bf16[1024,256]{1,0:T(8,128)(2,1)S(1)}, u32[]{:S(2)}, u32[]{:S(2)}) collective-permute-start(bf16[1024,256]{1,0:T(8,128)(2,1)S(1)} %bitcast.11), channel_id=1, source_target_pairs={{0,15},{1,2},{2,1},{3,4},{4,3},{5,6},{6,5},{7,8},{8,7},{9,10},{10,... | collective-permute-start | bytes 1572872 | tf_op jit(solution)/shard_map/ppermute | solution.py:420
  15.6 0.0 collective-permute-start
  15.6 0.0 copy-done.4
  15.6 0.1 copy.11.ids
  15.7 6.5 %forward_late.1 = (f32[8,256,256]{2,1,0:T(8,128)S(1)}, f32[8,256,256]{2,1,0:T(8,128)S(1)}, f32[8,256,256]{2,1,0:T(8,128)S(1)}, f32[8,256,256]{2,1,0:T(8,128)S(1)...) custom-call(f32[256,256]{1,0:T(8,128)} %start_hbm.3, ...), custom_call_target="tpu_custom_call" | custom-call | tf_op jit(solution)/shard_map/forward_late/pallas_call | solution.py:425
  22.3 0.0 collective-permute-done.1.odd_side
  22.3 1.5 %collective-permute-done.even_side = bf16[1024,256]{1,0:T(8,128)(2,1)S(1)} collective-permute-done((bf16[1024,256]{1,0:T(8,128)(2,1)S(1)}, bf16[1024,256]{1,0:T(8,128)(2,1)S(1)}, u32[]{:S(2)}, u32[]{:S(2)}) %collective-permute-start) | collective-permute-done | bytes 524320 | tf_op jit(solution)/shard_map/ppermute | solution.py:419
  23.8 0.0 copy-done.3
  23.8 0.0 copy-done.2
  23.8 0.0 copy-done
  23.8 4.2 %edge_products.1 = (bf16[272,128]{1,0:T(8,128)(2,1)S(1)}, bf16[272,128]{1,0:T(8,128)(2,1)S(1)}, bf16[272,128]{1,0:T(8,128)(2,1)S(1)}, bf16[272,128]{1,0:T(8,128)(2,1)S(1)}) custom-call(s32[8,4]{1,0:T(8,128)S(1)} %copy.11.ids, bf16[1024,256]{1,0:T(8,128)(2,1)S(1)} %bitcast.13, bf16[1024,256]{1,0:T(8,128)(2,1)S(1)} %collective-permute-done.even_side, ...), custom_call_target="tpu_custom_call" | custom-call | tf_op jit(solution)/shard_map/edge_products/pallas_call | solution.py:437
  28.0 0.1 collective-permute-start.2
  28.1 0.1 collective-permute-start.3
  28.1 2.7 %collective-permute-start.4 = (bf16[272,128]{1,0:T(8,128)(2,1)S(1)}, bf16[272,128]{1,0:T(8,128)(2,1)S(1)}, u32[]{:S(2)}, u32[]{:S(2)}) collective-permute-start(bf16[272,128]{1,0:T(8,128)(2,1)S(1)} %get-tuple-element.41), channel_id=1, source_target_pairs={{0,3},{1,0},{2,1},{3,2},{4,7},{5,4},{6,5},{7,6},{8,11},{9,8},{10,9... | collective-permute-start | bytes 208904 | tf_op jit(solution)/shard_map/ppermute | solution.py:357
  30.8 2.0 %collective-permute-done.2.first = bf16[272,128]{1,0:T(8,128)(2,1)S(1)} collective-permute-done((bf16[272,128]{1,0:T(8,128)(2,1)S(1)}, bf16[272,128]{1,0:T(8,128)(2,1)S(1)}, u32[]{:S(2)}, u32[]{:S(2)}) %collective-permute-start.2) | collective-permute-done | bytes 69664 | tf_op jit(solution)/shard_map/ppermute | solution.py:357
  32.8 0.4 collective-permute-done.3.second
  33.3 0.0 collective-permute-done.4.third
  33.3 0.7 %collective-permute-start.5 = (bf16[272,128]{1,0:T(8,128)(2,1)S(1)}, bf16[272,128]{1,0:T(8,128)(2,1)S(1)}, u32[]{:S(2)}, u32[]{:S(2)}) collective-permute-start(bf16[272,128]{1,0:T(8,128)(2,1)S(1)} %get-tuple-element.43), channel_id=1, source_target_pairs={{0,8},{1,9},{2,10},{3,11},{4,12},{5,13},{6,14},{7,15},{8,0},{9,1},... | collective-permute-start | bytes 208904 | tf_op jit(solution)/shard_map/ppermute | solution.py:357
  34.0 1.9 %collective-permute-start.6 = (bf16[272,128]{1,0:T(8,128)(2,1)S(1)}, bf16[272,128]{1,0:T(8,128)(2,1)S(1)}, u32[]{:S(2)}, u32[]{:S(2)}) collective-permute-start(bf16[272,128]{1,0:T(8,128)(2,1)S(1)} %get-tuple-element.44), channel_id=1, source_target_pairs={{0,4},{1,5},{2,6},{3,7},{4,8},{5,9},{6,10},{7,11},{8,12},{9,13},{1... | collective-permute-start | bytes 208904 | tf_op jit(solution)/shard_map/ppermute | solution.py:357
  36.0 0.7 %collective-permute-start.7 = (bf16[272,128]{1,0:T(8,128)(2,1)S(1)}, bf16[272,128]{1,0:T(8,128)(2,1)S(1)}, u32[]{:S(2)}, u32[]{:S(2)}) collective-permute-start(bf16[272,128]{1,0:T(8,128)(2,1)S(1)} %get-tuple-element.45), channel_id=1, source_target_pairs={{0,12},{1,13},{2,14},{3,15},{4,0},{5,1},{6,2},{7,3},{8,4},{9,5},{1... | collective-permute-start | bytes 208904 | tf_op jit(solution)/shard_map/ppermute | solution.py:357
  36.7 1.4 %collective-permute-done.5.first = bf16[272,128]{1,0:T(8,128)(2,1)S(1)} collective-permute-done((bf16[272,128]{1,0:T(8,128)(2,1)S(1)}, bf16[272,128]{1,0:T(8,128)(2,1)S(1)}, u32[]{:S(2)}, u32[]{:S(2)}) %collective-permute-start.5) | collective-permute-done | bytes 69664 | tf_op jit(solution)/shard_map/ppermute | solution.py:357
  38.1 0.7 %collective-permute-done.6.second = bf16[272,128]{1,0:T(8,128)(2,1)S(1)} collective-permute-done((bf16[272,128]{1,0:T(8,128)(2,1)S(1)}, bf16[272,128]{1,0:T(8,128)(2,1)S(1)}, u32[]{:S(2)}, u32[]{:S(2)}) %collective-permute-start.6) | collective-permute-done | bytes 69664 | tf_op jit(solution)/shard_map/ppermute | solution.py:357
  38.8 0.4 collective-permute-done.7.third
  39.2 1.3 %collective-permute-start.8 = (bf16[272,128]{1,0:T(8,128)(2,1)S(1)}, bf16[272,128]{1,0:T(8,128)(2,1)S(1)}, u32[]{:S(2)}, u32[]{:S(2)}) collective-permute-start(bf16[272,128]{1,0:T(8,128)(2,1)S(1)} %get-tuple-element.47), channel_id=1, source_target_pairs={{0,32},{16,48},{32,64},{48,80},{64,96},{80,112},{96,0},{112,16},{1... | collective-permute-start | bytes 208904 | tf_op jit(solution)/shard_map/ppermute | solution.py:357
  40.5 2.5 %collective-permute-start.9 = (bf16[272,128]{1,0:T(8,128)(2,1)S(1)}, bf16[272,128]{1,0:T(8,128)(2,1)S(1)}, u32[]{:S(2)}, u32[]{:S(2)}) collective-permute-start(bf16[272,128]{1,0:T(8,128)(2,1)S(1)} %get-tuple-element.48), channel_id=1, source_target_pairs={{0,64},{16,80},{32,96},{48,112},{64,0},{80,16},{96,32},{112,48},{1... | collective-permute-start | bytes 208904 | tf_op jit(solution)/shard_map/ppermute | solution.py:357
  42.9 1.2 %collective-permute-start.10 = (bf16[272,128]{1,0:T(8,128)(2,1)S(1)}, bf16[272,128]{1,0:T(8,128)(2,1)S(1)}, u32[]{:S(2)}, u32[]{:S(2)}) collective-permute-start(bf16[272,128]{1,0:T(8,128)(2,1)S(1)} %get-tuple-element.49), channel_id=1, source_target_pairs={{0,96},{16,112},{32,0},{48,16},{64,32},{80,48},{96,64},{112,80},{1... | collective-permute-start | bytes 208904 | tf_op jit(solution)/shard_map/ppermute | solution.py:357
  44.1 0.3 collective-permute-done.8
  44.4 1.3 %collective-permute-done.9 = bf16[272,128]{1,0:T(8,128)(2,1)S(1)} collective-permute-done((bf16[272,128]{1,0:T(8,128)(2,1)S(1)}, bf16[272,128]{1,0:T(8,128)(2,1)S(1)}, u32[]{:S(2)}, u32[]{:S(2)}) %collective-permute-start.9) | collective-permute-done | bytes 69664 | tf_op jit(solution)/shard_map/ppermute | solution.py:357
  45.7 0.5 collective-permute-done.10
  46.2 0.2 collective-permute-start.11
  46.4 0.4 local_gradients.1.mine
  46.7 1.1 %collective-permute-done.11.other = bf16[4,272,128]{2,1,0:T(8,128)(2,1)S(1)} collective-permute-done((bf16[4,272,128]{2,1,0:T(8,128)(2,1)S(1)}, bf16[4,272,128]{2,1,0:T(8,128)(2,1)S(1)}, u32[]{:S(2)}, u32[]{:S(2)}) %collective-permute-start.11) | collective-permute-done | bytes 278560 | tf_op jit(solution)/shard_map/ppermute | solution.py:464
  47.9 6.5 %backward_chain.1 = (f32[16,256]{1,0:T(8,128)}, f32[7,256,256]{2,1,0:T(8,128)}, f32[256,256]{1,0:T(8,128)}) custom-call(f32[4,256,256]{2,1,0:T(8,128)S(1)} %local_gradients.1.mine, bf16[4,272,128]{2,1,0:T(8,128)(2,1)S(1)} %collective-permute-done.11.other, f32[8,256,256]{2,1,0:T(8,128)S(1)} %get-tuple-element.51.keep, ...), custom_call_target="tpu_custom_call" | custom-call | tf_op jit(solution)/shard_map/backward_chain/pallas_call | solution.py:477
  (3 shorter events, 0.1 us)
Async XLA Ops:
  0.6 7.9 %copy-start.1 = (bf16[1,1024,256]{2,1,0:T(8,128)(2,1)S(1)}, bf16[1,1024,256]{2,1,0:T(8,128)(2,1)}, u32[]{:S(2)}) copy-start(bf16[1,1024,256]{2,1,0:T(8,128)(2,1)} %param.8) | copy-start | bytes 1572868
  0.6 15.0 %copy-start.4 = (s32[1,8,4]{1,2,0:T(4,128)S(1)}, s32[1,8,4]{1,2,0:T(4,128)}, u32[]{:S(2)}) copy-start(s32[1,8,4]{1,2,0:T(4,128)} %param.9) | copy-start | bytes 388
  0.7 23.1 %copy-start.3 = (s32[1,2,1024]{2,1,0:T(2,128)S(1)}, s32[1,2,1024]{2,1,0:T(2,128)}, u32[]{:S(2)}) copy-start(s32[1,2,1024]{2,1,0:T(2,128)} %param.12) | copy-start | bytes 24580
  0.7 23.1 %copy-start.2 = (s32[1,2,1024]{2,1,0:T(2,128)S(1)}, s32[1,2,1024]{2,1,0:T(2,128)}, u32[]{:S(2)}) copy-start(s32[1,2,1024]{2,1,0:T(2,128)} %param.11) | copy-start | bytes 24580
  0.7 23.1 %copy-start = (bf16[1,8,4,128,128]{4,3,2,1,0:T(8,128)(2,1)S(1)}, bf16[1,8,4,128,128]{4,3,2,1,0:T(8,128)(2,1)}, u32[]{:S(2)}) copy-start(bf16[1,8,4,128,128]{4,3,2,1,0:T(8,128)(2,1)} %param.10) | copy-start | bytes 3145732
  8.5 13.8 %collective-permute-start.1 = (bf16[1024,256]{1,0:T(8,128)(2,1)S(1)}, bf16[1024,256]{1,0:T(8,128)(2,1)S(1)}, u32[]{:S(2)}, u32[]{:S(2)}) collective-permute-start(bf16[1024,256]{1,0:T(8,128)(2,1)S(1)} %bitcast.11), channel_id=1, source_target_pairs={{0,15},{1,2},{2,1},{3,4},{4,3},{5,6},{6,5},{7,8},{8,7},{9,10},{10,... | collective-permute-start | bytes 1572872 | tf_op jit(solution)/shard_map/ppermute | solution.py:420
  15.6 8.1 %collective-permute-start = (bf16[1024,256]{1,0:T(8,128)(2,1)S(1)}, bf16[1024,256]{1,0:T(8,128)(2,1)S(1)}, u32[]{:S(2)}, u32[]{:S(2)}) collective-permute-start(bf16[1024,256]{1,0:T(8,128)(2,1)S(1)} %bitcast.12), channel_id=1, source_target_pairs={{0,1},{1,0},{2,3},{3,2},{4,5},{5,4},{6,7},{7,6},{8,9},{9,8},{10,11... | collective-permute-start | bytes 1572872 | tf_op jit(solution)/shard_map/ppermute | solution.py:419
  28.0 4.9 %collective-permute-start.2 = (bf16[272,128]{1,0:T(8,128)(2,1)S(1)}, bf16[272,128]{1,0:T(8,128)(2,1)S(1)}, u32[]{:S(2)}, u32[]{:S(2)}) collective-permute-start(bf16[272,128]{1,0:T(8,128)(2,1)S(1)} %get-tuple-element.39), channel_id=1, source_target_pairs={{0,2},{1,3},{2,0},{3,1},{4,6},{5,7},{6,4},{7,5},{8,10},{9,11},{10,... | collective-permute-start | bytes 208904 | tf_op jit(solution)/shard_map/ppermute | solution.py:357
  28.1 5.2 %collective-permute-start.3 = (bf16[272,128]{1,0:T(8,128)(2,1)S(1)}, bf16[272,128]{1,0:T(8,128)(2,1)S(1)}, u32[]{:S(2)}, u32[]{:S(2)}) collective-permute-start(bf16[272,128]{1,0:T(8,128)(2,1)S(1)} %get-tuple-element.40), channel_id=1, source_target_pairs={{0,1},{1,2},{2,3},{3,0},{4,5},{5,6},{6,7},{7,4},{8,9},{9,10},{10,1... | collective-permute-start | bytes 208904 | tf_op jit(solution)/shard_map/ppermute | solution.py:357
  28.1 5.1 %collective-permute-start.4 = (bf16[272,128]{1,0:T(8,128)(2,1)S(1)}, bf16[272,128]{1,0:T(8,128)(2,1)S(1)}, u32[]{:S(2)}, u32[]{:S(2)}) collective-permute-start(bf16[272,128]{1,0:T(8,128)(2,1)S(1)} %get-tuple-element.41), channel_id=1, source_target_pairs={{0,3},{1,0},{2,1},{3,2},{4,7},{5,4},{6,5},{7,6},{8,11},{9,8},{10,9... | collective-permute-start | bytes 208904 | tf_op jit(solution)/shard_map/ppermute | solution.py:357
  33.3 4.8 %collective-permute-start.5 = (bf16[272,128]{1,0:T(8,128)(2,1)S(1)}, bf16[272,128]{1,0:T(8,128)(2,1)S(1)}, u32[]{:S(2)}, u32[]{:S(2)}) collective-permute-start(bf16[272,128]{1,0:T(8,128)(2,1)S(1)} %get-tuple-element.43), channel_id=1, source_target_pairs={{0,8},{1,9},{2,10},{3,11},{4,12},{5,13},{6,14},{7,15},{8,0},{9,1},... | collective-permute-start | bytes 208904 | tf_op jit(solution)/shard_map/ppermute | solution.py:357
  34.0 4.7 %collective-permute-start.6 = (bf16[272,128]{1,0:T(8,128)(2,1)S(1)}, bf16[272,128]{1,0:T(8,128)(2,1)S(1)}, u32[]{:S(2)}, u32[]{:S(2)}) collective-permute-start(bf16[272,128]{1,0:T(8,128)(2,1)S(1)} %get-tuple-element.44), channel_id=1, source_target_pairs={{0,4},{1,5},{2,6},{3,7},{4,8},{5,9},{6,10},{7,11},{8,12},{9,13},{1... | collective-permute-start | bytes 208904 | tf_op jit(solution)/shard_map/ppermute | solution.py:357
  36.0 3.2 %collective-permute-start.7 = (bf16[272,128]{1,0:T(8,128)(2,1)S(1)}, bf16[272,128]{1,0:T(8,128)(2,1)S(1)}, u32[]{:S(2)}, u32[]{:S(2)}) collective-permute-start(bf16[272,128]{1,0:T(8,128)(2,1)S(1)} %get-tuple-element.45), channel_id=1, source_target_pairs={{0,12},{1,13},{2,14},{3,15},{4,0},{5,1},{6,2},{7,3},{8,4},{9,5},{1... | collective-permute-start | bytes 208904 | tf_op jit(solution)/shard_map/ppermute | solution.py:357
  39.2 5.2 %collective-permute-start.8 = (bf16[272,128]{1,0:T(8,128)(2,1)S(1)}, bf16[272,128]{1,0:T(8,128)(2,1)S(1)}, u32[]{:S(2)}, u32[]{:S(2)}) collective-permute-start(bf16[272,128]{1,0:T(8,128)(2,1)S(1)} %get-tuple-element.47), channel_id=1, source_target_pairs={{0,32},{16,48},{32,64},{48,80},{64,96},{80,112},{96,0},{112,16},{1... | collective-permute-start | bytes 208904 | tf_op jit(solution)/shard_map/ppermute | solution.py:357
  40.5 5.2 %collective-permute-start.9 = (bf16[272,128]{1,0:T(8,128)(2,1)S(1)}, bf16[272,128]{1,0:T(8,128)(2,1)S(1)}, u32[]{:S(2)}, u32[]{:S(2)}) collective-permute-start(bf16[272,128]{1,0:T(8,128)(2,1)S(1)} %get-tuple-element.48), channel_id=1, source_target_pairs={{0,64},{16,80},{32,96},{48,112},{64,0},{80,16},{96,32},{112,48},{1... | collective-permute-start | bytes 208904 | tf_op jit(solution)/shard_map/ppermute | solution.py:357
  42.9 3.2 %collective-permute-start.10 = (bf16[272,128]{1,0:T(8,128)(2,1)S(1)}, bf16[272,128]{1,0:T(8,128)(2,1)S(1)}, u32[]{:S(2)}, u32[]{:S(2)}) collective-permute-start(bf16[272,128]{1,0:T(8,128)(2,1)S(1)} %get-tuple-element.49), channel_id=1, source_target_pairs={{0,96},{16,112},{32,0},{48,16},{64,32},{80,48},{96,64},{112,80},{1... | collective-permute-start | bytes 208904 | tf_op jit(solution)/shard_map/ppermute | solution.py:357
  46.2 1.6 %collective-permute-start.11 = (bf16[4,272,128]{2,1,0:T(8,128)(2,1)S(1)}, bf16[4,272,128]{2,1,0:T(8,128)(2,1)S(1)}, u32[]{:S(2)}, u32[]{:S(2)}) collective-permute-start(bf16[4,272,128]{2,1,0:T(8,128)(2,1)S(1)} %pad_maximum_fusion.along), channel_id=1, source_target_pairs={{0,16},{16,0},{32,48},{48,32},{64,80},{80,64},{96,112},{112,96},{1... | collective-permute-start | bytes 835592 | tf_op jit(solution)/shard_map/ppermute | solution.py:464
